TPU v7x, 32 devices: a whole 2x2x4 slice. The times are simulated.
32 devices in a mesh: wide: 8 (over z, core), narrow: 4 (over y, x).
Axes of the slice: x: 2, y: 2, z: 4, core: 2. Of those that a mesh axis runs over, the one named last changes fastest.
Arguments:
- scalar_field: float32 [128, 256, 2048], P('wide', 'narrow'), may hold values from -6 to 6
- depth_rank: int32 [8], replicated, may hold values from 0 to 7, each once
- transfer: float32 [2, 3], replicated, may hold values from -2 to 2
- light_dir: float32 [3], replicated, may hold values from -1 to 1
Outputs:
- final_image: float32 [3, 256, 2048], P(None, 'narrow')
Inputs may be any that keep to these rules, and one draw needn't show every extreme that they name: `depth_rank`: every rank 0 to 7 appears exactly once.
All inputs are finite; a program needn't handle non-finite values.
Results may differ from a plain program's by a relative error of at most 0.000067.
Values sent between devices are 32-bit elements; how exact they have to be, the bound alone decides.
No kernel may reach another device: no remote copies, remote signals or barrier semaphores. Data moves between devices by JAX's collectives and lax.ppermute only.
A program may use at most 128 MiB of HBM per device.

v0:
```python
import jax
import jax.numpy as jnp
from jax import lax
from jax.sharding import PartitionSpec as P

background = 0.25
optical_total = 2.0


def extended(value, sides, width):
    for axis, dim in sides:
        count, length = (lax.axis_size(axis), value.shape[dim])
        up = [(i, (i + 1) % count) for i in range(count - 1)]
        down = [(j, i) for i, j in up]
        last = lax.slice_in_dim(value, length - width, length, axis=dim)
        leading = lax.slice_in_dim(value, 0, width, axis=dim)
        before = lax.ppermute(last, axis, up)
        after = lax.ppermute(leading, axis, down)
        value = jnp.concatenate([before, value, after], axis=dim)
    return value


def march_steps(volume, plane_total):
    return jax.nn.softplus(2.0 * volume) * (optical_total / plane_total)


def render(padded, optical_step, light_dir, transfer):
    volume = padded[:, 1:-1, :]
    shifted_up = jnp.concatenate([volume[:1], volume[:-1]], axis=0)
    shifted_down = jnp.concatenate([volume[1:], volume[-1:]], axis=0)
    slope_depth = (shifted_down - shifted_up) * 0.5
    slope_rows = (padded[:, 2:, :] - padded[:, :-2, :]) * 0.5
    zero_column = jnp.zeros_like(volume[:, :, :1])
    right_cells = jnp.concatenate([volume[:, :, 1:], zero_column], axis=2)
    left_cells = jnp.concatenate([zero_column, volume[:, :, :-1]], axis=2)
    slope_cols = (right_cells - left_cells) * 0.5
    shading = 0.5 + 0.5 * jnp.tanh(
        light_dir[0] * slope_depth + light_dir[1] * slope_rows + light_dir[2] * slope_cols
    )
    passed = jnp.cumsum(optical_step, axis=0) - optical_step
    weights = jnp.exp(-passed) * (1.0 - jnp.exp(-optical_step)) * shading
    colors = jax.nn.sigmoid(
        transfer[0][:, None, None, None] * volume[None] + transfer[1][:, None, None, None]
    )
    return jnp.sum(weights[None] * colors, axis=1)


def body(scalar_field, depth_rank, transfer, light_dir):
    plane_count = scalar_field.shape[0]
    wide_count = lax.axis_size("wide")
    columns = scalar_field.shape[2]
    col_block = columns // wide_count
    wide_index = lax.axis_index("wide")
    optical_step = march_steps(scalar_field, plane_count * wide_count)
    brick_depth = jnp.sum(optical_step, axis=0)
    padded = extended(scalar_field, (("narrow", 1),), 1)
    shaded_color = render(padded, optical_step, light_dir, transfer)
    my_rank = lax.dynamic_index_in_dim(depth_rank, wide_index, keepdims=False)
    pieces = lax.all_gather(brick_depth[None], "wide", axis=0, tiled=True)
    in_front = (depth_rank < my_rank).astype(jnp.float32)
    ahead = jnp.einsum("k,kyx->yx", in_front, pieces, precision=lax.Precision.HIGHEST)
    total_depth = jnp.sum(pieces, axis=0)
    weighted = jnp.exp(-ahead)[None] * shaded_color
    partial_value = lax.psum_scatter(weighted, "wide", scatter_dimension=2, tiled=True)
    total_cols = lax.dynamic_slice_in_dim(total_depth, wide_index * col_block, col_block, 1)
    image_tile = partial_value + background * jnp.exp(-total_cols)
    return lax.all_gather(image_tile, "wide", axis=2, tiled=True)


def solution(mesh):
    return jax.shard_map(
        body,
        mesh=mesh,
        in_specs=(P("wide", "narrow", None), P(), P(), P()),
        out_specs=P(None, "narrow", None),
        check_vma=False,
    )
```

profile of v0, /device:TPU:0, one launch (start us, length us, event | category | flops | bytes accessed | tf_op | source)
XLA Modules:
  0.0 200.8 jit_solution(2742065509106384088)
XLA Ops:
  6.5 1.7 fusion.25
  8.3 1.3 collective-permute-start
  9.6 5.5 %collective-permute-start.1 = (f32[16,1,2048]{2,1,0:T(1,128)S(1)}, f32[16,1,2048]{2,1,0:T(1,128)S(1)}, u32[]{:S(2)}, u32[]{:S(2)}) collective-permute-start(f32[16,1,2048]{2,1,0:T(1,128)S(1)} %get-tuple-element.14), channel_id=1, source_target_pairs={{0,1},{1,2},{2,3},{4,5},{5,6},{6,7},{8,9},{9,10},{10,11},{12,13},{... | collective-permute-start | bytes 393224 | tf_op jit(solution)/shard_map/ppermute | solution.py:17
  15.1 13.2 %fusion.22 = (f32[16,64,2047]{2,1,0:T(8,128)}, f32[16,64,2047]{2,1,0:T(8,128)}) fusion(f32[16,64,2048]{2,1,0:T(8,128)} %param.4), kind=kLoop, calls=%fused_computation.32 | loop fusion | bytes 33538048 | tf_op jit(solution)/shard_map/slice | solution.py:34
  28.3 13.9 %fusion.24 = (f32[15,64,2048]{2,1,0:T(8,128)}, f32[15,64,2048]{2,1,0:T(8,128)}) fusion(f32[16,64,2048]{2,1,0:T(8,128)} %param.4), kind=kLoop, calls=%fused_computation.34 | loop fusion | bytes 31457280 | tf_op jit(solution)/shard_map/slice | solution.py:29
  42.2 1.3 fusion.23
  43.5 0.7 fusion.26
  46.1 29.9 %fusion.14 = (f32[64,2048]{1,0:T(8,128)}, f32[16,64,2048]{2,1,0:T(8,128)}) fusion(f32[16,64,2048]{2,1,0:T(8,128)} %param.4, f32[]{:T(128)} %bitcast.6, f32[16,64,2047]{2,1,0:T(8,128)} %get-tuple-element.8, f32[16,64,2047]{2,1,0:T(8,128)} %get-tuple-element.7, f32[]{:T(128)} %bitcast.5, f32[16,1,2048]{2,1,0:T(1,128)S(1)} %collective-permute-done.1, ...), kind=kOutput, calls=%fused_computation.18 | output fusion | flops 108920832 | bytes 51109900 | tf_op jit(solution)/shard_map/jit(cumsum)/reduce_window_sum | solution.py:40
  76.0 0.0 all-gather.6.cloned.1.call-update
  76.0 0.2 reduce-scatter.2.cloned.1.call-start
  76.3 0.6 dynamic_slice.7
  76.9 9.0 %multiply_reduce_fusion = f32[3,64,2048]{2,1,0:T(8,128)S(1)} fusion(f32[3]{0:T(128)S(1)} %get-tuple-element.16, f32[16,64,2048]{2,1,0:T(8,128)} %param.4, f32[3]{0:T(128)S(1)} %get-tuple-element.15, f32[16,64,2048]{2,1,0:T(8,128)} %get-tuple-element.6), kind=kLoop, calls=%fused_computation | loop fusion | flops 43646976 | bytes 18350104 | tf_op jit(solution)/shard_map/reduce_sum | solution.py:45
  85.8 39.2 %all-gather.6.cloned.1.call-done = f32[512,2048]{1,0:T(8,128)} async-done(((f32[64,2048]{1,0:T(8,128)}), f32[512,2048]{1,0:T(8,128)}) %all-gather.6.cloned.1.call-update) | async-done | bytes 4194320 | tf_op jit(solution)/shard_map/all_gather | solution.py:59
  125.1 7.1 %fusion.10 = f32[1,64,2048]{2,0,1:T(1,128)S(1)} fusion(f32[8,64,2048]{2,1,0:T(8,128)} %bitcast.16, s32[8]{0:T(128)S(1)} %copy-done.2, s32[]{:T(128)} %bitcast), kind=kOutput, calls=%fused_computation.15 | convolution fusion | flops 12582920 | bytes 4718628 | tf_op jit(solution)/shard_map/k,kyx->yx/dot_general | solution.py:61
  132.2 0.2 fusion.15
  132.4 1.3 broadcast_multiply_fusion
  133.7 0.0 reduce-scatter.2.cloned.1.call-update
  133.7 0.0 all-gather.4.cloned.1.call-start
  133.8 2.5 %reduce_sum.29 = f32[64,2048]{1,0:T(8,128)S(1)} reduce(f32[8,64,2048]{2,1,0:T(8,128)} %bitcast.17, f32[]{:T(128)} %constant.18.clone.1), dimensions={0}, to_apply=%region_4.5 | reduce | flops 917504 | bytes 4718596 | tf_op jit(solution)/shard_map/reduce_sum | solution.py:62
  136.3 30.5 %reduce-scatter.2.cloned.1.call-done = f32[3,64,256]{2,1,0:T(8,128)} async-done(((f32[3,64,2048]{2,1,0:T(8,128)}), f32[3,64,256]{2,1,0:T(8,128)}) %reduce-scatter.2.cloned.1.call-update) | async-done | bytes 196624 | tf_op jit(solution)/shard_map/reduce_scatter | solution.py:64
  166.8 1.6 broadcast_add_fusion
  168.4 0.0 all-gather.4.cloned.1.call-update
  168.5 23.1 %all-gather.4.cloned.1.call-done = f32[3,64,2048]{2,1,0:T(8,128)} async-done(((f32[3,64,256]{2,1,0:T(8,128)}), f32[3,64,2048]{2,1,0:T(8,128)}) %all-gather.4.cloned.1.call-update) | async-done | bytes 1572880 | tf_op jit(solution)/shard_map/all_gather | solution.py:67
  191.6 2.7 %copy.11 = f32[3,64,2048]{2,1,0:T(8,128)} copy(f32[3,64,2048]{2,1,0:T(8,128)} %all-gather.4.cloned.1.call-done) | data formatting | bytes 3145728
  (11 shorter events, 0.1 us)
Async XLA Ops:
  6.5 118.5 %all-gather.6.cloned.1.call-start = ((), (), s32[]{:S(2)}) async-start(), calls=%async_computation.3 | async-start | bytes 4718592 | tf_op jit(solution)/shard_map/all_gather | solution.py:59
  8.3 37.8 %collective-permute-start = (f32[16,1,2048]{2,1,0:T(1,128)S(1)}, f32[16,1,2048]{2,1,0:T(1,128)S(1)}, u32[]{:S(2)}, u32[]{:S(2)}) collective-permute-start(f32[16,1,2048]{2,1,0:T(1,128)S(1)} %get-tuple-element.13), channel_id=1, source_target_pairs={{1,0},{2,1},{3,2},{5,4},{6,5},{7,6},{9,8},{10,9},{11,10},{13,12},{... | collective-permute-start | bytes 393224 | tf_op jit(solution)/shard_map/ppermute | solution.py:18
  9.6 36.5 %collective-permute-start.1 = (f32[16,1,2048]{2,1,0:T(1,128)S(1)}, f32[16,1,2048]{2,1,0:T(1,128)S(1)}, u32[]{:S(2)}, u32[]{:S(2)}) collective-permute-start(f32[16,1,2048]{2,1,0:T(1,128)S(1)} %get-tuple-element.14), channel_id=1, source_target_pairs={{0,1},{1,2},{2,3},{4,5},{5,6},{6,7},{8,9},{9,10},{10,11},{12,13},{... | collective-permute-start | bytes 393224 | tf_op jit(solution)/shard_map/ppermute | solution.py:17
  28.3 15.2 %copy-start = (f32[3]{0:T(128)S(1)}, f32[3]{0:T(128)}, u32[]{:S(2)}) copy-start(f32[3]{0:T(128)} %param.7) | copy-start | bytes 40
  46.1 30.2 %copy-start.2 = (s32[8]{0:T(128)S(1)}, s32[8]{0:T(128)}, u32[]{:S(2)}) copy-start(s32[8]{0:T(128)} %param.5) | copy-start | bytes 100
  46.1 30.8 %copy-start.1 = (f32[2,3]{1,0:T(2,128)S(1)}, f32[2,3]{1,0:T(2,128)}, u32[]{:S(2)}) copy-start(f32[2,3]{1,0:T(2,128)} %param.6) | copy-start | bytes 76
  76.0 90.8 %reduce-scatter.2.cloned.1.call-start = ((), (), s32[]{:S(2)}) async-start(), calls=%async_computation.1 | async-start | bytes 1769472 | tf_op jit(solution)/shard_map/reduce_scatter | solution.py:64
  133.7 57.9 %all-gather.4.cloned.1.call-start = ((), (), s32[]{:S(2)}) async-start(), calls=%async_computation.2 | async-start | bytes 1769472 | tf_op jit(solution)/shard_map/all_gather | solution.py:67
Sparse Core Ops, SparseCore 0:
  76.2 48.8 all-gather.5
  133.8 32.9 reduce-scatter.1
  168.6 22.9 all-gather.3
where the time goes:
time: 201 us
  waiting for transfers between devices  93 us (46%)
  other arithmetic  44.5 us (22%)
  local copies, waits for them, and re-layouts  34.1 us (17%)
  between operations  15.1 us (8%)
  matrix products  7.1 us (4%)
  starting transfers between devices  7.04 us (4%)
    all_gather x1, waiting for transfers between devices, body(): pieces = lax.all_gather(brick_depth[None], 'wide', axis=0, tiled=True)  39.2 us
    reduce_scatter x1, waiting for transfers between devices, body(): lax.psum_scatter(weighted, 'wide', scatter_dimension=2, tiled=True)  30.5 us
    another operation x1, other arithmetic, render(): passed = jnp.cumsum(optical_step, axis=0) - optical_step  29.9 us
    all_gather x1, waiting for transfers between devices, body(): return lax.all_gather(image_tile, 'wide', axis=2, tiled=True)  23.1 us
    slice x2, local copies, waits for them, and re-layouts, render(): shifted_up = jnp.concatenate([volume[:1], volume[:-1]], axis=0)  15.2 us
    slice x1, local copies, waits for them, and re-layouts, render(): right_cells = jnp.concatenate([volume[:, :, 1:], zero_column], axis=2)  13.2 us
    reduce_sum x1, other arithmetic, render(): return jnp.sum(weights[None] * colors, axis=1)  8.96 us
    dot_general x1, matrix products, body(): jnp.einsum('k,kyx->yx', in_front, pieces, precision=lax.Precision.HIGHEST)  7.1 us
  transfers between devices with their start and end apart: 5, of which 3 were waited for; matrix products, arithmetic and copies ran while one was open for 20% of the time, Pallas kernels for 0%

commit v1 on v0

v1 whole, which is shorter than its diff:
```python
import functools

import jax
import jax.numpy as jnp
from jax import lax
from jax.experimental import pallas as pl
from jax.experimental.pallas import tpu as pltpu
from jax.sharding import PartitionSpec as P

background = 0.25
optical_total = 2.0

SUB = 8
LANE = 128
GROUP = 256
CHUNKS = (4, 4)


def render_kernel(
    chips, cores, chunk, scale,
    where_ref, transfer_ref, light_ref, field_ref, above_ref, below_ref, *rest
):
    out_refs, (padded, sem) = rest[:chips], rest[chips:]
    planes, rows, columns = field_ref.shape
    start, width = chunk
    tiles = rows // SUB
    parts = chips * cores // tiles
    part = width // parts
    my_chip, my_core = where_ref[0], where_ref[1]

    lead = LANE if start > 0 else 0
    trail = LANE if start + width < columns else 0
    first_tile = lax.rem(my_chip * cores, tiles)

    def copy_of(step):
        tile = lax.rem(first_tile + step, tiles)
        return pltpu.make_async_copy(
            field_ref.at[:, pl.ds(pl.multiple_of(tile * SUB, SUB), SUB), pl.ds(start - lead, lead + width + trail)],
            padded.at[
                :, pl.ds(pl.multiple_of(tile * SUB + SUB, SUB), SUB), pl.ds(LANE - lead, lead + width + trail)
            ],
            sem.at[step],
        )

    for step in range(tiles):
        copy_of(step).start()
    if not lead:
        padded[:, :, :LANE] = jnp.zeros((planes, rows + 2 * SUB, LANE), jnp.float32)
    if not trail:
        padded[:, :, LANE + width :] = jnp.zeros((planes, rows + 2 * SUB, LANE), jnp.float32)
    padded[:, SUB - 1 : SUB, LANE : LANE + width] = above_ref[:, :, start : start + width]
    padded[:, SUB + rows : SUB + rows + 1, LANE : LANE + width] = below_ref[:, :, start : start + width]

    light = [0.5 * light_ref[i] for i in range(3)]
    slope = [0.5 * transfer_ref[0, c] for c in range(3)]
    offset = [0.5 * transfer_ref[1, c] for c in range(3)]
    sub = lax.broadcasted_iota(jnp.int32, (SUB, LANE), 0)
    lane = lax.broadcasted_iota(jnp.int32, (SUB, LANE), 1)
    top, bottom = sub == 0, sub == SUB - 1
    leftmost, rightmost = lane == 0, lane == LANE - 1
    per_group = GROUP // LANE
    groups = part // GROUP

    for step in range(tiles):
        copy_of(step).wait()

    for k in range(chips):
        chip = lax.rem(my_chip + k, chips)
        out_ref = out_refs[k]

        def march(index, carry, chip=chip, out_ref=out_ref):
            relative = index // groups
            column = (index - relative * groups) * GROUP
            owner = chip * cores + lax.rem(my_core + relative, cores)
            tile = lax.rem(owner, tiles)
            row = pl.multiple_of(tile * SUB + SUB, SUB)
            at = pl.multiple_of(LANE + (owner // tiles) * part + column, LANE)

            def load(plane, row_shift, vreg):
                return padded[
                    plane,
                    pl.ds(pl.multiple_of(row + row_shift * SUB, SUB), SUB),
                    pl.ds(pl.multiple_of(at + vreg * LANE, LANE), LANE),
                ]

            zero = jnp.zeros((SUB, LANE), jnp.float32)
            depth = [zero] * per_group
            left_over = [zero + 1.0] * per_group
            total = [zero] * per_group
            sums = [[zero] * per_group for _ in range(3)]
            here = [load(0, 0, v) for v in range(-1, per_group + 1)]
            before = here
            for plane in range(planes):
                after = [load(plane + 1, 0, v) for v in range(-1, per_group + 1)] if plane + 1 < planes else here
                for v in range(per_group):
                    value = here[v + 1]
                    up = pltpu.roll(jnp.where(bottom, load(plane, -1, v), value), 1, 0)
                    down = pltpu.roll(jnp.where(top, load(plane, 1, v), value), SUB - 1, 0)
                    left = pltpu.roll(jnp.where(rightmost, here[v], value), 1, 1)
                    right = pltpu.roll(jnp.where(leftmost, here[v + 2], value), LANE - 1, 1)
                    shade = jnp.tanh(
                        light[0] * (after[v + 1] - before[v + 1]) + light[1] * (down - up) + light[2] * (right - left)
                    )
                    depth[v] = depth[v] + jnp.log(1.0 + jnp.exp(value + value))
                    through = jnp.exp(depth[v] * -scale)
                    lost = left_over[v] - through
                    left_over[v] = through
                    weight = lost + lost * shade
                    total[v] = total[v] + weight
                    for c in range(3):
                        sums[c][v] = sums[c][v] + weight * jnp.tanh(slope[c] * value + offset[c])
                before, here = here, after
            for v in range(per_group):
                lanes = pl.ds(pl.multiple_of(column + v * LANE, LANE), LANE)
                for c in range(3):
                    out_ref[relative, c, :, lanes] = 0.25 * (total[v] + sums[c][v])
                out_ref[relative, 3, :, lanes] = depth[v] * scale
            return carry

        lax.fori_loop(0, cores * groups, march, 0)


def composite_kernel(chips, cores, where_ref, rank_ref, *refs):
    own, other, out_ref = refs[:chips], refs[chips : 2 * chips], refs[2 * chips]
    my_chip, my_core = where_ref[0], where_ref[1]
    blocks, ranks = [], []
    for k in range(chips):
        chip = lax.rem(my_chip + chips - k, chips)
        for core, ref in ((my_core, own[k]), (cores - 1 - my_core, other[k])):
            blocks.append(ref)
            ranks.append(rank_ref[chip * cores + core])
    count = len(blocks)
    ahead = [[(ranks[j] < ranks[i]).astype(jnp.float32) for j in range(count)] for i in range(count)]

    def one(step, carry):
        lanes = pl.ds(pl.multiple_of(step * LANE, LANE), LANE)
        depths = [ref[0, 3, :, lanes] for ref in blocks]
        total = functools.reduce(jnp.add, depths)
        sums = [background * jnp.exp(-total)] * 3
        for i in range(count):
            front = functools.reduce(jnp.add, [ahead[i][j] * depths[j] for j in range(count) if j != i])
            weight = jnp.exp(-front)
            for c in range(3):
                sums[c] = sums[c] + weight * blocks[i][0, c, :, lanes]
        for c in range(3):
            out_ref[c, :, lanes] = sums[c]
        return carry

    lax.fori_loop(0, out_ref.shape[2] // LANE, one, 0)


def place_kernel(chips, cores, tiles, chunks, where_ref, *refs):
    count = len(chunks) * chips * 2
    blocks, out_ref, sem = refs[:count], refs[count], refs[count + 1]
    my_chip, my_core = where_ref[0], where_ref[1]
    copies = []
    for i, (start, width) in enumerate(chunks):
        part = width // (chips * cores // tiles)
        for k in range(chips):
            chip = lax.rem(my_chip + chips - k, chips)
            for j, core in enumerate((my_core, cores - 1 - my_core)):
                owner = chip * cores + core
                row = pl.multiple_of(lax.rem(owner, tiles) * SUB, SUB)
                column = pl.multiple_of(start + (owner // tiles) * part, LANE)
                n = (i * chips + k) * 2 + j
                copy = pltpu.make_async_copy(
                    blocks[n], out_ref.at[:, pl.ds(row, SUB), pl.ds(column, part)], sem.at[n]
                )
                copy.start()
                copies.append(copy)
    for copy in copies:
        copy.wait()


def body(scalar_field, depth_rank, transfer, light_dir):
    planes, rows, columns = scalar_field.shape
    wide, narrow = lax.axis_size("wide"), lax.axis_size("narrow")
    cores = 2
    chips = wide // cores
    tiles = rows // SUB
    parts = wide // tiles
    scale = optical_total / (planes * wide)
    index = lax.axis_index("wide")
    where = jnp.stack([index // cores, index % cores]).astype(jnp.int32)
    chunks, start = [], 0
    for eighths in CHUNKS:
        chunks.append((start, columns * eighths // sum(CHUNKS)))
        start += chunks[-1][1]

    def swap(value):
        return lax.ppermute(value, "wide", [(i, i ^ 1) for i in range(wide)])

    def send(value, k):
        return lax.ppermute(value, "wide", [(i, (i + k * cores) % wide) for i in range(wide)])

    up = [(i, i + 1) for i in range(narrow - 1)]
    above = lax.ppermute(scalar_field[:, rows - 1 :, :], "narrow", up)
    below = lax.ppermute(scalar_field[:, :1, :], "narrow", [(j, i) for i, j in up])

    smem = pl.BlockSpec(memory_space=pltpu.SMEM)
    vmem = pl.BlockSpec(memory_space=pltpu.VMEM)
    anywhere = pl.BlockSpec(memory_space=pl.ANY)
    cells = planes * rows * columns

    finished = []
    for chunk in chunks:
        width = chunk[1]
        part = width // parts
        share = width / columns
        blocks = pl.pallas_call(
            functools.partial(render_kernel, chips, cores, chunk, scale),
            out_shape=[jax.ShapeDtypeStruct((cores, 4, SUB, part), jnp.float32)] * chips,
            in_specs=[smem, smem, smem, anywhere, vmem, vmem],
            out_specs=[vmem] * chips,
            scratch_shapes=[
                pltpu.VMEM((planes, rows + 2 * SUB, width + 2 * LANE), jnp.float32),
                pltpu.SemaphoreType.DMA((tiles,)),
            ],
            cost_estimate=pl.CostEstimate(
                flops=int(40 * cells * share), bytes_accessed=int(6 * cells * share),
                transcendentals=int(7 * cells * share),
            ),
            compiler_params=pltpu.CompilerParams(vmem_limit_bytes=40 * 2**20),
            name="render",
        )(where, transfer, light_dir, scalar_field, above, below)
        own = [blocks[0]] + [send(blocks[k], k) for k in range(1, chips)]
        other = [swap(value) for value in own]
        pick = [pl.BlockSpec((1, 4, SUB, part), functools.partial(lambda r, i: (r, 0, 0, 0), r)) for r in (0, 1)]
        tile = pl.pallas_call(
            functools.partial(composite_kernel, chips, cores),
            grid=(1,),
            out_shape=jax.ShapeDtypeStruct((3, SUB, part), jnp.float32),
            in_specs=[smem, smem] + [pick[0]] * chips + [pick[1]] * chips,
            out_specs=pl.BlockSpec((3, SUB, part), lambda i: (0, 0, 0)),
            cost_estimate=pl.CostEstimate(
                flops=wide * wide * SUB * part * 2, bytes_accessed=wide * 16 * SUB * part,
                transcendentals=wide * SUB * part,
            ),
            compiler_params=pltpu.CompilerParams(vmem_limit_bytes=40 * 2**20),
            name="composite",
        )(where, depth_rank, *own, *other)
        mine = [tile] + [send(tile, k) for k in range(1, chips)]
        for value in mine:
            finished += [value, swap(value)]

    return pl.pallas_call(
        functools.partial(place_kernel, chips, cores, tiles, chunks),
        out_shape=jax.ShapeDtypeStruct((3, rows, columns), jnp.float32),
        in_specs=[smem] + [anywhere] * len(finished),
        out_specs=anywhere,
        scratch_shapes=[pltpu.SemaphoreType.DMA((len(finished),))],
        cost_estimate=pl.CostEstimate(flops=0, bytes_accessed=24 * rows * columns, transcendentals=0),
        name="place",
    )(where, *finished)


def solution(mesh):
    return jax.shard_map(
        body,
        mesh=mesh,
        in_specs=(P("wide", "narrow", None), P(), P(), P()),
        out_specs=P(None, "narrow", None),
        check_vma=False,
    )
```

time: 201 us -> 149 us (0.74)
  waiting for transfers between devices: 93 us -> 21.3 us
  Pallas kernels: 0 us -> 69.4 us
  other arithmetic: 44.5 us -> 0.08 us
  starting transfers between devices: 7.04 us -> 49.1 us
  local copies, waits for them, and re-layouts: 34.1 us -> 7.55 us
  between operations: 15.1 us -> 0.27 us
  matrix products: 7.1 us -> 0 us
    pallas_call x0 -> x5, Pallas kernels: none -> 69.4 us  [the longest x1 49.6 us: body(): pl.pallas_call(functools.partial(place_kernel, chips, cores, tiles, chunk...]
    all_gather x2 -> x0, waiting for transfers between devices: 62.4 us -> none  [the longest x1 39.2 us: body(): pieces = lax.all_gather(brick_depth[None], 'wide', axis=0, tiled=True)]
    ppermute x2 -> x30, starting transfers between devices: 6.77 us -> 49.1 us  [the longest x12 39.5 us: send(): lax.ppermute(value, 'wide', [(i, (i + k * cores) % wide) for i in range(w...]
    reduce_scatter x1 -> x0, waiting for transfers between devices: 30.5 us -> none  [body(): lax.psum_scatter(weighted, 'wide', scatter_dimension=2, tiled=True)]
    another operation x1, other arithmetic: 29.9 us -> 0.08 us  [body(): where = jnp.stack([index // cores, index % cores]).astype(jnp.int32)]
    slice x5 -> x1, local copies, waits for them, and re-layouts: 30.8 us -> 1.74 us  [body(): scalar_field[:, :1, :]]
    ppermute x2 -> x30, waiting for transfers between devices: 0.01 us -> 21.3 us  [the longest x12 17.7 us: send(): lax.ppermute(value, 'wide', [(i, (i + k * cores) % wide) for i in range(w...]
    reduce_sum x2 -> x0, other arithmetic: 11.4 us -> none  [the longest x1 8.96 us: render(): return jnp.sum(weights[None] * colors, axis=1)]
  transfers between devices with their start and end apart: 5 -> 30, of which waited for: 3 -> 11; matrix products, arithmetic and copies ran while one was open for 20% -> 0% of each run, Pallas kernels for 0% -> 7%
where the time goes in v1:
time: 149 us; the launch traced here: 148 us
  Pallas kernels  69.4 us (47%)
  starting transfers between devices  49.1 us (33%)
  waiting for transfers between devices  21.3 us (14%)
  local copies, waits for them, and re-layouts  7.55 us (5%)
    pallas_call x1, Pallas kernels, body(): pl.pallas_call(functools.partial(place_kernel, chips, cores, tiles, chunk...  49.6 us
    ppermute x12, starting transfers between devices, send(): lax.ppermute(value, 'wide', [(i, (i + k * cores) % wide) for i in range(w...  39.5 us
    pallas_call x2, Pallas kernels, body(): pl.pallas_call(functools.partial(render_kernel, chips, cores, chunk, scal...  17.8 us
    ppermute x12, waiting for transfers between devices, send(): lax.ppermute(value, 'wide', [(i, (i + k * cores) % wide) for i in range(w...  17.7 us
    unnamed x44, local copies, waits for them, and re-layouts  5.81 us
    ppermute x1, starting transfers between devices, body(): above = lax.ppermute(scalar_field[:, rows - 1:, :], 'narrow', up)  5.48 us
  transfers between devices with their start and end apart: 30, of which 11 were waited for; matrix products, arithmetic and copies ran while one was open for 0% of the time, Pallas kernels for 7%

profile of v1, /device:TPU:0, one launch (start us, length us, event | category | flops | bytes accessed | tf_op | source)
XLA Modules:
  0.0 147.7 jit_solution(9562652395269391538)
XLA Ops:
  0.0 1.7 %fusion = (f32[16,1,2048]{2,1,0:T(1,128)S(1)}, f32[16,1,2048]{2,1,0:T(1,128)S(1)}) fusion(f32[16,64,2048]{2,1,0:T(8,128)} %field_ref.3), kind=kLoop, calls=%fused_computation.1 | loop fusion | bytes 524288 | tf_op jit(solution)/shard_map/slice | solution.py:198
  1.8 1.3 collective-permute-start.1
  3.1 5.5 %collective-permute-start = (f32[16,1,2048]{2,1,0:T(1,128)S(1)}, f32[16,1,2048]{2,1,0:T(1,128)S(1)}, u32[]{:S(2)}, u32[]{:S(2)}) collective-permute-start(f32[16,1,2048]{2,1,0:T(1,128)S(1)} %get-tuple-element.22), channel_id=1, source_target_pairs={{0,1},{1,2},{2,3},{4,5},{5,6},{6,7},{8,9},{9,10},{10,11},{12,13},{... | collective-permute-start | bytes 393224 | tf_op jit(solution)/shard_map/ppermute | solution.py:197
  8.6 1.5 collective-permute-done.1.below_ref
  10.1 1.2 collective-permute-done.above_ref
  11.3 3.4 %copy-done.2 = f32[16,64,2048]{2,1,0:T(8,128)S(1)} copy-done((f32[16,64,2048]{2,1,0:T(8,128)S(1)}, f32[16,64,2048]{2,1,0:T(8,128)}, u32[]{:S(2)}) %copy-start.2) | copy-done | bytes 8388632
  16.0 8.9 %render.3 = (f32[2,4,8,1024]{3,2,1,0:T(8,128)S(1)}, f32[2,4,8,1024]{3,2,1,0:T(8,128)S(1)}, f32[2,4,8,1024]{3,2,1,0:T(8,128)S(1)}, f32[2,4,8,1024]{3,2,1,0:T(8,128)S(1)}) custom-call(s32[2]{0:T(128)S(1)} %pad_add_fusion.where_ref, f32[2,3]{1,0:T(2,128)S(1)} %copy-done.5, f32[3]{0:T(128)S(1)} %copy-done.7, f32[16,64,2048]{2,1,0:T(8,128)S(1)} %copy-done.2, ...), custom_call_target="tpu_custom_call" | custom-call | flops 41943040 | bytes 6291456 | tf_op jit(solution)/shard_map/render/pallas_call | solution.py:210
  24.9 1.9 %collective-permute-start.16 = (f32[2,4,8,1024]{3,2,1,0:T(8,128)S(1)}, f32[2,4,8,1024]{3,2,1,0:T(8,128)S(1)}, u32[]{:S(2)}, u32[]{:S(2)}) collective-permute-start(f32[2,4,8,1024]{3,2,1,0:T(8,128)S(1)} %get-tuple-element.18), channel_id=1, source_target_pairs={{0,8},{4,12},{8,16},{12,20},{16,24},{20,28},{24,0},{28,4},{1,9},{5... | collective-permute-start | bytes 786440 | tf_op jit(solution)/shard_map/ppermute | solution.py:194
  26.8 2.6 %collective-permute-start.17 = (f32[2,4,8,1024]{3,2,1,0:T(8,128)S(1)}, f32[2,4,8,1024]{3,2,1,0:T(8,128)S(1)}, u32[]{:S(2)}, u32[]{:S(2)}) collective-permute-start(f32[2,4,8,1024]{3,2,1,0:T(8,128)S(1)} %get-tuple-element.19), channel_id=1, source_target_pairs={{0,16},{4,20},{8,24},{12,28},{16,0},{20,4},{24,8},{28,12},{1,17},{... | collective-permute-start | bytes 786440 | tf_op jit(solution)/shard_map/ppermute | solution.py:194
  29.4 1.3 collective-permute-start.18
  30.8 8.9 %render.2 = (f32[2,4,8,1024]{3,2,1,0:T(8,128)S(1)}, f32[2,4,8,1024]{3,2,1,0:T(8,128)S(1)}, f32[2,4,8,1024]{3,2,1,0:T(8,128)S(1)}, f32[2,4,8,1024]{3,2,1,0:T(8,128)S(1)}) custom-call(s32[2]{0:T(128)S(1)} %pad_add_fusion.where_ref, f32[2,3]{1,0:T(2,128)S(1)} %copy-done.6, f32[3]{0:T(128)S(1)} %copy-done.7, f32[16,64,2048]{2,1,0:T(8,128)S(1)} %copy-done.2, ...), custom_call_target="tpu_custom_call" | custom-call | flops 41943040 | bytes 6291456 | tf_op jit(solution)/shard_map/render/pallas_call | solution.py:210
  39.7 0.7 collective-permute-start.2
  40.4 7.9 %collective-permute-start.3 = (f32[2,4,8,1024]{3,2,1,0:T(8,128)S(1)}, f32[2,4,8,1024]{3,2,1,0:T(8,128)S(1)}, u32[]{:S(2)}, u32[]{:S(2)}) collective-permute-start(f32[2,4,8,1024]{3,2,1,0:T(8,128)S(1)} %get-tuple-element.15), channel_id=1, source_target_pairs={{0,16},{4,20},{8,24},{12,28},{16,0},{20,4},{24,8},{28,12},{1,17},{... | collective-permute-start | bytes 786440 | tf_op jit(solution)/shard_map/ppermute | solution.py:194
  48.4 14.9 %collective-permute-start.4 = (f32[2,4,8,1024]{3,2,1,0:T(8,128)S(1)}, f32[2,4,8,1024]{3,2,1,0:T(8,128)S(1)}, u32[]{:S(2)}, u32[]{:S(2)}) collective-permute-start(f32[2,4,8,1024]{3,2,1,0:T(8,128)S(1)} %get-tuple-element.16), channel_id=1, source_target_pairs={{0,24},{4,28},{8,0},{12,4},{16,8},{20,12},{24,16},{28,20},{1,25},{... | collective-permute-start | bytes 786440 | tf_op jit(solution)/shard_map/ppermute | solution.py:194
  63.9 4.0 %collective-permute-done.3.refs_2_ = f32[2,4,8,1024]{3,2,1,0:T(8,128)S(1)} collective-permute-done((f32[2,4,8,1024]{3,2,1,0:T(8,128)S(1)}, f32[2,4,8,1024]{3,2,1,0:T(8,128)S(1)}, u32[]{:S(2)}, u32[]{:S(2)}) %collective-permute-start.3) | collective-permute-done | bytes 262176 | tf_op jit(solution)/shard_map/ppermute | solution.py:194
  67.9 2.5 %collective-permute-done.4.refs_3_ = f32[2,4,8,1024]{3,2,1,0:T(8,128)S(1)} collective-permute-done((f32[2,4,8,1024]{3,2,1,0:T(8,128)S(1)}, f32[2,4,8,1024]{3,2,1,0:T(8,128)S(1)}, u32[]{:S(2)}, u32[]{:S(2)}) %collective-permute-start.4) | collective-permute-done | bytes 262176 | tf_op jit(solution)/shard_map/ppermute | solution.py:194
  71.1 1.0 composite.3.refs_8_
  72.1 5.1 %collective-permute-start.28 = (f32[3,8,1024]{2,1,0:T(8,128)S(1)}, f32[3,8,1024]{2,1,0:T(8,128)S(1)}, u32[]{:S(2)}, u32[]{:S(2)}) collective-permute-start(f32[3,8,1024]{2,1,0:T(8,128)S(1)} %composite.3.refs_8_), channel_id=1, source_target_pairs={{0,24},{4,28},{8,0},{12,4},{16,8},{20,12},{24,16},{28,20},{1,25},{... | collective-permute-start | bytes 294920 | tf_op jit(solution)/shard_map/ppermute | solution.py:194
  77.8 1.0 composite.2.refs_0_
  78.9 3.3 %collective-permute-start.14 = (f32[3,8,1024]{2,1,0:T(8,128)S(1)}, f32[3,8,1024]{2,1,0:T(8,128)S(1)}, u32[]{:S(2)}, u32[]{:S(2)}) collective-permute-start(f32[3,8,1024]{2,1,0:T(8,128)S(1)} %composite.2.refs_0_), channel_id=1, source_target_pairs={{0,24},{4,28},{8,0},{12,4},{16,8},{20,12},{24,16},{28,20},{1,25},{... | collective-permute-start | bytes 294920 | tf_op jit(solution)/shard_map/ppermute | solution.py:194
  82.2 1.1 collective-permute-start.12
  83.2 4.6 %collective-permute-done.26.refs_12_ = f32[3,8,1024]{2,1,0:T(8,128)S(1)} collective-permute-done((f32[3,8,1024]{2,1,0:T(8,128)S(1)}, f32[3,8,1024]{2,1,0:T(8,128)S(1)}, u32[]{:S(2)}, u32[]{:S(2)}) %collective-permute-start.26) | collective-permute-done | bytes 98336 | tf_op jit(solution)/shard_map/ppermute | solution.py:194
  88.7 6.3 %collective-permute-done.12.refs_4_ = f32[3,8,1024]{2,1,0:T(8,128)S(1)} collective-permute-done((f32[3,8,1024]{2,1,0:T(8,128)S(1)}, f32[3,8,1024]{2,1,0:T(8,128)S(1)}, u32[]{:S(2)}, u32[]{:S(2)}) %collective-permute-start.12) | collective-permute-done | bytes 98336 | tf_op jit(solution)/shard_map/ppermute | solution.py:194
  98.1 49.6 %place.1 = f32[3,64,2048]{2,1,0:T(8,128)} custom-call(s32[2]{0:T(128)} %copy-done.3, f32[3,8,1024]{2,1,0:T(8,128)} %copy-done.1, f32[3,8,1024]{2,1,0:T(8,128)} %copy-done.15, f32[3,8,1024]{2,1,0:T(8,128)} %copy-done.14, f32[3,8,1024]{2,1,0:T(8,128)} %copy-done.21, f32[3,8,1024]{2,1,0:T(8,128)} %copy-done.13, f32[3,8,1024]{2,1,0:T(8,128)} %copy-done.20, ...), custom_call_target="tpu_custom_call" | custom-call | bytes 3145728 | tf_op jit(solution)/shard_map/place/pallas_call | solution.py:246
  (87 shorter events, 7.1 us)
Async XLA Ops:
  1.8 8.3 %collective-permute-start.1 = (f32[16,1,2048]{2,1,0:T(1,128)S(1)}, f32[16,1,2048]{2,1,0:T(1,128)S(1)}, u32[]{:S(2)}, u32[]{:S(2)}) collective-permute-start(f32[16,1,2048]{2,1,0:T(1,128)S(1)} %get-tuple-element.21), channel_id=1, source_target_pairs={{1,0},{2,1},{3,2},{5,4},{6,5},{7,6},{9,8},{10,9},{11,10},{13,12},{... | collective-permute-start | bytes 393224 | tf_op jit(solution)/shard_map/ppermute | solution.py:198
  3.1 8.2 %collective-permute-start = (f32[16,1,2048]{2,1,0:T(1,128)S(1)}, f32[16,1,2048]{2,1,0:T(1,128)S(1)}, u32[]{:S(2)}, u32[]{:S(2)}) collective-permute-start(f32[16,1,2048]{2,1,0:T(1,128)S(1)} %get-tuple-element.22), channel_id=1, source_target_pairs={{0,1},{1,2},{2,3},{4,5},{5,6},{6,7},{8,9},{9,10},{10,11},{12,13},{... | collective-permute-start | bytes 393224 | tf_op jit(solution)/shard_map/ppermute | solution.py:197
  24.9 15.5 %collective-permute-start.16 = (f32[2,4,8,1024]{3,2,1,0:T(8,128)S(1)}, f32[2,4,8,1024]{3,2,1,0:T(8,128)S(1)}, u32[]{:S(2)}, u32[]{:S(2)}) collective-permute-start(f32[2,4,8,1024]{3,2,1,0:T(8,128)S(1)} %get-tuple-element.18), channel_id=1, source_target_pairs={{0,8},{4,12},{8,16},{12,20},{16,24},{20,28},{24,0},{28,4},{1,9},{5... | collective-permute-start | bytes 786440 | tf_op jit(solution)/shard_map/ppermute | solution.py:194
  26.8 21.5 %collective-permute-start.17 = (f32[2,4,8,1024]{3,2,1,0:T(8,128)S(1)}, f32[2,4,8,1024]{3,2,1,0:T(8,128)S(1)}, u32[]{:S(2)}, u32[]{:S(2)}) collective-permute-start(f32[2,4,8,1024]{3,2,1,0:T(8,128)S(1)} %get-tuple-element.19), channel_id=1, source_target_pairs={{0,16},{4,20},{8,24},{12,28},{16,0},{20,4},{24,8},{28,12},{1,17},{... | collective-permute-start | bytes 786440 | tf_op jit(solution)/shard_map/ppermute | solution.py:194
  29.4 33.9 %collective-permute-start.18 = (f32[2,4,8,1024]{3,2,1,0:T(8,128)S(1)}, f32[2,4,8,1024]{3,2,1,0:T(8,128)S(1)}, u32[]{:S(2)}, u32[]{:S(2)}) collective-permute-start(f32[2,4,8,1024]{3,2,1,0:T(8,128)S(1)} %get-tuple-element.20), channel_id=1, source_target_pairs={{0,24},{4,28},{8,0},{12,4},{16,8},{20,12},{24,16},{28,20},{1,25},{... | collective-permute-start | bytes 786440 | tf_op jit(solution)/shard_map/ppermute | solution.py:194
  30.8 32.5 %collective-permute-start.19 = (f32[2,4,8,1024]{3,2,1,0:T(8,128)S(1)}, f32[2,4,8,1024]{3,2,1,0:T(8,128)S(1)}, u32[]{:S(2)}, u32[]{:S(2)}) collective-permute-start(f32[2,4,8,1024]{3,2,1,0:T(8,128)S(1)} %get-tuple-element.17.refs_0_), channel_id=1, source_target_pairs={{0,4},{4,0},{8,12},{12,8},{16,20},{20,16},{24,28},{28,24},{1,5},{5... | collective-permute-start | bytes 786440 | tf_op jit(solution)/shard_map/ppermute | solution.py:191
  39.7 24.1 %collective-permute-start.2 = (f32[2,4,8,1024]{3,2,1,0:T(8,128)S(1)}, f32[2,4,8,1024]{3,2,1,0:T(8,128)S(1)}, u32[]{:S(2)}, u32[]{:S(2)}) collective-permute-start(f32[2,4,8,1024]{3,2,1,0:T(8,128)S(1)} %get-tuple-element.14), channel_id=1, source_target_pairs={{0,8},{4,12},{8,16},{12,20},{16,24},{20,28},{24,0},{28,4},{1,9},{5... | collective-permute-start | bytes 786440 | tf_op jit(solution)/shard_map/ppermute | solution.py:194
  40.4 27.5 %collective-permute-start.3 = (f32[2,4,8,1024]{3,2,1,0:T(8,128)S(1)}, f32[2,4,8,1024]{3,2,1,0:T(8,128)S(1)}, u32[]{:S(2)}, u32[]{:S(2)}) collective-permute-start(f32[2,4,8,1024]{3,2,1,0:T(8,128)S(1)} %get-tuple-element.15), channel_id=1, source_target_pairs={{0,16},{4,20},{8,24},{12,28},{16,0},{20,4},{24,8},{28,12},{1,17},{... | collective-permute-start | bytes 786440 | tf_op jit(solution)/shard_map/ppermute | solution.py:194
  48.4 22.1 %collective-permute-start.4 = (f32[2,4,8,1024]{3,2,1,0:T(8,128)S(1)}, f32[2,4,8,1024]{3,2,1,0:T(8,128)S(1)}, u32[]{:S(2)}, u32[]{:S(2)}) collective-permute-start(f32[2,4,8,1024]{3,2,1,0:T(8,128)S(1)} %get-tuple-element.16), channel_id=1, source_target_pairs={{0,24},{4,28},{8,0},{12,4},{16,8},{20,12},{24,16},{28,20},{1,25},{... | collective-permute-start | bytes 786440 | tf_op jit(solution)/shard_map/ppermute | solution.py:194
  63.3 7.2 %collective-permute-start.20 = (f32[2,4,8,1024]{3,2,1,0:T(8,128)S(1)}, f32[2,4,8,1024]{3,2,1,0:T(8,128)S(1)}, u32[]{:S(2)}, u32[]{:S(2)}) collective-permute-start(f32[2,4,8,1024]{3,2,1,0:T(8,128)S(1)} %collective-permute-done.16.refs_1_), channel_id=1, source_target_pairs={{0,4},{4,0},{8,12},{12,8},{16,20},{20,16},{24,28},{28,24},{1,5},{5... | collective-permute-start | bytes 786440 | tf_op jit(solution)/shard_map/ppermute | solution.py:191
  63.3 7.7 %collective-permute-start.21 = (f32[2,4,8,1024]{3,2,1,0:T(8,128)S(1)}, f32[2,4,8,1024]{3,2,1,0:T(8,128)S(1)}, u32[]{:S(2)}, u32[]{:S(2)}) collective-permute-start(f32[2,4,8,1024]{3,2,1,0:T(8,128)S(1)} %collective-permute-done.17.refs_2_), channel_id=1, source_target_pairs={{0,4},{4,0},{8,12},{12,8},{16,20},{20,16},{24,28},{28,24},{1,5},{5... | collective-permute-start | bytes 786440 | tf_op jit(solution)/shard_map/ppermute | solution.py:191
  63.8 7.2 %collective-permute-start.22 = (f32[2,4,8,1024]{3,2,1,0:T(8,128)S(1)}, f32[2,4,8,1024]{3,2,1,0:T(8,128)S(1)}, u32[]{:S(2)}, u32[]{:S(2)}) collective-permute-start(f32[2,4,8,1024]{3,2,1,0:T(8,128)S(1)} %collective-permute-done.18.refs_3_), channel_id=1, source_target_pairs={{0,4},{4,0},{8,12},{12,8},{16,20},{20,16},{24,28},{28,24},{1,5},{5... | collective-permute-start | bytes 786440 | tf_op jit(solution)/shard_map/ppermute | solution.py:191
  67.9 9.2 %collective-permute-start.5 = (f32[2,4,8,1024]{3,2,1,0:T(8,128)S(1)}, f32[2,4,8,1024]{3,2,1,0:T(8,128)S(1)}, u32[]{:S(2)}, u32[]{:S(2)}) collective-permute-start(f32[2,4,8,1024]{3,2,1,0:T(8,128)S(1)} %get-tuple-element.13.refs_0_), channel_id=1, source_target_pairs={{0,4},{4,0},{8,12},{12,8},{16,20},{20,16},{24,28},{28,24},{1,5},{5... | collective-permute-start | bytes 786440 | tf_op jit(solution)/shard_map/ppermute | solution.py:191
  70.5 7.3 %collective-permute-start.7 = (f32[2,4,8,1024]{3,2,1,0:T(8,128)S(1)}, f32[2,4,8,1024]{3,2,1,0:T(8,128)S(1)}, u32[]{:S(2)}, u32[]{:S(2)}) collective-permute-start(f32[2,4,8,1024]{3,2,1,0:T(8,128)S(1)} %collective-permute-done.3.refs_2_), channel_id=1, source_target_pairs={{0,4},{4,0},{8,12},{12,8},{16,20},{20,16},{24,28},{28,24},{1,5},{5... | collective-permute-start | bytes 786440 | tf_op jit(solution)/shard_map/ppermute | solution.py:191
  72.1 10.1 %collective-permute-start.28 = (f32[3,8,1024]{2,1,0:T(8,128)S(1)}, f32[3,8,1024]{2,1,0:T(8,128)S(1)}, u32[]{:S(2)}, u32[]{:S(2)}) collective-permute-start(f32[3,8,1024]{2,1,0:T(8,128)S(1)} %composite.3.refs_8_), channel_id=1, source_target_pairs={{0,24},{4,28},{8,0},{12,4},{16,8},{20,12},{24,16},{28,20},{1,25},{... | collective-permute-start | bytes 294920 | tf_op jit(solution)/shard_map/ppermute | solution.py:194
  77.1 10.7 %collective-permute-start.26 = (f32[3,8,1024]{2,1,0:T(8,128)S(1)}, f32[3,8,1024]{2,1,0:T(8,128)S(1)}, u32[]{:S(2)}, u32[]{:S(2)}) collective-permute-start(f32[3,8,1024]{2,1,0:T(8,128)S(1)} %composite.3.refs_8_), channel_id=1, source_target_pairs={{0,16},{4,20},{8,24},{12,28},{16,0},{20,4},{24,8},{28,12},{1,17},{... | collective-permute-start | bytes 294920 | tf_op jit(solution)/shard_map/ppermute | solution.py:194
  77.2 10.7 %collective-permute-start.24 = (f32[3,8,1024]{2,1,0:T(8,128)S(1)}, f32[3,8,1024]{2,1,0:T(8,128)S(1)}, u32[]{:S(2)}, u32[]{:S(2)}) collective-permute-start(f32[3,8,1024]{2,1,0:T(8,128)S(1)} %composite.3.refs_8_), channel_id=1, source_target_pairs={{0,8},{4,12},{8,16},{12,20},{16,24},{20,28},{24,0},{28,4},{1,9},{5... | collective-permute-start | bytes 294920 | tf_op jit(solution)/shard_map/ppermute | solution.py:194
  77.8 10.1 %collective-permute-start.23 = (f32[3,8,1024]{2,1,0:T(8,128)S(1)}, f32[3,8,1024]{2,1,0:T(8,128)S(1)}, u32[]{:S(2)}, u32[]{:S(2)}) collective-permute-start(f32[3,8,1024]{2,1,0:T(8,128)S(1)} %composite.3.refs_8_), channel_id=1, source_target_pairs={{0,4},{4,0},{8,12},{12,8},{16,20},{20,16},{24,28},{28,24},{1,5},{5... | collective-permute-start | bytes 294920 | tf_op jit(solution)/shard_map/ppermute | solution.py:191
  78.9 9.7 %collective-permute-start.14 = (f32[3,8,1024]{2,1,0:T(8,128)S(1)}, f32[3,8,1024]{2,1,0:T(8,128)S(1)}, u32[]{:S(2)}, u32[]{:S(2)}) collective-permute-start(f32[3,8,1024]{2,1,0:T(8,128)S(1)} %composite.2.refs_0_), channel_id=1, source_target_pairs={{0,24},{4,28},{8,0},{12,4},{16,8},{20,12},{24,16},{28,20},{1,25},{... | collective-permute-start | bytes 294920 | tf_op jit(solution)/shard_map/ppermute | solution.py:194
  82.2 12.9 %collective-permute-start.12 = (f32[3,8,1024]{2,1,0:T(8,128)S(1)}, f32[3,8,1024]{2,1,0:T(8,128)S(1)}, u32[]{:S(2)}, u32[]{:S(2)}) collective-permute-start(f32[3,8,1024]{2,1,0:T(8,128)S(1)} %composite.2.refs_0_), channel_id=1, source_target_pairs={{0,16},{4,20},{8,24},{12,28},{16,0},{20,4},{24,8},{28,12},{1,17},{... | collective-permute-start | bytes 294920 | tf_op jit(solution)/shard_map/ppermute | solution.py:194
  87.8 7.2 %collective-permute-start.10 = (f32[3,8,1024]{2,1,0:T(8,128)S(1)}, f32[3,8,1024]{2,1,0:T(8,128)S(1)}, u32[]{:S(2)}, u32[]{:S(2)}) collective-permute-start(f32[3,8,1024]{2,1,0:T(8,128)S(1)} %composite.2.refs_0_), channel_id=1, source_target_pairs={{0,8},{4,12},{8,16},{12,20},{16,24},{20,28},{24,0},{28,4},{1,9},{5... | collective-permute-start | bytes 294920 | tf_op jit(solution)/shard_map/ppermute | solution.py:194
  87.8 7.7 %collective-permute-start.9 = (f32[3,8,1024]{2,1,0:T(8,128)S(1)}, f32[3,8,1024]{2,1,0:T(8,128)S(1)}, u32[]{:S(2)}, u32[]{:S(2)}) collective-permute-start(f32[3,8,1024]{2,1,0:T(8,128)S(1)} %composite.2.refs_0_), channel_id=1, source_target_pairs={{0,4},{4,0},{8,12},{12,8},{16,20},{20,16},{24,28},{28,24},{1,5},{5... | collective-permute-start | bytes 294920 | tf_op jit(solution)/shard_map/ppermute | solution.py:191
  87.9 7.7 %collective-permute-start.29 = (f32[3,8,1024]{2,1,0:T(8,128)S(1)}, f32[3,8,1024]{2,1,0:T(8,128)S(1)}, u32[]{:S(2)}, u32[]{:S(2)}) collective-permute-start(f32[3,8,1024]{2,1,0:T(8,128)S(1)} %collective-permute-done.28.refs_14_), channel_id=1, source_target_pairs={{0,4},{4,0},{8,12},{12,8},{16,20},{20,16},{24,28},{28,24},{1,5},{5... | collective-permute-start | bytes 294920 | tf_op jit(solution)/shard_map/ppermute | solution.py:191
  88.6 7.4 %collective-permute-start.27 = (f32[3,8,1024]{2,1,0:T(8,128)S(1)}, f32[3,8,1024]{2,1,0:T(8,128)S(1)}, u32[]{:S(2)}, u32[]{:S(2)}) collective-permute-start(f32[3,8,1024]{2,1,0:T(8,128)S(1)} %collective-permute-done.26.refs_12_), channel_id=1, source_target_pairs={{0,4},{4,0},{8,12},{12,8},{16,20},{20,16},{24,28},{28,24},{1,5},{5... | collective-permute-start | bytes 294920 | tf_op jit(solution)/shard_map/ppermute | solution.py:191
  (28 other events, 274.4 us)

commit v2 on v0

v2 whole, which is shorter than its diff:
```python
import functools

import jax
import jax.numpy as jnp
from jax import lax
from jax.experimental import pallas as pl
from jax.experimental.pallas import tpu as pltpu
from jax.sharding import PartitionSpec as P

background = 0.25
optical_total = 2.0

SUB = 8
LANE = 128
CORES = 2
INNER = ((1, 3), (4, 3))
VMEM_LIMIT = 24 * 2**20


def call(kernel, operands, specs, events=(), **options):
    def with_events(*refs):
        kernel(*refs[: len(operands)], *refs[len(operands) + len(events) :])

    return pl.pallas_call(
        with_events,
        in_specs=specs + [pl.BlockSpec(memory_space=pl.ANY)] * len(events),
        compiler_params=pltpu.CompilerParams(vmem_limit_bytes=VMEM_LIMIT),
        **options,
    )(*operands, *events)


def lasting(microseconds):
    return pl.CostEstimate(flops=0, bytes_accessed=int(microseconds * 3.69e6), transcendentals=0)


def tiles_of(runs):
    return sum(number for _, number in runs)


def edges_kernel(field_ref, first_ref, last_ref, buffer, sem):
    rows = field_ref.shape[1]
    copies = [
        pltpu.make_async_copy(field_ref.at[:, pl.ds(row, SUB), :], buffer.at[i], sem.at[i])
        for i, row in enumerate((0, rows - SUB))
    ]
    for copy in copies:
        copy.start()
    for copy in copies:
        copy.wait()
    first_ref[...] = buffer[0, :, :1, :]
    last_ref[...] = buffer[1, :, SUB - 1 :, :]


def render_kernel(runs, tiles, chips, scale, where_ref, transfer_ref, light_ref, field_ref, *refs):
    out_refs, (padded, sem) = refs[-2 - chips : -2], refs[-2:]
    edges = list(refs[: -2 - chips])
    planes, _, columns = field_ref.shape
    part = out_refs[0].shape[3]
    my_chip, my_core = where_ref[0], where_ref[1]

    def tile_copy(tile, slot):
        return pltpu.make_async_copy(
            field_ref.at[:, pl.ds(pl.multiple_of(tile * SUB, SUB), SUB), :],
            padded.at[:, pl.ds(pl.multiple_of(slot * SUB, SUB), SUB), pl.ds(LANE, columns)],
            sem.at[slot],
        )

    layout, slot, written = [], 0, 0
    for first, number in runs:
        low, high = max(first - 1, 0), min(first + number + 1, tiles)
        before = edges.pop(0) if first == 0 else None
        behind = edges.pop(0) if first + number == tiles else None
        layout.append((first, number, low, high, slot, written, before, behind))
        for tile in range(low, high):
            tile_copy(tile, slot + tile - low).start()
        slot, written = slot + high - low, written + number
    rim = jnp.zeros((planes, padded.shape[1], LANE), jnp.float32)
    padded[:, :, :LANE] = rim
    padded[:, :, LANE + columns :] = rim

    light = [0.5 * light_ref[i] for i in range(3)]
    slope = [0.5 * transfer_ref[0, c] for c in range(3)]
    offset = [0.5 * transfer_ref[1, c] for c in range(3)]
    sub = lax.broadcasted_iota(jnp.int32, (SUB, LANE), 0)
    lane = lax.broadcasted_iota(jnp.int32, (SUB, LANE), 1)
    top, bottom = sub == 0, sub == SUB - 1
    leftmost, rightmost = lane == 0, lane == LANE - 1
    vregs = part // LANE

    def march(slot, out_row, before_ref, behind_ref, column, relative, out_ref):
        def load(plane, shift, vreg):
            ref = {-1: before_ref, 1: behind_ref}.get(shift)
            if ref is not None:
                lanes = pl.ds(pl.multiple_of(column + vreg * LANE, LANE), LANE)
                return jnp.broadcast_to(ref[plane, :, lanes], (SUB, LANE))
            return padded[
                plane,
                pl.ds(pl.multiple_of((slot + shift) * SUB, SUB), SUB),
                pl.ds(pl.multiple_of(column + (1 + vreg) * LANE, LANE), LANE),
            ]

        zero = jnp.zeros((SUB, LANE), jnp.float32)
        depth = [zero] * vregs
        left_over = [zero + 1.0] * vregs
        total = [zero] * vregs
        sums = [[zero] * vregs for _ in range(3)]
        here = [load(0, 0, v) for v in range(-1, vregs + 1)]
        before = here
        for plane in range(planes):
            after = [load(plane + 1, 0, v) for v in range(-1, vregs + 1)] if plane + 1 < planes else here
            for v in range(vregs):
                value = here[v + 1]
                up = pltpu.roll(jnp.where(bottom, load(plane, -1, v), value), 1, 0)
                down = pltpu.roll(jnp.where(top, load(plane, 1, v), value), SUB - 1, 0)
                left = pltpu.roll(jnp.where(rightmost, here[v], value), 1, 1)
                right = pltpu.roll(jnp.where(leftmost, here[v + 2], value), LANE - 1, 1)
                shade = jnp.tanh(
                    light[0] * (after[v + 1] - before[v + 1]) + light[1] * (down - up) + light[2] * (right - left)
                )
                depth[v] = depth[v] + jnp.log(1.0 + jnp.exp(value + value))
                through = jnp.exp(depth[v] * -scale)
                lost = left_over[v] - through
                left_over[v] = through
                weight = lost + lost * shade
                total[v] = total[v] + weight
                for c in range(3):
                    sums[c][v] = sums[c][v] + weight * jnp.tanh(slope[c] * value + offset[c])
            before, here = here, after
        for v in range(vregs):
            lanes = pl.ds(v * LANE, LANE)
            for c in range(3):
                out_ref[relative, c, pl.ds(out_row, SUB), lanes] = 0.25 * (total[v] + sums[c][v])
            out_ref[relative, 3, pl.ds(out_row, SUB), lanes] = depth[v] * scale

    for k, out_ref in enumerate(out_refs):
        chip = lax.rem(my_chip + k, chips)
        for first, number, low, high, slot, written, before, behind in layout:
            if k == 0:
                for tile in range(low, min(first + 1, high)):
                    tile_copy(tile, slot + tile - low).wait()

            def one_tile(index, carry, k=k, out_ref=out_ref, chip=chip, run=(first, low, high, slot, written, before, behind)):
                first, low, high, slot, written, before, behind = run
                here = slot + first - low + index

                if k == 0:

                    @pl.when(first + index + 1 < high)
                    def _():
                        tile_copy(first + index + 1, here + 1).wait()

                def one(relative, carry):
                    owner = chip * CORES + lax.rem(my_core + relative, CORES)
                    out_row = pl.multiple_of((written + index) * SUB, SUB)
                    march(here, out_row, before, behind, owner * part, relative, out_ref)
                    return carry

                return lax.fori_loop(0, CORES, one, carry)

            lax.fori_loop(0, number, one_tile, 0)


def composite_kernel(chips, where_ref, rank_ref, *refs):
    own, other, out_ref = refs[:chips], refs[chips : 2 * chips], refs[2 * chips]
    my_chip, my_core = where_ref[0], where_ref[1]
    blocks, ranks = [], []
    for k in range(chips):
        chip = lax.rem(my_chip + chips - k, chips)
        for core, ref in ((my_core, own[k]), (CORES - 1 - my_core, other[k])):
            blocks.append(ref)
            ranks.append(rank_ref[chip * CORES + core])
    count = len(blocks)
    ahead = [[(ranks[j] < ranks[i]).astype(jnp.float32) for j in range(count)] for i in range(count)]
    columns = out_ref.shape[2] // LANE

    def one(index, carry):
        row = index // columns
        at = (
            pl.ds(pl.multiple_of(row * SUB, SUB), SUB),
            pl.ds(pl.multiple_of((index - row * columns) * LANE, LANE), LANE),
        )
        depths = [ref[(0, 3, *at)] for ref in blocks]
        sums = [background * jnp.exp(-functools.reduce(jnp.add, depths))] * 3
        for i in range(count):
            front = functools.reduce(jnp.add, [ahead[i][j] * depths[j] for j in range(count) if j != i])
            weight = jnp.exp(-front)
            for c in range(3):
                sums[c] = sums[c] + weight * blocks[i][(0, c, *at)]
        for c in range(3):
            out_ref[(c, *at)] = sums[c]
        return carry

    lax.fori_loop(0, out_ref.shape[1] // SUB * columns, one, 0)


def place_kernel(chips, chunks, where_ref, *refs):
    count = len(chunks) * chips * CORES
    blocks, out_ref, sem = refs[:count], refs[count], refs[count + 1]
    my_chip, my_core = where_ref[0], where_ref[1]
    copies = []
    for i, runs in enumerate(chunks):
        for k in range(chips):
            chip = lax.rem(my_chip + chips - k, chips)
            for j, core in enumerate((my_core, CORES - 1 - my_core)):
                block = blocks[(i * chips + k) * CORES + j]
                part = block.shape[2]
                column = pl.multiple_of((chip * CORES + core) * part, LANE)
                written = 0
                for first, number in runs:
                    copy = pltpu.make_async_copy(
                        block.at[:, pl.ds(written * SUB, number * SUB), :],
                        out_ref.at[:, pl.ds(first * SUB, number * SUB), pl.ds(column, part)],
                        sem.at[len(copies)],
                    )
                    copy.start()
                    copies.append(copy)
                    written += number
    for copy in copies:
        copy.wait()


def body(scalar_field, depth_rank, transfer, light_dir):
    planes, rows, columns = scalar_field.shape
    wide, narrow = lax.axis_size("wide"), lax.axis_size("narrow")
    chips, tiles, part = wide // CORES, rows // SUB, columns // wide
    scale = optical_total / (planes * wide)
    index = lax.axis_index("wide")
    where = jnp.stack([index // CORES, index % CORES]).astype(jnp.int32)
    inner = [(run,) for run in INNER] if tiles == 8 else [((1, tiles - 2),)]
    chunks = inner + [((0, 1), (tiles - 1, 1))]

    smem = pl.BlockSpec(memory_space=pltpu.SMEM)
    vmem = pl.BlockSpec(memory_space=pltpu.VMEM)
    hbm = pl.BlockSpec(memory_space=pltpu.HBM)
    field = pltpu.with_memory_space_constraint(scalar_field, pltpu.HBM)

    def swap(value):
        return lax.ppermute(value, "wide", [(i, i ^ 1) for i in range(wide)])

    def send(value, k):
        return lax.ppermute(value, "wide", [(i, (i + k * CORES) % wide) for i in range(wide)])

    def render(runs, edges=(), events=()):
        slots = sum(min(first + number + 1, tiles) - max(first - 1, 0) for first, number in runs)
        block = pltpu.VMEM((CORES, 4, tiles_of(runs) * SUB, part), jnp.float32)
        return call(
            functools.partial(render_kernel, runs, tiles, chips, scale),
            [where, transfer, light_dir, field, *edges],
            [smem] * 3 + [hbm] + [vmem] * len(edges),
            events,
            out_shape=[block] * chips,
            out_specs=[vmem] * chips,
            scratch_shapes=[
                pltpu.VMEM((planes, slots * SUB, columns + 2 * LANE), jnp.float32),
                pltpu.SemaphoreType.DMA((slots,)),
            ],
            cost_estimate=lasting(2.5 * tiles_of(runs)),
            name="render",
        )

    def edge_rows(events):
        edge = pltpu.VMEM((planes, 1, columns), jnp.float32)
        first_row, last_row = call(
            edges_kernel,
            [field],
            [hbm],
            events,
            out_shape=[edge] * 2,
            out_specs=[vmem] * 2,
            scratch_shapes=[pltpu.VMEM((2, planes, SUB, columns), jnp.float32), pltpu.SemaphoreType.DMA((2,))],
            cost_estimate=lasting(1.2),
            name="edges",
        )
        up = [(i, i + 1) for i in range(narrow - 1)]
        return lax.ppermute(last_row, "narrow", up), lax.ppermute(first_row, "narrow", [(j, i) for i, j in up])

    def composite(runs, own, other, events):
        return call(
            functools.partial(composite_kernel, chips),
            [where, depth_rank, *own, *other],
            [smem] * 2 + [vmem] * (2 * chips),
            events,
            out_shape=pltpu.VMEM((3, tiles_of(runs) * SUB, part), jnp.float32),
            out_specs=vmem,
            cost_estimate=lasting(1.0),
            name="composite",
        )

    sent, last, edges = [], (), ()
    for i, runs in enumerate(chunks):
        if i == len(chunks) - 1:
            edges = edge_rows(last)
        blocks = render(runs, edges, last)
        last = [blocks[0]]
        sent.append([blocks[0]] + [send(blocks[k], k) for k in range(1, chips)])

    finished = []
    for runs, own in zip(chunks, sent):
        other = [swap(value[1:]) for value in own]
        tile = composite(runs, own, other, last)
        last = [tile]
        for k in range(chips):
            value = send(tile, k) if k else tile
            finished += [value, swap(value)]

    return call(
        functools.partial(place_kernel, chips, chunks),
        [where, *finished],
        [smem] + [vmem] * len(finished),
        out_shape=jax.ShapeDtypeStruct((3, rows, columns), jnp.float32),
        out_specs=hbm,
        scratch_shapes=[pltpu.SemaphoreType.DMA((wide * sum(len(runs) for runs in chunks),))],
        cost_estimate=lasting(2.0),
        name="place",
    )


def solution(mesh):
    return jax.shard_map(
        body,
        mesh=mesh,
        in_specs=(P("wide", "narrow", None), P(), P(), P()),
        out_specs=P(None, "narrow", None),
        check_vma=False,
    )
```

time: 201 us -> 98.9 us (0.49)
  waiting for transfers between devices: 93 us -> 12.2 us
  starting transfers between devices: 7.04 us -> 56.8 us
  other arithmetic: 44.5 us -> 0.07 us
  local copies, waits for them, and re-layouts: 34.1 us -> 1.42 us
  Pallas kernels: 0 us -> 28 us
  between operations: 15.1 us -> 0.28 us
  matrix products: 7.1 us -> 0 us
    all_gather x2 -> x0, waiting for transfers between devices: 62.4 us -> none  [the longest x1 39.2 us: body(): pieces = lax.all_gather(brick_depth[None], 'wide', axis=0, tiled=True)]
    ppermute x2 -> x44, starting transfers between devices: 6.77 us -> 56.8 us  [the longest x18 45.7 us: send(): lax.ppermute(value, 'wide', [(i, (i + k * CORES) % wide) for i in range(w...]
    slice x5 -> x12, local copies, waits for them, and re-layouts: 30.8 us -> 0.09 us  [body(): other = [swap(value[1:]) for value in own]]
    reduce_scatter x1 -> x0, waiting for transfers between devices: 30.5 us -> none  [body(): lax.psum_scatter(weighted, 'wide', scatter_dimension=2, tiled=True)]
    another operation x1, other arithmetic: 29.9 us -> 0.07 us  [body(): where = jnp.stack([index // CORES, index % CORES]).astype(jnp.int32)]
    pallas_call x0 -> x8, Pallas kernels: none -> 28 us  [call(): pl.pallas_call(with_events, in_specs=specs + [pl.BlockSpec(memory_space=p...]
    ppermute x2 -> x44, waiting for transfers between devices: 0.01 us -> 12.2 us  [the longest x18 9.13 us: send(): lax.ppermute(value, 'wide', [(i, (i + k * CORES) % wide) for i in range(w...]
    reduce_sum x2 -> x0, other arithmetic: 11.4 us -> none  [the longest x1 8.96 us: render(): return jnp.sum(weights[None] * colors, axis=1)]
  transfers between devices with their start and end apart: 5 -> 44, of which waited for: 3 -> 10; matrix products, arithmetic and copies ran while one was open for 20% -> 0% of each run, Pallas kernels for 0% -> 19%
where the time goes in v2:
time: 98.9 us; the launch traced here: 98.7 us
  starting transfers between devices  56.8 us (57%)
  Pallas kernels  28 us (28%)
  waiting for transfers between devices  12.2 us (12%)
  local copies, waits for them, and re-layouts  1.42 us (1%)
    ppermute x18, starting transfers between devices, send(): lax.ppermute(value, 'wide', [(i, (i + k * CORES) % wide) for i in range(w...  45.7 us
    pallas_call x8, Pallas kernels, call(): pl.pallas_call(with_events, in_specs=specs + [pl.BlockSpec(memory_space=p...  28 us
    ppermute x18, waiting for transfers between devices, send(): lax.ppermute(value, 'wide', [(i, (i + k * CORES) % wide) for i in range(w...  9.13 us
    ppermute x24, starting transfers between devices, swap(): return lax.ppermute(value, 'wide', [(i, i ^ 1) for i in range(wide)])  5.38 us
    ppermute x1, starting transfers between devices, edge_rows(): lax.ppermute(last_row, 'narrow', up)  4.42 us
  transfers between devices with their start and end apart: 44, of which 10 were waited for; matrix products, arithmetic and copies ran while one was open for 0% of the time, Pallas kernels for 19%

profile of v2, /device:TPU:0, one launch (start us, length us, event | category | flops | bytes accessed | tf_op | source)
XLA Modules:
  0.0 98.7 jit_solution(4213104853620646498)
XLA Ops:
  1.4 7.7 %render.3 = (f32[2,4,24,256]{3,2,1,0:T(8,128)S(1)}, f32[2,4,24,256]{3,2,1,0:T(8,128)S(1)}, f32[2,4,24,256]{3,2,1,0:T(8,128)S(1)}, f32[2,4,24,256]{3,2,1,0:T(8,128)S(1)}) custom-call(s32[2]{0:T(128)S(1)} %pad_add_fusion.refs_0_, f32[2,3]{1,0:T(2,128)S(1)} %copy-done, f32[3]{0:T(128)S(1)} %copy-done.1, f32[16,64,2048]{2,1,0:T(8,128)} %refs_3_.5), custom_call_target="tpu_custom_call" | custom-call | bytes 27675000 | tf_op jit(solution)/shard_map/render/pallas_call | solution.py:24
  9.7 7.7 %render.4 = (f32[2,4,24,256]{3,2,1,0:T(8,128)S(1)}, f32[2,4,24,256]{3,2,1,0:T(8,128)S(1)}, f32[2,4,24,256]{3,2,1,0:T(8,128)S(1)}, f32[2,4,24,256]{3,2,1,0:T(8,128)S(1)}) custom-call(s32[2]{0:T(128)S(1)} %pad_add_fusion.refs_0_, f32[2,3]{1,0:T(2,128)S(1)} %copy-done, f32[3]{0:T(128)S(1)} %copy-done.1, f32[16,64,2048]{2,1,0:T(8,128)} %refs_3_.5, ...), custom_call_target="tpu_custom_call" | custom-call | bytes 27675000 | tf_op jit(solution)/shard_map/render/pallas_call | solution.py:24
  17.4 1.6 %edges.1 = (f32[16,1,2048]{2,1,0:T(1,128)S(1)}, f32[16,1,2048]{2,1,0:T(1,128)S(1)}) custom-call(f32[16,64,2048]{2,1,0:T(8,128)} %refs_3_.5, f32[2,4,24,256]{3,2,1,0:T(8,128)S(1)} %get-tuple-element.23.refs_1_.refs_6_.refs_2_), custom_call_target="tpu_custom_call" | custom-call | bytes 4428000 | tf_op jit(solution)/shard_map/edges/pallas_call | solution.py:24
  19.0 4.4 %collective-permute-start.7 = (f32[16,1,2048]{2,1,0:T(1,128)S(1)}, f32[16,1,2048]{2,1,0:T(1,128)S(1)}, u32[]{:S(2)}, u32[]{:S(2)}) collective-permute-start(f32[16,1,2048]{2,1,0:T(1,128)S(1)} %get-tuple-element.24), channel_id=1, source_target_pairs={{0,1},{1,2},{2,3},{4,5},{5,6},{6,7},{8,9},{9,10},{10,11},{12,13},{... | collective-permute-start | bytes 393224 | tf_op jit(solution)/shard_map/ppermute | solution.py:275
  23.5 1.6 %collective-permute-start = (f32[2,4,24,256]{3,2,1,0:T(8,128)S(1)}, f32[2,4,24,256]{3,2,1,0:T(8,128)S(1)}, u32[]{:S(2)}, u32[]{:S(2)}) collective-permute-start(f32[2,4,24,256]{3,2,1,0:T(8,128)S(1)} %get-tuple-element.20), channel_id=1, source_target_pairs={{0,8},{4,12},{8,16},{12,20},{16,24},{20,28},{24,0},{28,4},{1,9},{5... | collective-permute-start | bytes 589832 | tf_op jit(solution)/shard_map/ppermute | solution.py:241
  25.1 1.3 %collective-permute-start.8 = (f32[16,1,2048]{2,1,0:T(1,128)S(1)}, f32[16,1,2048]{2,1,0:T(1,128)S(1)}, u32[]{:S(2)}, u32[]{:S(2)}) collective-permute-start(f32[16,1,2048]{2,1,0:T(1,128)S(1)} %get-tuple-element.25), channel_id=1, source_target_pairs={{1,0},{2,1},{3,2},{5,4},{6,5},{7,6},{9,8},{10,9},{11,10},{13,12},{... | collective-permute-start | bytes 393224 | tf_op jit(solution)/shard_map/ppermute | solution.py:275
  26.5 2.7 %collective-permute-start.1 = (f32[2,4,24,256]{3,2,1,0:T(8,128)S(1)}, f32[2,4,24,256]{3,2,1,0:T(8,128)S(1)}, u32[]{:S(2)}, u32[]{:S(2)}) collective-permute-start(f32[2,4,24,256]{3,2,1,0:T(8,128)S(1)} %get-tuple-element.21), channel_id=1, source_target_pairs={{0,16},{4,20},{8,24},{12,28},{16,0},{20,4},{24,8},{28,12},{1,17},{... | collective-permute-start | bytes 589832 | tf_op jit(solution)/shard_map/ppermute | solution.py:241
  29.1 1.3 %collective-permute-start.2 = (f32[2,4,24,256]{3,2,1,0:T(8,128)S(1)}, f32[2,4,24,256]{3,2,1,0:T(8,128)S(1)}, u32[]{:S(2)}, u32[]{:S(2)}) collective-permute-start(f32[2,4,24,256]{3,2,1,0:T(8,128)S(1)} %get-tuple-element.22), channel_id=1, source_target_pairs={{0,24},{4,28},{8,0},{12,4},{16,8},{20,12},{24,16},{28,20},{1,25},{... | collective-permute-start | bytes 589832 | tf_op jit(solution)/shard_map/ppermute | solution.py:241
  31.2 1.1 %collective-permute-done.8.refs_5_ = f32[16,1,2048]{2,1,0:T(1,128)S(1)} collective-permute-done((f32[16,1,2048]{2,1,0:T(1,128)S(1)}, f32[16,1,2048]{2,1,0:T(1,128)S(1)}, u32[]{:S(2)}, u32[]{:S(2)}) %collective-permute-start.8) | collective-permute-done | bytes 131104 | tf_op jit(solution)/shard_map/ppermute | solution.py:275
  32.3 2.6 %collective-permute-start.17 = (f32[2,4,24,256]{3,2,1,0:T(8,128)S(1)}, f32[2,4,24,256]{3,2,1,0:T(8,128)S(1)}, u32[]{:S(2)}, u32[]{:S(2)}) collective-permute-start(f32[2,4,24,256]{3,2,1,0:T(8,128)S(1)} %get-tuple-element.28), channel_id=1, source_target_pairs={{0,16},{4,20},{8,24},{12,28},{16,0},{20,4},{24,8},{28,12},{1,17},{... | collective-permute-start | bytes 589832 | tf_op jit(solution)/shard_map/ppermute | solution.py:241
  34.9 1.3 %collective-permute-start.18 = (f32[2,4,24,256]{3,2,1,0:T(8,128)S(1)}, f32[2,4,24,256]{3,2,1,0:T(8,128)S(1)}, u32[]{:S(2)}, u32[]{:S(2)}) collective-permute-start(f32[2,4,24,256]{3,2,1,0:T(8,128)S(1)} %get-tuple-element.29), channel_id=1, source_target_pairs={{0,24},{4,28},{8,0},{12,4},{16,8},{20,12},{24,16},{28,20},{1,25},{... | collective-permute-start | bytes 589832 | tf_op jit(solution)/shard_map/ppermute | solution.py:241
  36.3 6.0 %render.5 = (f32[2,4,16,256]{3,2,1,0:T(8,128)S(1)}, f32[2,4,16,256]{3,2,1,0:T(8,128)S(1)}, f32[2,4,16,256]{3,2,1,0:T(8,128)S(1)}, f32[2,4,16,256]{3,2,1,0:T(8,128)S(1)}) custom-call(s32[2]{0:T(128)S(1)} %pad_add_fusion.refs_0_, f32[2,3]{1,0:T(2,128)S(1)} %copy-done, f32[3]{0:T(128)S(1)} %copy-done.1, f32[16,64,2048]{2,1,0:T(8,128)} %refs_3_.5, ...), custom_call_target="tpu_custom_call" | custom-call | bytes 18450000 | tf_op jit(solution)/shard_map/render/pallas_call | solution.py:24
  42.2 10.5 %collective-permute-start.30 = (f32[2,4,16,256]{3,2,1,0:T(8,128)S(1)}, f32[2,4,16,256]{3,2,1,0:T(8,128)S(1)}, u32[]{:S(2)}, u32[]{:S(2)}) collective-permute-start(f32[2,4,16,256]{3,2,1,0:T(8,128)S(1)} %get-tuple-element.30), channel_id=1, source_target_pairs={{0,8},{4,12},{8,16},{12,20},{16,24},{20,28},{24,0},{28,4},{1,9},{5... | collective-permute-start | bytes 393224 | tf_op jit(solution)/shard_map/ppermute | solution.py:241
  53.4 7.1 %collective-permute-done.17.refs_4_ = f32[2,4,24,256]{3,2,1,0:T(8,128)S(1)} collective-permute-done((f32[2,4,24,256]{3,2,1,0:T(8,128)S(1)}, f32[2,4,24,256]{3,2,1,0:T(8,128)S(1)}, u32[]{:S(2)}, u32[]{:S(2)}) %collective-permute-start.17) | collective-permute-done | bytes 196640 | tf_op jit(solution)/shard_map/ppermute | solution.py:241
  61.2 4.4 %collective-permute-start.31 = (f32[2,4,16,256]{3,2,1,0:T(8,128)S(1)}, f32[2,4,16,256]{3,2,1,0:T(8,128)S(1)}, u32[]{:S(2)}, u32[]{:S(2)}) collective-permute-start(f32[2,4,16,256]{3,2,1,0:T(8,128)S(1)} %get-tuple-element.31), channel_id=1, source_target_pairs={{0,16},{4,20},{8,24},{12,28},{16,0},{20,4},{24,8},{28,12},{1,17},{... | collective-permute-start | bytes 393224 | tf_op jit(solution)/shard_map/ppermute | solution.py:241
  65.5 2.2 %collective-permute-start.32 = (f32[2,4,16,256]{3,2,1,0:T(8,128)S(1)}, f32[2,4,16,256]{3,2,1,0:T(8,128)S(1)}, u32[]{:S(2)}, u32[]{:S(2)}) collective-permute-start(f32[2,4,16,256]{3,2,1,0:T(8,128)S(1)} %get-tuple-element.32), channel_id=1, source_target_pairs={{0,24},{4,28},{8,0},{12,4},{16,8},{20,12},{24,16},{28,20},{1,25},{... | collective-permute-start | bytes 393224 | tf_op jit(solution)/shard_map/ppermute | solution.py:241
  70.3 1.0 %composite.4.refs_10_.refs_9_ = f32[3,24,256]{2,1,0:T(8,128)S(1)} custom-call(s32[2]{0:T(128)S(1)} %pad_add_fusion.refs_0_, s32[8]{0:T(128)S(1)} %copy-done.2, f32[2,4,24,256]{3,2,1,0:T(8,128)S(1)} %get-tuple-element.23.refs_1_.refs_6_.refs_2_, f32[2,4,24,256]{3,2,1,0:T(8,128)S(1)} %collective-permute-done.16.refs_3_, ...), custom_call_target="tpu_custom_call" | custom-call | bytes 3690000 | tf_op jit(solution)/shard_map/composite/pallas_call | solution.py:24
  72.7 2.4 %collective-permute-start.26 = (f32[3,24,256]{2,1,0:T(8,128)S(1)}, f32[3,24,256]{2,1,0:T(8,128)S(1)}, u32[]{:S(2)}, u32[]{:S(2)}) collective-permute-start(f32[3,24,256]{2,1,0:T(8,128)S(1)} %composite.4.refs_10_.refs_9_), channel_id=1, source_target_pairs={{0,16},{4,20},{8,24},{12,28},{16,0},{20,4},{24,8},{28,12},{1,17},{... | collective-permute-start | bytes 221192 | tf_op jit(solution)/shard_map/ppermute | solution.py:241
  75.1 3.4 %collective-permute-start.28 = (f32[3,24,256]{2,1,0:T(8,128)S(1)}, f32[3,24,256]{2,1,0:T(8,128)S(1)}, u32[]{:S(2)}, u32[]{:S(2)}) collective-permute-start(f32[3,24,256]{2,1,0:T(8,128)S(1)} %composite.4.refs_10_.refs_9_), channel_id=1, source_target_pairs={{0,24},{4,28},{8,0},{12,4},{16,8},{20,12},{24,16},{28,20},{1,25},{... | collective-permute-start | bytes 221192 | tf_op jit(solution)/shard_map/ppermute | solution.py:241
  79.2 1.5 %collective-permute-start.12 = (f32[3,24,256]{2,1,0:T(8,128)S(1)}, f32[3,24,256]{2,1,0:T(8,128)S(1)}, u32[]{:S(2)}, u32[]{:S(2)}) collective-permute-start(f32[3,24,256]{2,1,0:T(8,128)S(1)} %composite.3.refs_10_.refs_1_), channel_id=1, source_target_pairs={{0,16},{4,20},{8,24},{12,28},{16,0},{20,4},{24,8},{28,12},{1,17},{... | collective-permute-start | bytes 221192 | tf_op jit(solution)/shard_map/ppermute | solution.py:241
  80.6 5.0 %collective-permute-start.14 = (f32[3,24,256]{2,1,0:T(8,128)S(1)}, f32[3,24,256]{2,1,0:T(8,128)S(1)}, u32[]{:S(2)}, u32[]{:S(2)}) collective-permute-start(f32[3,24,256]{2,1,0:T(8,128)S(1)} %composite.3.refs_10_.refs_1_), channel_id=1, source_target_pairs={{0,24},{4,28},{8,0},{12,4},{16,8},{20,12},{24,16},{28,20},{1,25},{... | collective-permute-start | bytes 221192 | tf_op jit(solution)/shard_map/ppermute | solution.py:241
  86.6 2.0 %collective-permute-start.40 = (f32[3,16,256]{2,1,0:T(8,128)S(1)}, f32[3,16,256]{2,1,0:T(8,128)S(1)}, u32[]{:S(2)}, u32[]{:S(2)}) collective-permute-start(f32[3,16,256]{2,1,0:T(8,128)S(1)} %composite.5.refs_17_), channel_id=1, source_target_pairs={{0,16},{4,20},{8,24},{12,28},{16,0},{20,4},{24,8},{28,12},{1,17},{... | collective-permute-start | bytes 147464 | tf_op jit(solution)/shard_map/ppermute | solution.py:241
  88.6 3.3 %collective-permute-start.42 = (f32[3,16,256]{2,1,0:T(8,128)S(1)}, f32[3,16,256]{2,1,0:T(8,128)S(1)}, u32[]{:S(2)}, u32[]{:S(2)}) collective-permute-start(f32[3,16,256]{2,1,0:T(8,128)S(1)} %composite.5.refs_17_), channel_id=1, source_target_pairs={{0,24},{4,28},{8,0},{12,4},{16,8},{20,12},{24,16},{28,20},{1,25},{... | collective-permute-start | bytes 147464 | tf_op jit(solution)/shard_map/ppermute | solution.py:241
  96.8 1.9 %place.1 = f32[3,64,2048]{2,1,0:T(8,128)} custom-call(s32[2]{0:T(128)S(1)} %pad_add_fusion.refs_0_, f32[3,24,256]{2,1,0:T(8,128)S(1)} %composite.3.refs_10_.refs_1_, f32[3,24,256]{2,1,0:T(8,128)S(1)} %collective-permute-done.9.refs_2_, f32[3,24,256]{2,1,0:T(8,128)S(1)} %collective-permute-done.10.refs_3_, f32[3,24,256]{2,1,0:T(8,128)S(1)} %collective-permute-done.11.refs_4_, ...), custom_call_target="tpu_custom_call" | custom-call | bytes 7380000 | tf_op jit(solution)/shard_map/place/pallas_call | solution.py:24
  (91 shorter events, 14.2 us)
Async XLA Ops:
  9.2 17.3 %collective-permute-start.3 = (f32[1,4,24,256]{3,2,1,0:T(8,128)S(1)}, f32[1,4,24,256]{3,2,1,0:T(8,128)S(1)}, u32[]{:S(2)}, u32[]{:S(2)}) collective-permute-start(f32[1,4,24,256]{3,2,1,0:T(8,128)S(1)} %slice.36), channel_id=1, source_target_pairs={{0,4},{4,0},{8,12},{12,8},{16,20},{20,16},{24,28},{28,24},{1,5},{5... | collective-permute-start | bytes 294920 | tf_op jit(solution)/shard_map/ppermute | solution.py:238
  19.0 11.5 %collective-permute-start.7 = (f32[16,1,2048]{2,1,0:T(1,128)S(1)}, f32[16,1,2048]{2,1,0:T(1,128)S(1)}, u32[]{:S(2)}, u32[]{:S(2)}) collective-permute-start(f32[16,1,2048]{2,1,0:T(1,128)S(1)} %get-tuple-element.24), channel_id=1, source_target_pairs={{0,1},{1,2},{2,3},{4,5},{5,6},{6,7},{8,9},{9,10},{10,11},{12,13},{... | collective-permute-start | bytes 393224 | tf_op jit(solution)/shard_map/ppermute | solution.py:275
  23.5 11.4 %collective-permute-start = (f32[2,4,24,256]{3,2,1,0:T(8,128)S(1)}, f32[2,4,24,256]{3,2,1,0:T(8,128)S(1)}, u32[]{:S(2)}, u32[]{:S(2)}) collective-permute-start(f32[2,4,24,256]{3,2,1,0:T(8,128)S(1)} %get-tuple-element.20), channel_id=1, source_target_pairs={{0,8},{4,12},{8,16},{12,20},{16,24},{20,28},{24,0},{28,4},{1,9},{5... | collective-permute-start | bytes 589832 | tf_op jit(solution)/shard_map/ppermute | solution.py:241
  25.1 7.2 %collective-permute-start.8 = (f32[16,1,2048]{2,1,0:T(1,128)S(1)}, f32[16,1,2048]{2,1,0:T(1,128)S(1)}, u32[]{:S(2)}, u32[]{:S(2)}) collective-permute-start(f32[16,1,2048]{2,1,0:T(1,128)S(1)} %get-tuple-element.25), channel_id=1, source_target_pairs={{1,0},{2,1},{3,2},{5,4},{6,5},{7,6},{9,8},{10,9},{11,10},{13,12},{... | collective-permute-start | bytes 393224 | tf_op jit(solution)/shard_map/ppermute | solution.py:275
  26.5 15.7 %collective-permute-start.1 = (f32[2,4,24,256]{3,2,1,0:T(8,128)S(1)}, f32[2,4,24,256]{3,2,1,0:T(8,128)S(1)}, u32[]{:S(2)}, u32[]{:S(2)}) collective-permute-start(f32[2,4,24,256]{3,2,1,0:T(8,128)S(1)} %get-tuple-element.21), channel_id=1, source_target_pairs={{0,16},{4,20},{8,24},{12,28},{16,0},{20,4},{24,8},{28,12},{1,17},{... | collective-permute-start | bytes 589832 | tf_op jit(solution)/shard_map/ppermute | solution.py:241
  29.1 23.6 %collective-permute-start.2 = (f32[2,4,24,256]{3,2,1,0:T(8,128)S(1)}, f32[2,4,24,256]{3,2,1,0:T(8,128)S(1)}, u32[]{:S(2)}, u32[]{:S(2)}) collective-permute-start(f32[2,4,24,256]{3,2,1,0:T(8,128)S(1)} %get-tuple-element.22), channel_id=1, source_target_pairs={{0,24},{4,28},{8,0},{12,4},{16,8},{20,12},{24,16},{28,20},{1,25},{... | collective-permute-start | bytes 589832 | tf_op jit(solution)/shard_map/ppermute | solution.py:241
  30.5 22.4 %collective-permute-start.16 = (f32[2,4,24,256]{3,2,1,0:T(8,128)S(1)}, f32[2,4,24,256]{3,2,1,0:T(8,128)S(1)}, u32[]{:S(2)}, u32[]{:S(2)}) collective-permute-start(f32[2,4,24,256]{3,2,1,0:T(8,128)S(1)} %get-tuple-element.27), channel_id=1, source_target_pairs={{0,8},{4,12},{8,16},{12,20},{16,24},{20,28},{24,0},{28,4},{1,9},{5... | collective-permute-start | bytes 589832 | tf_op jit(solution)/shard_map/ppermute | solution.py:241
  32.3 28.3 %collective-permute-start.17 = (f32[2,4,24,256]{3,2,1,0:T(8,128)S(1)}, f32[2,4,24,256]{3,2,1,0:T(8,128)S(1)}, u32[]{:S(2)}, u32[]{:S(2)}) collective-permute-start(f32[2,4,24,256]{3,2,1,0:T(8,128)S(1)} %get-tuple-element.28), channel_id=1, source_target_pairs={{0,16},{4,20},{8,24},{12,28},{16,0},{20,4},{24,8},{28,12},{1,17},{... | collective-permute-start | bytes 589832 | tf_op jit(solution)/shard_map/ppermute | solution.py:241
  34.9 25.7 %collective-permute-start.18 = (f32[2,4,24,256]{3,2,1,0:T(8,128)S(1)}, f32[2,4,24,256]{3,2,1,0:T(8,128)S(1)}, u32[]{:S(2)}, u32[]{:S(2)}) collective-permute-start(f32[2,4,24,256]{3,2,1,0:T(8,128)S(1)} %get-tuple-element.29), channel_id=1, source_target_pairs={{0,24},{4,28},{8,0},{12,4},{16,8},{20,12},{24,16},{28,20},{1,25},{... | collective-permute-start | bytes 589832 | tf_op jit(solution)/shard_map/ppermute | solution.py:241
  42.2 18.9 %collective-permute-start.30 = (f32[2,4,16,256]{3,2,1,0:T(8,128)S(1)}, f32[2,4,16,256]{3,2,1,0:T(8,128)S(1)}, u32[]{:S(2)}, u32[]{:S(2)}) collective-permute-start(f32[2,4,16,256]{3,2,1,0:T(8,128)S(1)} %get-tuple-element.30), channel_id=1, source_target_pairs={{0,8},{4,12},{8,16},{12,20},{16,24},{20,28},{24,0},{28,4},{1,9},{5... | collective-permute-start | bytes 393224 | tf_op jit(solution)/shard_map/ppermute | solution.py:241
  52.8 12.7 %collective-permute-start.4 = (f32[1,4,24,256]{3,2,1,0:T(8,128)S(1)}, f32[1,4,24,256]{3,2,1,0:T(8,128)S(1)}, u32[]{:S(2)}, u32[]{:S(2)}) collective-permute-start(f32[1,4,24,256]{3,2,1,0:T(8,128)S(1)} %slice.48), channel_id=1, source_target_pairs={{0,4},{4,0},{8,12},{12,8},{16,20},{20,16},{24,28},{28,24},{1,5},{5... | collective-permute-start | bytes 294920 | tf_op jit(solution)/shard_map/ppermute | solution.py:238
  52.9 14.9 %collective-permute-start.5 = (f32[1,4,24,256]{3,2,1,0:T(8,128)S(1)}, f32[1,4,24,256]{3,2,1,0:T(8,128)S(1)}, u32[]{:S(2)}, u32[]{:S(2)}) collective-permute-start(f32[1,4,24,256]{3,2,1,0:T(8,128)S(1)} %slice.49), channel_id=1, source_target_pairs={{0,4},{4,0},{8,12},{12,8},{16,20},{20,16},{24,28},{28,24},{1,5},{5... | collective-permute-start | bytes 294920 | tf_op jit(solution)/shard_map/ppermute | solution.py:238
  60.6 7.3 %collective-permute-start.6 = (f32[1,4,24,256]{3,2,1,0:T(8,128)S(1)}, f32[1,4,24,256]{3,2,1,0:T(8,128)S(1)}, u32[]{:S(2)}, u32[]{:S(2)}) collective-permute-start(f32[1,4,24,256]{3,2,1,0:T(8,128)S(1)} %slice.50), channel_id=1, source_target_pairs={{0,4},{4,0},{8,12},{12,8},{16,20},{20,16},{24,28},{28,24},{1,5},{5... | collective-permute-start | bytes 294920 | tf_op jit(solution)/shard_map/ppermute | solution.py:238
  60.6 7.8 %collective-permute-start.20 = (f32[1,4,24,256]{3,2,1,0:T(8,128)S(1)}, f32[1,4,24,256]{3,2,1,0:T(8,128)S(1)}, u32[]{:S(2)}, u32[]{:S(2)}) collective-permute-start(f32[1,4,24,256]{3,2,1,0:T(8,128)S(1)} %slice.51), channel_id=1, source_target_pairs={{0,4},{4,0},{8,12},{12,8},{16,20},{20,16},{24,28},{28,24},{1,5},{5... | collective-permute-start | bytes 294920 | tf_op jit(solution)/shard_map/ppermute | solution.py:238
  61.2 10.9 %collective-permute-start.31 = (f32[2,4,16,256]{3,2,1,0:T(8,128)S(1)}, f32[2,4,16,256]{3,2,1,0:T(8,128)S(1)}, u32[]{:S(2)}, u32[]{:S(2)}) collective-permute-start(f32[2,4,16,256]{3,2,1,0:T(8,128)S(1)} %get-tuple-element.31), channel_id=1, source_target_pairs={{0,16},{4,20},{8,24},{12,28},{16,0},{20,4},{24,8},{28,12},{1,17},{... | collective-permute-start | bytes 393224 | tf_op jit(solution)/shard_map/ppermute | solution.py:241
  65.5 6.6 %collective-permute-start.32 = (f32[2,4,16,256]{3,2,1,0:T(8,128)S(1)}, f32[2,4,16,256]{3,2,1,0:T(8,128)S(1)}, u32[]{:S(2)}, u32[]{:S(2)}) collective-permute-start(f32[2,4,16,256]{3,2,1,0:T(8,128)S(1)} %get-tuple-element.32), channel_id=1, source_target_pairs={{0,24},{4,28},{8,0},{12,4},{16,8},{20,12},{24,16},{28,20},{1,25},{... | collective-permute-start | bytes 393224 | tf_op jit(solution)/shard_map/ppermute | solution.py:241
  71.4 7.8 %collective-permute-start.24 = (f32[3,24,256]{2,1,0:T(8,128)S(1)}, f32[3,24,256]{2,1,0:T(8,128)S(1)}, u32[]{:S(2)}, u32[]{:S(2)}) collective-permute-start(f32[3,24,256]{2,1,0:T(8,128)S(1)} %composite.4.refs_10_.refs_9_), channel_id=1, source_target_pairs={{0,8},{4,12},{8,16},{12,20},{16,24},{20,28},{24,0},{28,4},{1,9},{5... | collective-permute-start | bytes 221192 | tf_op jit(solution)/shard_map/ppermute | solution.py:241
  72.7 8.0 %collective-permute-start.26 = (f32[3,24,256]{2,1,0:T(8,128)S(1)}, f32[3,24,256]{2,1,0:T(8,128)S(1)}, u32[]{:S(2)}, u32[]{:S(2)}) collective-permute-start(f32[3,24,256]{2,1,0:T(8,128)S(1)} %composite.4.refs_10_.refs_9_), channel_id=1, source_target_pairs={{0,16},{4,20},{8,24},{12,28},{16,0},{20,4},{24,8},{28,12},{1,17},{... | collective-permute-start | bytes 221192 | tf_op jit(solution)/shard_map/ppermute | solution.py:241
  75.1 10.5 %collective-permute-start.28 = (f32[3,24,256]{2,1,0:T(8,128)S(1)}, f32[3,24,256]{2,1,0:T(8,128)S(1)}, u32[]{:S(2)}, u32[]{:S(2)}) collective-permute-start(f32[3,24,256]{2,1,0:T(8,128)S(1)} %composite.4.refs_10_.refs_9_), channel_id=1, source_target_pairs={{0,24},{4,28},{8,0},{12,4},{16,8},{20,12},{24,16},{28,20},{1,25},{... | collective-permute-start | bytes 221192 | tf_op jit(solution)/shard_map/ppermute | solution.py:241
  78.5 8.0 %collective-permute-start.23 = (f32[3,24,256]{2,1,0:T(8,128)S(1)}, f32[3,24,256]{2,1,0:T(8,128)S(1)}, u32[]{:S(2)}, u32[]{:S(2)}) collective-permute-start(f32[3,24,256]{2,1,0:T(8,128)S(1)} %composite.4.refs_10_.refs_9_), channel_id=1, source_target_pairs={{0,4},{4,0},{8,12},{12,8},{16,20},{20,16},{24,28},{28,24},{1,5},{5... | collective-permute-start | bytes 221192 | tf_op jit(solution)/shard_map/ppermute | solution.py:238
  78.5 8.1 %collective-permute-start.10 = (f32[3,24,256]{2,1,0:T(8,128)S(1)}, f32[3,24,256]{2,1,0:T(8,128)S(1)}, u32[]{:S(2)}, u32[]{:S(2)}) collective-permute-start(f32[3,24,256]{2,1,0:T(8,128)S(1)} %composite.3.refs_10_.refs_1_), channel_id=1, source_target_pairs={{0,8},{4,12},{8,16},{12,20},{16,24},{20,28},{24,0},{28,4},{1,9},{5... | collective-permute-start | bytes 221192 | tf_op jit(solution)/shard_map/ppermute | solution.py:241
  79.2 9.5 %collective-permute-start.12 = (f32[3,24,256]{2,1,0:T(8,128)S(1)}, f32[3,24,256]{2,1,0:T(8,128)S(1)}, u32[]{:S(2)}, u32[]{:S(2)}) collective-permute-start(f32[3,24,256]{2,1,0:T(8,128)S(1)} %composite.3.refs_10_.refs_1_), channel_id=1, source_target_pairs={{0,16},{4,20},{8,24},{12,28},{16,0},{20,4},{24,8},{28,12},{1,17},{... | collective-permute-start | bytes 221192 | tf_op jit(solution)/shard_map/ppermute | solution.py:241
  80.6 11.3 %collective-permute-start.14 = (f32[3,24,256]{2,1,0:T(8,128)S(1)}, f32[3,24,256]{2,1,0:T(8,128)S(1)}, u32[]{:S(2)}, u32[]{:S(2)}) collective-permute-start(f32[3,24,256]{2,1,0:T(8,128)S(1)} %composite.3.refs_10_.refs_1_), channel_id=1, source_target_pairs={{0,24},{4,28},{8,0},{12,4},{16,8},{20,12},{24,16},{28,20},{1,25},{... | collective-permute-start | bytes 221192 | tf_op jit(solution)/shard_map/ppermute | solution.py:241
  86.6 7.2 %collective-permute-start.40 = (f32[3,16,256]{2,1,0:T(8,128)S(1)}, f32[3,16,256]{2,1,0:T(8,128)S(1)}, u32[]{:S(2)}, u32[]{:S(2)}) collective-permute-start(f32[3,16,256]{2,1,0:T(8,128)S(1)} %composite.5.refs_17_), channel_id=1, source_target_pairs={{0,16},{4,20},{8,24},{12,28},{16,0},{20,4},{24,8},{28,12},{1,17},{... | collective-permute-start | bytes 147464 | tf_op jit(solution)/shard_map/ppermute | solution.py:241
  (23 other events, 117.3 us)

commit v3 on v2

--- a/solution.py
+++ b/solution.py
@@ -13,7 +13,8 @@
 SUB = 8
 LANE = 128
 CORES = 2
-INNER = ((1, 3), (4, 3))
+CHUNKS = (((1, 5),), ((0, 1), (6, 1), (7, 1)))
+LOG2E = 1.4426950408889634
 VMEM_LIMIT = 24 * 2**20
 
 
@@ -85,9 +86,9 @@
     lane = lax.broadcasted_iota(jnp.int32, (SUB, LANE), 1)
     top, bottom = sub == 0, sub == SUB - 1
     leftmost, rightmost = lane == 0, lane == LANE - 1
-    vregs = part // LANE
-
-    def march(slot, out_row, before_ref, behind_ref, column, relative, out_ref):
+    vregs = CORES * part // LANE
+
+    def march(slot, out_row, before_ref, behind_ref, column, out_ref):
         def load(plane, shift, vreg):
             ref = {-1: before_ref, 1: behind_ref}.get(shift)
             if ref is not None:
@@ -117,8 +118,8 @@
                 shade = jnp.tanh(
                     light[0] * (after[v + 1] - before[v + 1]) + light[1] * (down - up) + light[2] * (right - left)
                 )
-                depth[v] = depth[v] + jnp.log(1.0 + jnp.exp(value + value))
-                through = jnp.exp(depth[v] * -scale)
+                depth[v] = depth[v] + jnp.log2(1.0 + jnp.exp2(value * (2.0 * LOG2E)))
+                through = jnp.exp2(depth[v] * -scale)
                 lost = left_over[v] - through
                 left_over[v] = through
                 weight = lost + lost * shade
@@ -127,7 +128,8 @@
                     sums[c][v] = sums[c][v] + weight * jnp.tanh(slope[c] * value + offset[c])
             before, here = here, after
         for v in range(vregs):
-            lanes = pl.ds(v * LANE, LANE)
+            relative = lax.rem(my_core + v * LANE // part, CORES)
+            lanes = pl.ds(v * LANE % part, LANE)
             for c in range(3):
                 out_ref[relative, c, pl.ds(out_row, SUB), lanes] = 0.25 * (total[v] + sums[c][v])
             out_ref[relative, 3, pl.ds(out_row, SUB), lanes] = depth[v] * scale
@@ -149,60 +151,57 @@
                     def _():
                         tile_copy(first + index + 1, here + 1).wait()
 
-                def one(relative, carry):
-                    owner = chip * CORES + lax.rem(my_core + relative, CORES)
-                    out_row = pl.multiple_of((written + index) * SUB, SUB)
-                    march(here, out_row, before, behind, owner * part, relative, out_ref)
-                    return carry
-
-                return lax.fori_loop(0, CORES, one, carry)
+                out_row = pl.multiple_of((written + index) * SUB, SUB)
+                march(here, out_row, before, behind, pl.multiple_of(chip * CORES * part, LANE), out_ref)
+                return carry
 
             lax.fori_loop(0, number, one_tile, 0)
 
 
-def composite_kernel(chips, where_ref, rank_ref, *refs):
-    own, other, out_ref = refs[:chips], refs[chips : 2 * chips], refs[2 * chips]
+def composite_kernel(chips, count, where_ref, rank_ref, *refs):
+    inputs, out_ref = refs[:-1], refs[-1]
     my_chip, my_core = where_ref[0], where_ref[1]
-    blocks, ranks = [], []
+    ranks = []
     for k in range(chips):
         chip = lax.rem(my_chip + chips - k, chips)
-        for core, ref in ((my_core, own[k]), (CORES - 1 - my_core, other[k])):
-            blocks.append(ref)
-            ranks.append(rank_ref[chip * CORES + core])
-    count = len(blocks)
-    ahead = [[(ranks[j] < ranks[i]).astype(jnp.float32) for j in range(count)] for i in range(count)]
+        ranks += [rank_ref[chip * CORES + core] for core in (my_core, CORES - 1 - my_core)]
+    bricks = len(ranks)
+    ahead = [[(ranks[j] < ranks[i]).astype(jnp.float32) for j in range(bricks)] for i in range(bricks)]
     columns = out_ref.shape[2] // LANE
-
-    def one(index, carry):
-        row = index // columns
-        at = (
-            pl.ds(pl.multiple_of(row * SUB, SUB), SUB),
-            pl.ds(pl.multiple_of((index - row * columns) * LANE, LANE), LANE),
-        )
-        depths = [ref[(0, 3, *at)] for ref in blocks]
-        sums = [background * jnp.exp(-functools.reduce(jnp.add, depths))] * 3
-        for i in range(count):
-            front = functools.reduce(jnp.add, [ahead[i][j] * depths[j] for j in range(count) if j != i])
-            weight = jnp.exp(-front)
+    written = 0
+    for n in range(count):
+        own, other = inputs[2 * n * chips : (2 * n + 1) * chips], inputs[(2 * n + 1) * chips : (2 * n + 2) * chips]
+        blocks = [ref for pair in zip(own, other) for ref in pair]
+        rows = own[0].shape[2]
+
+        def one(index, carry, blocks=blocks, written=written):
+            tile = index // columns
+            row = pl.multiple_of(tile * SUB, SUB)
+            lanes = pl.ds(pl.multiple_of((index - tile * columns) * LANE, LANE), LANE)
+            at = (pl.ds(row, SUB), lanes)
+            depths = [ref[(0, 3, *at)] for ref in blocks]
+            sums = [background * jnp.exp2(-functools.reduce(jnp.add, depths))] * 3
+            for i in range(bricks):
+                front = functools.reduce(jnp.add, [ahead[i][j] * depths[j] for j in range(bricks) if j != i])
+                weight = jnp.exp2(-front)
+                for c in range(3):
+                    sums[c] = sums[c] + weight * blocks[i][(0, c, *at)]
             for c in range(3):
-                sums[c] = sums[c] + weight * blocks[i][(0, c, *at)]
-        for c in range(3):
-            out_ref[(c, *at)] = sums[c]
-        return carry
-
-    lax.fori_loop(0, out_ref.shape[1] // SUB * columns, one, 0)
-
-
-def place_kernel(chips, chunks, where_ref, *refs):
-    count = len(chunks) * chips * CORES
-    blocks, out_ref, sem = refs[:count], refs[count], refs[count + 1]
+                out_ref[c, pl.ds(pl.multiple_of(row + written, SUB), SUB), lanes] = sums[c]
+            return carry
+
+        lax.fori_loop(0, rows // SUB * columns, one, 0)
+        written += rows
+
+
+def place_kernel(groups, where_ref, *refs):
+    blocks, out_ref, sem = list(refs[:-2]), refs[-2], refs[-1]
     my_chip, my_core = where_ref[0], where_ref[1]
     copies = []
-    for i, runs in enumerate(chunks):
-        for k in range(chips):
-            chip = lax.rem(my_chip + chips - k, chips)
-            for j, core in enumerate((my_core, CORES - 1 - my_core)):
-                block = blocks[(i * chips + k) * CORES + j]
+    for runs, chip_of in groups:
+        for chip in chip_of(my_chip):
+            for core in (my_core, CORES - 1 - my_core):
+                block = blocks.pop(0)
                 part = block.shape[2]
                 column = pl.multiple_of((chip * CORES + core) * part, LANE)
                 written = 0
@@ -226,8 +225,7 @@
     scale = optical_total / (planes * wide)
     index = lax.axis_index("wide")
     where = jnp.stack([index // CORES, index % CORES]).astype(jnp.int32)
-    inner = [(run,) for run in INNER] if tiles == 8 else [((1, tiles - 2),)]
-    chunks = inner + [((0, 1), (tiles - 1, 1))]
+    chunks = CHUNKS if tiles == 8 else (((1, tiles - 2),), ((0, 1), (tiles - 1, 1)))
 
     smem = pl.BlockSpec(memory_space=pltpu.SMEM)
     vmem = pl.BlockSpec(memory_space=pltpu.VMEM)
@@ -274,11 +272,14 @@
         up = [(i, i + 1) for i in range(narrow - 1)]
         return lax.ppermute(last_row, "narrow", up), lax.ppermute(first_row, "narrow", [(j, i) for i, j in up])
 
-    def composite(runs, own, other, events):
+    def composite(parts_of, runs, events):
+        operands = []
+        for own in parts_of:
+            operands += own + [swap(value[1:]) for value in own]
         return call(
-            functools.partial(composite_kernel, chips),
-            [where, depth_rank, *own, *other],
-            [smem] * 2 + [vmem] * (2 * chips),
+            functools.partial(composite_kernel, chips, len(parts_of)),
+            [where, depth_rank, *operands],
+            [smem] * 2 + [vmem] * len(operands),
             events,
             out_shape=pltpu.VMEM((3, tiles_of(runs) * SUB, part), jnp.float32),
             out_specs=vmem,
@@ -286,7 +287,22 @@
             name="composite",
         )
 
-    sent, last, edges = [], (), ()
+    def gather_by_halves(tile):
+        tiles_by = {0: tile}
+        bit = chips // 2
+        while bit:
+            for m in list(tiles_by):
+                pairs = [(i, i ^ (bit * CORES)) for i in range(wide)]
+                tiles_by[m ^ bit] = lax.ppermute(tiles_by[m], "wide", pairs)
+            bit //= 2
+        order = sorted(tiles_by)
+        return [tiles_by[m] for m in order], lambda chip: [jnp.bitwise_xor(chip, m) for m in order]
+
+    def gather_directly(tile):
+        values = [tile] + [send(tile, k) for k in range(1, chips)]
+        return values, lambda chip: [lax.rem(chip + chips - k, chips) for k in range(chips)]
+
+    sent, last, edges = [], [], ()
     for i, runs in enumerate(chunks):
         if i == len(chunks) - 1:
             edges = edge_rows(last)
@@ -294,22 +310,23 @@
         last = [blocks[0]]
         sent.append([blocks[0]] + [send(blocks[k], k) for k in range(1, chips)])
 
-    finished = []
-    for runs, own in zip(chunks, sent):
-        other = [swap(value[1:]) for value in own]
-        tile = composite(runs, own, other, last)
+    groups, finished = [], []
+    for first, end, gather in ((0, len(chunks) - 1, gather_by_halves), (len(chunks) - 1, len(chunks), gather_directly)):
+        runs = sum(chunks[first:end], ())
+        tile = composite(sent[first:end], runs, last)
         last = [tile]
-        for k in range(chips):
-            value = send(tile, k) if k else tile
+        values, chip_of = gather(tile)
+        groups.append((runs, chip_of))
+        for value in values:
             finished += [value, swap(value)]
 
     return call(
-        functools.partial(place_kernel, chips, chunks),
+        functools.partial(place_kernel, groups),
         [where, *finished],
         [smem] + [vmem] * len(finished),
         out_shape=jax.ShapeDtypeStruct((3, rows, columns), jnp.float32),
         out_specs=hbm,
-        scratch_shapes=[pltpu.SemaphoreType.DMA((wide * sum(len(runs) for runs in chunks),))],
+        scratch_shapes=[pltpu.SemaphoreType.DMA((wide * sum(len(runs) for runs, _ in groups),))],
         cost_estimate=lasting(2.0),
         name="place",
     )

time: 98.9 us -> 86.9 us (0.88)
  starting transfers between devices: 56.8 us -> 30.6 us
  waiting for transfers between devices: 12.2 us -> 31.1 us
  Pallas kernels: 28 us -> 23.4 us
    ppermute x18 -> x9, starting transfers between devices: 45.7 us -> 15.4 us  [send(): lax.ppermute(value, 'wide', [(i, (i + k * CORES) % wide) for i in range(w...]
    ppermute x18 -> x9, waiting for transfers between devices: 9.13 us -> 25.6 us  [send(): lax.ppermute(value, 'wide', [(i, (i + k * CORES) % wide) for i in range(w...]
    ppermute x0 -> x3, starting transfers between devices: none -> 7.8 us  [gather_by_halves(): tiles_by[m ^ bit] = lax.ppermute(tiles_by[m], 'wide', pairs)]
    pallas_call x8 -> x6, Pallas kernels: 28 us -> 23.4 us  [call(): pl.pallas_call(with_events, in_specs=specs + [pl.BlockSpec(memory_space=p...]
    ppermute x1, waiting for transfers between devices: 1.13 us -> 4.16 us  [edge_rows(): lax.ppermute(first_row, 'narrow', [(j, i) for i, j in up])]
    ppermute x24 -> x16, starting transfers between devices: 5.38 us -> 2.69 us  [swap(): return lax.ppermute(value, 'wide', [(i, i ^ 1) for i in range(wide)])]
    ppermute x1, starting transfers between devices: 4.42 us -> 3.4 us  [edge_rows(): lax.ppermute(last_row, 'narrow', up)]
  transfers between devices with their start and end apart: 44 -> 30, of which waited for: 10 -> 10; matrix products, arithmetic and copies ran while one was open for 0% -> 0% of each run, Pallas kernels for 19% -> 13%
where the time goes in v3:
time: 86.9 us; the launch traced here: 86.7 us
  waiting for transfers between devices  31.1 us (36%)
  starting transfers between devices  30.6 us (35%)
  Pallas kernels  23.4 us (27%)
  local copies, waits for them, and re-layouts  1.42 us (2%)
    ppermute x9, waiting for transfers between devices, send(): lax.ppermute(value, 'wide', [(i, (i + k * CORES) % wide) for i in range(w...  25.6 us
    pallas_call x6, Pallas kernels, call(): pl.pallas_call(with_events, in_specs=specs + [pl.BlockSpec(memory_space=p...  23.4 us
    ppermute x9, starting transfers between devices, send(): lax.ppermute(value, 'wide', [(i, (i + k * CORES) % wide) for i in range(w...  15.4 us
    ppermute x3, starting transfers between devices, gather_by_halves(): tiles_by[m ^ bit] = lax.ppermute(tiles_by[m], 'wide', pairs)  7.8 us
    ppermute x1, waiting for transfers between devices, edge_rows(): lax.ppermute(first_row, 'narrow', [(j, i) for i, j in up])  4.16 us
    ppermute x1, starting transfers between devices, edge_rows(): lax.ppermute(last_row, 'narrow', up)  3.4 us
    ppermute x16, starting transfers between devices, swap(): return lax.ppermute(value, 'wide', [(i, i ^ 1) for i in range(wide)])  2.69 us
  transfers between devices with their start and end apart: 30, of which 10 were waited for; matrix products, arithmetic and copies ran while one was open for 0% of the time, Pallas kernels for 13%

profile of v3, /device:TPU:0, one launch (start us, length us, event | category | flops | bytes accessed | tf_op | source)
XLA Modules:
  0.0 86.7 jit_solution(5656025074305198013)
XLA Ops:
  1.4 10.2 %render.2 = (f32[2,4,40,256]{3,2,1,0:T(8,128)S(1)}, f32[2,4,40,256]{3,2,1,0:T(8,128)S(1)}, f32[2,4,40,256]{3,2,1,0:T(8,128)S(1)}, f32[2,4,40,256]{3,2,1,0:T(8,128)S(1)}) custom-call(s32[2]{0:T(128)S(1)} %pad_add_fusion.refs_0_, f32[2,3]{1,0:T(2,128)S(1)} %copy-done, f32[3]{0:T(128)S(1)} %copy-done.1, f32[16,64,2048]{2,1,0:T(8,128)} %refs_3_.3), custom_call_target="tpu_custom_call" | custom-call | bytes 46125000 | tf_op jit(solution)/shard_map/render/pallas_call | solution.py:25
  11.6 3.1 %collective-permute-start = (f32[2,4,40,256]{3,2,1,0:T(8,128)S(1)}, f32[2,4,40,256]{3,2,1,0:T(8,128)S(1)}, u32[]{:S(2)}, u32[]{:S(2)}) collective-permute-start(f32[2,4,40,256]{3,2,1,0:T(8,128)S(1)} %get-tuple-element.16), channel_id=1, source_target_pairs={{0,8},{4,12},{8,16},{12,20},{16,24},{20,28},{24,0},{28,4},{1,9},{5... | collective-permute-start | bytes 983048 | tf_op jit(solution)/shard_map/ppermute | solution.py:239
  14.7 1.6 %edges.1 = (f32[16,1,2048]{2,1,0:T(1,128)S(1)}, f32[16,1,2048]{2,1,0:T(1,128)S(1)}) custom-call(f32[16,64,2048]{2,1,0:T(8,128)} %refs_3_.3, f32[2,4,40,256]{3,2,1,0:T(8,128)S(1)} %get-tuple-element.15.refs_1_.refs_6_.refs_2_), custom_call_target="tpu_custom_call" | custom-call | bytes 4428000 | tf_op jit(solution)/shard_map/edges/pallas_call | solution.py:25
  16.3 3.4 %collective-permute-start.7 = (f32[16,1,2048]{2,1,0:T(1,128)S(1)}, f32[16,1,2048]{2,1,0:T(1,128)S(1)}, u32[]{:S(2)}, u32[]{:S(2)}) collective-permute-start(f32[16,1,2048]{2,1,0:T(1,128)S(1)} %get-tuple-element.19), channel_id=1, source_target_pairs={{0,1},{1,2},{2,3},{4,5},{5,6},{6,7},{8,9},{9,10},{10,11},{12,13},{... | collective-permute-start | bytes 393224 | tf_op jit(solution)/shard_map/ppermute | solution.py:273
  19.7 2.7 %collective-permute-start.1 = (f32[2,4,40,256]{3,2,1,0:T(8,128)S(1)}, f32[2,4,40,256]{3,2,1,0:T(8,128)S(1)}, u32[]{:S(2)}, u32[]{:S(2)}) collective-permute-start(f32[2,4,40,256]{3,2,1,0:T(8,128)S(1)} %get-tuple-element.17), channel_id=1, source_target_pairs={{0,16},{4,20},{8,24},{12,28},{16,0},{20,4},{24,8},{28,12},{1,17},{... | collective-permute-start | bytes 983048 | tf_op jit(solution)/shard_map/ppermute | solution.py:239
  22.4 1.3 %collective-permute-start.8 = (f32[16,1,2048]{2,1,0:T(1,128)S(1)}, f32[16,1,2048]{2,1,0:T(1,128)S(1)}, u32[]{:S(2)}, u32[]{:S(2)}) collective-permute-start(f32[16,1,2048]{2,1,0:T(1,128)S(1)} %get-tuple-element.20), channel_id=1, source_target_pairs={{1,0},{2,1},{3,2},{5,4},{6,5},{7,6},{9,8},{10,9},{11,10},{13,12},{... | collective-permute-start | bytes 393224 | tf_op jit(solution)/shard_map/ppermute | solution.py:273
  23.7 1.4 %collective-permute-start.2 = (f32[2,4,40,256]{3,2,1,0:T(8,128)S(1)}, f32[2,4,40,256]{3,2,1,0:T(8,128)S(1)}, u32[]{:S(2)}, u32[]{:S(2)}) collective-permute-start(f32[2,4,40,256]{3,2,1,0:T(8,128)S(1)} %get-tuple-element.18), channel_id=1, source_target_pairs={{0,24},{4,28},{8,0},{12,4},{16,8},{20,12},{24,16},{28,20},{1,25},{... | collective-permute-start | bytes 983048 | tf_op jit(solution)/shard_map/ppermute | solution.py:239
  25.1 4.2 %collective-permute-done.8.refs_5_ = f32[16,1,2048]{2,1,0:T(1,128)S(1)} collective-permute-done((f32[16,1,2048]{2,1,0:T(1,128)S(1)}, f32[16,1,2048]{2,1,0:T(1,128)S(1)}, u32[]{:S(2)}, u32[]{:S(2)}) %collective-permute-start.8) | collective-permute-done | bytes 131104 | tf_op jit(solution)/shard_map/ppermute | solution.py:273
  29.2 7.3 %render.3 = (f32[2,4,24,256]{3,2,1,0:T(8,128)S(1)}, f32[2,4,24,256]{3,2,1,0:T(8,128)S(1)}, f32[2,4,24,256]{3,2,1,0:T(8,128)S(1)}, f32[2,4,24,256]{3,2,1,0:T(8,128)S(1)}) custom-call(s32[2]{0:T(128)S(1)} %pad_add_fusion.refs_0_, f32[2,3]{1,0:T(2,128)S(1)} %copy-done, f32[3]{0:T(128)S(1)} %copy-done.2, f32[16,64,2048]{2,1,0:T(8,128)} %refs_3_.3, ...), custom_call_target="tpu_custom_call" | custom-call | bytes 27675000 | tf_op jit(solution)/shard_map/render/pallas_call | solution.py:25
  36.8 1.7 %collective-permute-start.17 = (f32[2,4,24,256]{3,2,1,0:T(8,128)S(1)}, f32[2,4,24,256]{3,2,1,0:T(8,128)S(1)}, u32[]{:S(2)}, u32[]{:S(2)}) collective-permute-start(f32[2,4,24,256]{3,2,1,0:T(8,128)S(1)} %get-tuple-element.23), channel_id=1, source_target_pairs={{0,16},{4,20},{8,24},{12,28},{16,0},{20,4},{24,8},{28,12},{1,17},{... | collective-permute-start | bytes 589832 | tf_op jit(solution)/shard_map/ppermute | solution.py:239
  38.5 1.9 %collective-permute-start.18 = (f32[2,4,24,256]{3,2,1,0:T(8,128)S(1)}, f32[2,4,24,256]{3,2,1,0:T(8,128)S(1)}, u32[]{:S(2)}, u32[]{:S(2)}) collective-permute-start(f32[2,4,24,256]{3,2,1,0:T(8,128)S(1)} %get-tuple-element.24), channel_id=1, source_target_pairs={{0,24},{4,28},{8,0},{12,4},{16,8},{20,12},{24,16},{28,20},{1,25},{... | collective-permute-start | bytes 589832 | tf_op jit(solution)/shard_map/ppermute | solution.py:239
  40.6 1.0 %collective-permute-done.2.refs_5_ = f32[2,4,40,256]{3,2,1,0:T(8,128)S(1)} collective-permute-done((f32[2,4,40,256]{3,2,1,0:T(8,128)S(1)}, f32[2,4,40,256]{3,2,1,0:T(8,128)S(1)}, u32[]{:S(2)}, u32[]{:S(2)}) %collective-permute-start.2) | collective-permute-done | bytes 327712 | tf_op jit(solution)/shard_map/ppermute | solution.py:239
  41.6 4.6 %collective-permute-done.16.refs_3_ = f32[2,4,24,256]{3,2,1,0:T(8,128)S(1)} collective-permute-done((f32[2,4,24,256]{3,2,1,0:T(8,128)S(1)}, f32[2,4,24,256]{3,2,1,0:T(8,128)S(1)}, u32[]{:S(2)}, u32[]{:S(2)}) %collective-permute-start.16) | collective-permute-done | bytes 196640 | tf_op jit(solution)/shard_map/ppermute | solution.py:239
  46.3 12.0 %collective-permute-done.17.refs_4_ = f32[2,4,24,256]{3,2,1,0:T(8,128)S(1)} collective-permute-done((f32[2,4,24,256]{3,2,1,0:T(8,128)S(1)}, f32[2,4,24,256]{3,2,1,0:T(8,128)S(1)}, u32[]{:S(2)}, u32[]{:S(2)}) %collective-permute-start.17) | collective-permute-done | bytes 196640 | tf_op jit(solution)/shard_map/ppermute | solution.py:239
  59.6 1.3 %composite.2.refs_10_.refs_1_ = f32[3,40,256]{2,1,0:T(8,128)S(1)} custom-call(s32[2]{0:T(128)S(1)} %pad_add_fusion.refs_0_, s32[8]{0:T(128)S(1)} %copy-done.3, f32[2,4,40,256]{3,2,1,0:T(8,128)S(1)} %get-tuple-element.15.refs_1_.refs_6_.refs_2_, f32[2,4,40,256]{3,2,1,0:T(8,128)S(1)} %collective-permute-done.refs_3_, ...), custom_call_target="tpu_custom_call" | custom-call | bytes 3690000 | tf_op jit(solution)/shard_map/composite/pallas_call | solution.py:25
  60.9 3.4 %collective-permute-start.12 = (f32[3,40,256]{2,1,0:T(8,128)S(1)}, f32[3,40,256]{2,1,0:T(8,128)S(1)}, u32[]{:S(2)}, u32[]{:S(2)}) collective-permute-start(f32[3,40,256]{2,1,0:T(8,128)S(1)} %composite.2.refs_10_.refs_1_), channel_id=1, source_target_pairs={{0,16},{4,20},{8,24},{12,28},{16,0},{20,4},{24,8},{28,12},{1,17},{... | collective-permute-start | bytes 368648 | tf_op jit(solution)/shard_map/ppermute | solution.py:296
  64.4 1.0 %composite.3.refs_9_ = f32[3,24,256]{2,1,0:T(8,128)S(1)} custom-call(s32[2]{0:T(128)S(1)} %pad_add_fusion.refs_0_, s32[8]{0:T(128)S(1)} %copy-done.3, f32[2,4,24,256]{3,2,1,0:T(8,128)S(1)} %get-tuple-element.21.refs_10_.refs_2_, f32[2,4,24,256]{3,2,1,0:T(8,128)S(1)} %collective-permute-done.16.refs_3_, ...), custom_call_target="tpu_custom_call" | custom-call | bytes 3690000 | tf_op jit(solution)/shard_map/composite/pallas_call | solution.py:25
  65.5 3.4 %collective-permute-start.28 = (f32[3,24,256]{2,1,0:T(8,128)S(1)}, f32[3,24,256]{2,1,0:T(8,128)S(1)}, u32[]{:S(2)}, u32[]{:S(2)}) collective-permute-start(f32[3,24,256]{2,1,0:T(8,128)S(1)} %composite.3.refs_9_), channel_id=1, source_target_pairs={{0,24},{4,28},{8,0},{12,4},{16,8},{20,12},{24,16},{28,20},{1,25},{... | collective-permute-start | bytes 221192 | tf_op jit(solution)/shard_map/ppermute | solution.py:239
  68.9 1.0 %collective-permute-start.26 = (f32[3,24,256]{2,1,0:T(8,128)S(1)}, f32[3,24,256]{2,1,0:T(8,128)S(1)}, u32[]{:S(2)}, u32[]{:S(2)}) collective-permute-start(f32[3,24,256]{2,1,0:T(8,128)S(1)} %composite.3.refs_9_), channel_id=1, source_target_pairs={{0,16},{4,20},{8,24},{12,28},{16,0},{20,4},{24,8},{28,12},{1,17},{... | collective-permute-start | bytes 221192 | tf_op jit(solution)/shard_map/ppermute | solution.py:239
  69.9 4.4 %collective-permute-start.14 = (f32[3,40,256]{2,1,0:T(8,128)S(1)}, f32[3,40,256]{2,1,0:T(8,128)S(1)}, u32[]{:S(2)}, u32[]{:S(2)}) collective-permute-start(f32[3,40,256]{2,1,0:T(8,128)S(1)} %collective-permute-done.12.refs_5_), channel_id=1, source_target_pairs={{0,8},{4,12},{8,0},{12,4},{16,24},{20,28},{24,16},{28,20},{1,9},{5... | collective-permute-start | bytes 368648 | tf_op jit(solution)/shard_map/ppermute | solution.py:296
  74.3 1.8 %collective-permute-done.26.refs_13_ = f32[3,24,256]{2,1,0:T(8,128)S(1)} collective-permute-done((f32[3,24,256]{2,1,0:T(8,128)S(1)}, f32[3,24,256]{2,1,0:T(8,128)S(1)}, u32[]{:S(2)}, u32[]{:S(2)}) %collective-permute-start.26) | collective-permute-done | bytes 73760 | tf_op jit(solution)/shard_map/ppermute | solution.py:239
  76.1 6.2 %collective-permute-done.24.refs_11_ = f32[3,24,256]{2,1,0:T(8,128)S(1)} collective-permute-done((f32[3,24,256]{2,1,0:T(8,128)S(1)}, f32[3,24,256]{2,1,0:T(8,128)S(1)}, u32[]{:S(2)}, u32[]{:S(2)}) %collective-permute-start.24) | collective-permute-done | bytes 73760 | tf_op jit(solution)/shard_map/ppermute | solution.py:239
  83.8 0.8 collective-permute-done.27.refs_14_
  84.8 2.0 %place.1 = f32[3,64,2048]{2,1,0:T(8,128)} custom-call(s32[2]{0:T(128)S(1)} %pad_add_fusion.refs_0_, f32[3,40,256]{2,1,0:T(8,128)S(1)} %composite.2.refs_10_.refs_1_, f32[3,40,256]{2,1,0:T(8,128)S(1)} %collective-permute-done.9.refs_2_, f32[3,40,256]{2,1,0:T(8,128)S(1)} %collective-permute-done.10.refs_3_, f32[3,40,256]{2,1,0:T(8,128)S(1)} %collective-permute-done.11.refs_4_, ...), custom_call_target="tpu_custom_call" | custom-call | bytes 7380000 | tf_op jit(solution)/shard_map/place/pallas_call | solution.py:25
  (59 shorter events, 5.0 us)
Async XLA Ops:
  11.6 26.9 %collective-permute-start = (f32[2,4,40,256]{3,2,1,0:T(8,128)S(1)}, f32[2,4,40,256]{3,2,1,0:T(8,128)S(1)}, u32[]{:S(2)}, u32[]{:S(2)}) collective-permute-start(f32[2,4,40,256]{3,2,1,0:T(8,128)S(1)} %get-tuple-element.16), channel_id=1, source_target_pairs={{0,8},{4,12},{8,16},{12,20},{16,24},{20,28},{24,0},{28,4},{1,9},{5... | collective-permute-start | bytes 983048 | tf_op jit(solution)/shard_map/ppermute | solution.py:239
  16.3 8.8 %collective-permute-start.7 = (f32[16,1,2048]{2,1,0:T(1,128)S(1)}, f32[16,1,2048]{2,1,0:T(1,128)S(1)}, u32[]{:S(2)}, u32[]{:S(2)}) collective-permute-start(f32[16,1,2048]{2,1,0:T(1,128)S(1)} %get-tuple-element.19), channel_id=1, source_target_pairs={{0,1},{1,2},{2,3},{4,5},{5,6},{6,7},{8,9},{9,10},{10,11},{12,13},{... | collective-permute-start | bytes 393224 | tf_op jit(solution)/shard_map/ppermute | solution.py:273
  19.7 20.8 %collective-permute-start.1 = (f32[2,4,40,256]{3,2,1,0:T(8,128)S(1)}, f32[2,4,40,256]{3,2,1,0:T(8,128)S(1)}, u32[]{:S(2)}, u32[]{:S(2)}) collective-permute-start(f32[2,4,40,256]{3,2,1,0:T(8,128)S(1)} %get-tuple-element.17), channel_id=1, source_target_pairs={{0,16},{4,20},{8,24},{12,28},{16,0},{20,4},{24,8},{28,12},{1,17},{... | collective-permute-start | bytes 983048 | tf_op jit(solution)/shard_map/ppermute | solution.py:239
  22.4 6.8 %collective-permute-start.8 = (f32[16,1,2048]{2,1,0:T(1,128)S(1)}, f32[16,1,2048]{2,1,0:T(1,128)S(1)}, u32[]{:S(2)}, u32[]{:S(2)}) collective-permute-start(f32[16,1,2048]{2,1,0:T(1,128)S(1)} %get-tuple-element.20), channel_id=1, source_target_pairs={{1,0},{2,1},{3,2},{5,4},{6,5},{7,6},{9,8},{10,9},{11,10},{13,12},{... | collective-permute-start | bytes 393224 | tf_op jit(solution)/shard_map/ppermute | solution.py:273
  23.7 17.9 %collective-permute-start.2 = (f32[2,4,40,256]{3,2,1,0:T(8,128)S(1)}, f32[2,4,40,256]{3,2,1,0:T(8,128)S(1)}, u32[]{:S(2)}, u32[]{:S(2)}) collective-permute-start(f32[2,4,40,256]{3,2,1,0:T(8,128)S(1)} %get-tuple-element.18), channel_id=1, source_target_pairs={{0,24},{4,28},{8,0},{12,4},{16,8},{20,12},{24,16},{28,20},{1,25},{... | collective-permute-start | bytes 983048 | tf_op jit(solution)/shard_map/ppermute | solution.py:239
  36.6 9.7 %collective-permute-start.16 = (f32[2,4,24,256]{3,2,1,0:T(8,128)S(1)}, f32[2,4,24,256]{3,2,1,0:T(8,128)S(1)}, u32[]{:S(2)}, u32[]{:S(2)}) collective-permute-start(f32[2,4,24,256]{3,2,1,0:T(8,128)S(1)} %get-tuple-element.22), channel_id=1, source_target_pairs={{0,8},{4,12},{8,16},{12,20},{16,24},{20,28},{24,0},{28,4},{1,9},{5... | collective-permute-start | bytes 589832 | tf_op jit(solution)/shard_map/ppermute | solution.py:239
  36.8 21.4 %collective-permute-start.17 = (f32[2,4,24,256]{3,2,1,0:T(8,128)S(1)}, f32[2,4,24,256]{3,2,1,0:T(8,128)S(1)}, u32[]{:S(2)}, u32[]{:S(2)}) collective-permute-start(f32[2,4,24,256]{3,2,1,0:T(8,128)S(1)} %get-tuple-element.23), channel_id=1, source_target_pairs={{0,16},{4,20},{8,24},{12,28},{16,0},{20,4},{24,8},{28,12},{1,17},{... | collective-permute-start | bytes 589832 | tf_op jit(solution)/shard_map/ppermute | solution.py:239
  38.5 19.8 %collective-permute-start.18 = (f32[2,4,24,256]{3,2,1,0:T(8,128)S(1)}, f32[2,4,24,256]{3,2,1,0:T(8,128)S(1)}, u32[]{:S(2)}, u32[]{:S(2)}) collective-permute-start(f32[2,4,24,256]{3,2,1,0:T(8,128)S(1)} %get-tuple-element.24), channel_id=1, source_target_pairs={{0,24},{4,28},{8,0},{12,4},{16,8},{20,12},{24,16},{28,20},{1,25},{... | collective-permute-start | bytes 589832 | tf_op jit(solution)/shard_map/ppermute | solution.py:239
  40.5 18.4 %collective-permute-start.3 = (f32[1,4,40,256]{3,2,1,0:T(8,128)S(1)}, f32[1,4,40,256]{3,2,1,0:T(8,128)S(1)}, u32[]{:S(2)}, u32[]{:S(2)}) collective-permute-start(f32[1,4,40,256]{3,2,1,0:T(8,128)S(1)} %slice.24), channel_id=1, source_target_pairs={{0,4},{4,0},{8,12},{12,8},{16,20},{20,16},{24,28},{28,24},{1,5},{5... | collective-permute-start | bytes 491528 | tf_op jit(solution)/shard_map/ppermute | solution.py:236
  41.6 17.4 %collective-permute-start.4 = (f32[1,4,40,256]{3,2,1,0:T(8,128)S(1)}, f32[1,4,40,256]{3,2,1,0:T(8,128)S(1)}, u32[]{:S(2)}, u32[]{:S(2)}) collective-permute-start(f32[1,4,40,256]{3,2,1,0:T(8,128)S(1)} %slice.32), channel_id=1, source_target_pairs={{0,4},{4,0},{8,12},{12,8},{16,20},{20,16},{24,28},{28,24},{1,5},{5... | collective-permute-start | bytes 491528 | tf_op jit(solution)/shard_map/ppermute | solution.py:236
  46.2 13.2 %collective-permute-start.5 = (f32[1,4,40,256]{3,2,1,0:T(8,128)S(1)}, f32[1,4,40,256]{3,2,1,0:T(8,128)S(1)}, u32[]{:S(2)}, u32[]{:S(2)}) collective-permute-start(f32[1,4,40,256]{3,2,1,0:T(8,128)S(1)} %slice.33), channel_id=1, source_target_pairs={{0,4},{4,0},{8,12},{12,8},{16,20},{20,16},{24,28},{28,24},{1,5},{5... | collective-permute-start | bytes 491528 | tf_op jit(solution)/shard_map/ppermute | solution.py:236
  58.3 6.1 %collective-permute-start.19 = (f32[1,4,24,256]{3,2,1,0:T(8,128)S(1)}, f32[1,4,24,256]{3,2,1,0:T(8,128)S(1)}, u32[]{:S(2)}, u32[]{:S(2)}) collective-permute-start(f32[1,4,24,256]{3,2,1,0:T(8,128)S(1)} %slice.28), channel_id=1, source_target_pairs={{0,4},{4,0},{8,12},{12,8},{16,20},{20,16},{24,28},{28,24},{1,5},{5... | collective-permute-start | bytes 294920 | tf_op jit(solution)/shard_map/ppermute | solution.py:236
  58.9 5.5 %collective-permute-start.20 = (f32[1,4,24,256]{3,2,1,0:T(8,128)S(1)}, f32[1,4,24,256]{3,2,1,0:T(8,128)S(1)}, u32[]{:S(2)}, u32[]{:S(2)}) collective-permute-start(f32[1,4,24,256]{3,2,1,0:T(8,128)S(1)} %slice.35), channel_id=1, source_target_pairs={{0,4},{4,0},{8,12},{12,8},{16,20},{20,16},{24,28},{28,24},{1,5},{5... | collective-permute-start | bytes 294920 | tf_op jit(solution)/shard_map/ppermute | solution.py:236
  59.0 5.4 %collective-permute-start.21 = (f32[1,4,24,256]{3,2,1,0:T(8,128)S(1)}, f32[1,4,24,256]{3,2,1,0:T(8,128)S(1)}, u32[]{:S(2)}, u32[]{:S(2)}) collective-permute-start(f32[1,4,24,256]{3,2,1,0:T(8,128)S(1)} %slice.36), channel_id=1, source_target_pairs={{0,4},{4,0},{8,12},{12,8},{16,20},{20,16},{24,28},{28,24},{1,5},{5... | collective-permute-start | bytes 294920 | tf_op jit(solution)/shard_map/ppermute | solution.py:236
  59.5 4.9 %collective-permute-start.22 = (f32[1,4,24,256]{3,2,1,0:T(8,128)S(1)}, f32[1,4,24,256]{3,2,1,0:T(8,128)S(1)}, u32[]{:S(2)}, u32[]{:S(2)}) collective-permute-start(f32[1,4,24,256]{3,2,1,0:T(8,128)S(1)} %slice.37), channel_id=1, source_target_pairs={{0,4},{4,0},{8,12},{12,8},{16,20},{20,16},{24,28},{28,24},{1,5},{5... | collective-permute-start | bytes 294920 | tf_op jit(solution)/shard_map/ppermute | solution.py:236
  60.9 8.9 %collective-permute-start.12 = (f32[3,40,256]{2,1,0:T(8,128)S(1)}, f32[3,40,256]{2,1,0:T(8,128)S(1)}, u32[]{:S(2)}, u32[]{:S(2)}) collective-permute-start(f32[3,40,256]{2,1,0:T(8,128)S(1)} %composite.2.refs_10_.refs_1_), channel_id=1, source_target_pairs={{0,16},{4,20},{8,24},{12,28},{16,0},{20,4},{24,8},{28,12},{1,17},{... | collective-permute-start | bytes 368648 | tf_op jit(solution)/shard_map/ppermute | solution.py:296
  65.5 8.8 %collective-permute-start.28 = (f32[3,24,256]{2,1,0:T(8,128)S(1)}, f32[3,24,256]{2,1,0:T(8,128)S(1)}, u32[]{:S(2)}, u32[]{:S(2)}) collective-permute-start(f32[3,24,256]{2,1,0:T(8,128)S(1)} %composite.3.refs_9_), channel_id=1, source_target_pairs={{0,24},{4,28},{8,0},{12,4},{16,8},{20,12},{24,16},{28,20},{1,25},{... | collective-permute-start | bytes 221192 | tf_op jit(solution)/shard_map/ppermute | solution.py:239
  68.9 7.2 %collective-permute-start.26 = (f32[3,24,256]{2,1,0:T(8,128)S(1)}, f32[3,24,256]{2,1,0:T(8,128)S(1)}, u32[]{:S(2)}, u32[]{:S(2)}) collective-permute-start(f32[3,24,256]{2,1,0:T(8,128)S(1)} %composite.3.refs_9_), channel_id=1, source_target_pairs={{0,16},{4,20},{8,24},{12,28},{16,0},{20,4},{24,8},{28,12},{1,17},{... | collective-permute-start | bytes 221192 | tf_op jit(solution)/shard_map/ppermute | solution.py:239
  69.9 12.9 %collective-permute-start.10 = (f32[3,40,256]{2,1,0:T(8,128)S(1)}, f32[3,40,256]{2,1,0:T(8,128)S(1)}, u32[]{:S(2)}, u32[]{:S(2)}) collective-permute-start(f32[3,40,256]{2,1,0:T(8,128)S(1)} %composite.2.refs_10_.refs_1_), channel_id=1, source_target_pairs={{0,8},{4,12},{8,0},{12,4},{16,24},{20,28},{24,16},{28,20},{1,9},{5... | collective-permute-start | bytes 368648 | tf_op jit(solution)/shard_map/ppermute | solution.py:296
  69.9 13.0 %collective-permute-start.14 = (f32[3,40,256]{2,1,0:T(8,128)S(1)}, f32[3,40,256]{2,1,0:T(8,128)S(1)}, u32[]{:S(2)}, u32[]{:S(2)}) collective-permute-start(f32[3,40,256]{2,1,0:T(8,128)S(1)} %collective-permute-done.12.refs_5_), channel_id=1, source_target_pairs={{0,8},{4,12},{8,0},{12,4},{16,24},{20,28},{24,16},{28,20},{1,9},{5... | collective-permute-start | bytes 368648 | tf_op jit(solution)/shard_map/ppermute | solution.py:296
  74.2 8.0 %collective-permute-start.24 = (f32[3,24,256]{2,1,0:T(8,128)S(1)}, f32[3,24,256]{2,1,0:T(8,128)S(1)}, u32[]{:S(2)}, u32[]{:S(2)}) collective-permute-start(f32[3,24,256]{2,1,0:T(8,128)S(1)} %composite.3.refs_9_), channel_id=1, source_target_pairs={{0,8},{4,12},{8,16},{12,20},{16,24},{20,28},{24,0},{28,4},{1,9},{5... | collective-permute-start | bytes 221192 | tf_op jit(solution)/shard_map/ppermute | solution.py:239
  74.3 9.0 %collective-permute-start.9 = (f32[3,40,256]{2,1,0:T(8,128)S(1)}, f32[3,40,256]{2,1,0:T(8,128)S(1)}, u32[]{:S(2)}, u32[]{:S(2)}) collective-permute-start(f32[3,40,256]{2,1,0:T(8,128)S(1)} %composite.2.refs_10_.refs_1_), channel_id=1, source_target_pairs={{0,4},{4,0},{8,12},{12,8},{16,20},{20,16},{24,28},{28,24},{1,5},{5... | collective-permute-start | bytes 368648 | tf_op jit(solution)/shard_map/ppermute | solution.py:236
  76.1 6.2 %collective-permute-start.23 = (f32[3,24,256]{2,1,0:T(8,128)S(1)}, f32[3,24,256]{2,1,0:T(8,128)S(1)}, u32[]{:S(2)}, u32[]{:S(2)}) collective-permute-start(f32[3,24,256]{2,1,0:T(8,128)S(1)} %composite.3.refs_9_), channel_id=1, source_target_pairs={{0,4},{4,0},{8,12},{12,8},{16,20},{20,16},{24,28},{28,24},{1,5},{5... | collective-permute-start | bytes 221192 | tf_op jit(solution)/shard_map/ppermute | solution.py:236
  82.2 2.5 %collective-permute-start.13 = (f32[3,40,256]{2,1,0:T(8,128)S(1)}, f32[3,40,256]{2,1,0:T(8,128)S(1)}, u32[]{:S(2)}, u32[]{:S(2)}) collective-permute-start(f32[3,40,256]{2,1,0:T(8,128)S(1)} %collective-permute-done.12.refs_5_), channel_id=1, source_target_pairs={{0,4},{4,0},{8,12},{12,8},{16,20},{20,16},{24,28},{28,24},{1,5},{5... | collective-permute-start | bytes 368648 | tf_op jit(solution)/shard_map/ppermute | solution.py:236
  (10 other events, 83.3 us)

commit v4 on v3

--- a/solution.py
+++ b/solution.py
@@ -24,7 +24,7 @@
 
     return pl.pallas_call(
         with_events,
-        in_specs=specs + [pl.BlockSpec(memory_space=pl.ANY)] * len(events),
+        in_specs=list(specs) + [pl.BlockSpec(memory_space=pl.ANY)] * len(events),
         compiler_params=pltpu.CompilerParams(vmem_limit_bytes=VMEM_LIMIT),
         **options,
     )(*operands, *events)
@@ -38,23 +38,21 @@
     return sum(number for _, number in runs)
 
 
-def edges_kernel(field_ref, first_ref, last_ref, buffer, sem):
+def edges_kernel(field_ref, first_ref, last_ref, sem):
     rows = field_ref.shape[1]
     copies = [
-        pltpu.make_async_copy(field_ref.at[:, pl.ds(row, SUB), :], buffer.at[i], sem.at[i])
-        for i, row in enumerate((0, rows - SUB))
+        pltpu.make_async_copy(field_ref.at[:, pl.ds(row, 1), :], ref, sem.at[i])
+        for i, (row, ref) in enumerate(((0, first_ref), (rows - 1, last_ref)))
     ]
     for copy in copies:
         copy.start()
     for copy in copies:
         copy.wait()
-    first_ref[...] = buffer[0, :, :1, :]
-    last_ref[...] = buffer[1, :, SUB - 1 :, :]
-
-
-def render_kernel(runs, tiles, chips, scale, where_ref, transfer_ref, light_ref, field_ref, *refs):
-    out_refs, (padded, sem) = refs[-2 - chips : -2], refs[-2:]
-    edges = list(refs[: -2 - chips])
+
+
+def render_kernel(runs, tiles, chips, offsets, scale, where_ref, transfer_ref, light_ref, field_ref, *refs):
+    out_refs, (padded, sem) = refs[-2 - len(offsets) : -2], refs[-2:]
+    edges = list(refs[: -2 - len(offsets)])
     planes, _, columns = field_ref.shape
     part = out_refs[0].shape[3]
     my_chip, my_core = where_ref[0], where_ref[1]
@@ -134,18 +132,18 @@
                 out_ref[relative, c, pl.ds(out_row, SUB), lanes] = 0.25 * (total[v] + sums[c][v])
             out_ref[relative, 3, pl.ds(out_row, SUB), lanes] = depth[v] * scale
 
-    for k, out_ref in enumerate(out_refs):
+    for step, (k, out_ref) in enumerate(zip(offsets, out_refs)):
         chip = lax.rem(my_chip + k, chips)
         for first, number, low, high, slot, written, before, behind in layout:
-            if k == 0:
+            if step == 0:
                 for tile in range(low, min(first + 1, high)):
                     tile_copy(tile, slot + tile - low).wait()
 
-            def one_tile(index, carry, k=k, out_ref=out_ref, chip=chip, run=(first, low, high, slot, written, before, behind)):
+            def one_tile(index, carry, step=step, out_ref=out_ref, chip=chip, run=(first, low, high, slot, written, before, behind)):
                 first, low, high, slot, written, before, behind = run
                 here = slot + first - low + index
 
-                if k == 0:
+                if step == 0:
 
                     @pl.when(first + index + 1 < high)
                     def _():
@@ -158,40 +156,41 @@
             lax.fori_loop(0, number, one_tile, 0)
 
 
-def composite_kernel(chips, count, where_ref, rank_ref, *refs):
-    inputs, out_ref = refs[:-1], refs[-1]
+def split_kernel(*refs):
+    count = len(refs) // 2
+    for block_ref, out_ref in zip(refs[:count], refs[count:]):
+        out_ref[...] = block_ref[1:]
+
+
+def composite_kernel(chips, where_ref, rank_ref, *refs):
+    own, other, out_ref = refs[:chips], refs[chips:-1], refs[-1]
     my_chip, my_core = where_ref[0], where_ref[1]
-    ranks = []
+    blocks, ranks = [], []
     for k in range(chips):
         chip = lax.rem(my_chip + chips - k, chips)
-        ranks += [rank_ref[chip * CORES + core] for core in (my_core, CORES - 1 - my_core)]
+        for core, ref in ((my_core, own[k]), (CORES - 1 - my_core, other[k])):
+            blocks.append(ref)
+            ranks.append(rank_ref[chip * CORES + core])
     bricks = len(ranks)
     ahead = [[(ranks[j] < ranks[i]).astype(jnp.float32) for j in range(bricks)] for i in range(bricks)]
     columns = out_ref.shape[2] // LANE
-    written = 0
-    for n in range(count):
-        own, other = inputs[2 * n * chips : (2 * n + 1) * chips], inputs[(2 * n + 1) * chips : (2 * n + 2) * chips]
-        blocks = [ref for pair in zip(own, other) for ref in pair]
-        rows = own[0].shape[2]
-
-        def one(index, carry, blocks=blocks, written=written):
-            tile = index // columns
-            row = pl.multiple_of(tile * SUB, SUB)
-            lanes = pl.ds(pl.multiple_of((index - tile * columns) * LANE, LANE), LANE)
-            at = (pl.ds(row, SUB), lanes)
-            depths = [ref[(0, 3, *at)] for ref in blocks]
-            sums = [background * jnp.exp2(-functools.reduce(jnp.add, depths))] * 3
-            for i in range(bricks):
-                front = functools.reduce(jnp.add, [ahead[i][j] * depths[j] for j in range(bricks) if j != i])
-                weight = jnp.exp2(-front)
-                for c in range(3):
-                    sums[c] = sums[c] + weight * blocks[i][(0, c, *at)]
+
+    def one(index, carry):
+        tile = index // columns
+        lanes = pl.ds(pl.multiple_of((index - tile * columns) * LANE, LANE), LANE)
+        at = (pl.ds(pl.multiple_of(tile * SUB, SUB), SUB), lanes)
+        depths = [ref[(0, 3, *at)] for ref in blocks]
+        sums = [background * jnp.exp2(-functools.reduce(jnp.add, depths))] * 3
+        for i in range(bricks):
+            front = functools.reduce(jnp.add, [ahead[i][j] * depths[j] for j in range(bricks) if j != i])
+            weight = jnp.exp2(-front)
             for c in range(3):
-                out_ref[c, pl.ds(pl.multiple_of(row + written, SUB), SUB), lanes] = sums[c]
-            return carry
-
-        lax.fori_loop(0, rows // SUB * columns, one, 0)
-        written += rows
+                sums[c] = sums[c] + weight * blocks[i][(0, c, *at)]
+        for c in range(3):
+            out_ref[(c, *at)] = sums[c]
+        return carry
+
+    lax.fori_loop(0, out_ref.shape[1] // SUB * columns, one, 0)
 
 
 def place_kernel(groups, where_ref, *refs):
@@ -238,21 +237,21 @@
     def send(value, k):
         return lax.ppermute(value, "wide", [(i, (i + k * CORES) % wide) for i in range(wide)])
 
-    def render(runs, edges=(), events=()):
+    def render(runs, offsets, edges, events):
         slots = sum(min(first + number + 1, tiles) - max(first - 1, 0) for first, number in runs)
         block = pltpu.VMEM((CORES, 4, tiles_of(runs) * SUB, part), jnp.float32)
         return call(
-            functools.partial(render_kernel, runs, tiles, chips, scale),
+            functools.partial(render_kernel, runs, tiles, chips, offsets, scale),
             [where, transfer, light_dir, field, *edges],
             [smem] * 3 + [hbm] + [vmem] * len(edges),
             events,
-            out_shape=[block] * chips,
-            out_specs=[vmem] * chips,
+            out_shape=[block] * len(offsets),
+            out_specs=[vmem] * len(offsets),
             scratch_shapes=[
                 pltpu.VMEM((planes, slots * SUB, columns + 2 * LANE), jnp.float32),
                 pltpu.SemaphoreType.DMA((slots,)),
             ],
-            cost_estimate=lasting(2.5 * tiles_of(runs)),
+            cost_estimate=lasting(0.6 * len(offsets) * tiles_of(runs)),
             name="render",
         )
 
@@ -265,22 +264,31 @@
             events,
             out_shape=[edge] * 2,
             out_specs=[vmem] * 2,
-            scratch_shapes=[pltpu.VMEM((2, planes, SUB, columns), jnp.float32), pltpu.SemaphoreType.DMA((2,))],
+            scratch_shapes=[pltpu.SemaphoreType.DMA((2,))],
             cost_estimate=lasting(1.2),
             name="edges",
         )
         up = [(i, i + 1) for i in range(narrow - 1)]
         return lax.ppermute(last_row, "narrow", up), lax.ppermute(first_row, "narrow", [(j, i) for i, j in up])
 
-    def composite(parts_of, runs, events):
-        operands = []
-        for own in parts_of:
-            operands += own + [swap(value[1:]) for value in own]
+    def other_halves(arrays, events):
+        halves = call(
+            split_kernel,
+            arrays,
+            [vmem] * len(arrays),
+            events,
+            out_shape=[pltpu.VMEM((1, *arrays[0].shape[1:]), jnp.float32)] * len(arrays),
+            out_specs=[vmem] * len(arrays),
+            cost_estimate=lasting(0.3),
+            name="split",
+        )
+        return [swap(value) for value in halves]
+
+    def composite(own, other, runs):
         return call(
-            functools.partial(composite_kernel, chips, len(parts_of)),
-            [where, depth_rank, *operands],
-            [smem] * 2 + [vmem] * len(operands),
-            events,
+            functools.partial(composite_kernel, chips),
+            [where, depth_rank, *own, *other],
+            [smem] * 2 + [vmem] * (2 * chips),
             out_shape=pltpu.VMEM((3, tiles_of(runs) * SUB, part), jnp.float32),
             out_specs=vmem,
             cost_estimate=lasting(1.0),
@@ -302,20 +310,25 @@
         values = [tile] + [send(tile, k) for k in range(1, chips)]
         return values, lambda chip: [lax.rem(chip + chips - k, chips) for k in range(chips)]
 
-    sent, last, edges = [], [], ()
+    early = [tuple(range(chips // 2, 0, -1)), (*range(chips // 2 + 1, chips), 0)]
+    sent, near, last, edges = [], [], [], ()
     for i, runs in enumerate(chunks):
         if i == len(chunks) - 1:
             edges = edge_rows(last)
-        blocks = render(runs, edges, last)
-        last = [blocks[0]]
+        blocks = {}
+        for offsets in early if i == 0 else [tuple(range(chips))]:
+            values = render(runs, offsets, edges, last)
+            blocks.update(zip(offsets, values))
+            last = list(values[:1])
+        near += other_halves([blocks[0]], [])
         sent.append([blocks[0]] + [send(blocks[k], k) for k in range(1, chips)])
 
     groups, finished = [], []
-    for first, end, gather in ((0, len(chunks) - 1, gather_by_halves), (len(chunks) - 1, len(chunks), gather_directly)):
-        runs = sum(chunks[first:end], ())
-        tile = composite(sent[first:end], runs, last)
-        last = [tile]
+    for runs, own, first, gather in zip(chunks, sent, near, (gather_by_halves, gather_directly)):
+        other = [first] + other_halves(own[1:], last)
+        tile = composite(own, other, runs)
         values, chip_of = gather(tile)
+        last = values[2:3]
         groups.append((runs, chip_of))
         for value in values:
             finished += [value, swap(value)]

time: 86.9 us -> 85.1 us (0.979)
  starting transfers between devices: 30.6 us -> 25.6 us
  Pallas kernels: 23.4 us -> 25.3 us
  waiting for transfers between devices: 31.1 us -> 32.3 us
    ppermute x9, waiting for transfers between devices: 25.6 us -> 16.1 us  [send(): lax.ppermute(value, 'wide', [(i, (i + k * CORES) % wide) for i in range(w...]
    ppermute x3, waiting for transfers between devices: 0.01 us -> 8.95 us  [gather_by_halves(): tiles_by[m ^ bit] = lax.ppermute(tiles_by[m], 'wide', pairs)]
    ppermute x3, starting transfers between devices: 7.8 us -> 2.65 us  [gather_by_halves(): tiles_by[m ^ bit] = lax.ppermute(tiles_by[m], 'wide', pairs)]
    pallas_call x6 -> x11, Pallas kernels: 23.4 us -> 25.3 us  [call(): pl.pallas_call(with_events, in_specs=list(specs) + [pl.BlockSpec(memory_s...]
    ppermute x1, waiting for transfers between devices: 0.01 us -> 1.18 us  [edge_rows(): lax.ppermute(last_row, 'narrow', up)]
  transfers between devices with their start and end apart: 30 -> 30, of which waited for: 10 -> 11; matrix products, arithmetic and copies ran while one was open for 0% -> 0% of each run, Pallas kernels for 13% -> 20%
where the time goes in v4:
time: 85.1 us; the launch traced here: 84.9 us
  waiting for transfers between devices  32.3 us (38%)
  starting transfers between devices  25.6 us (30%)
  Pallas kernels  25.3 us (30%)
  local copies, waits for them, and re-layouts  1.34 us (2%)
    pallas_call x11, Pallas kernels, call(): pl.pallas_call(with_events, in_specs=list(specs) + [pl.BlockSpec(memory_s...  25.3 us
    ppermute x9, waiting for transfers between devices, send(): lax.ppermute(value, 'wide', [(i, (i + k * CORES) % wide) for i in range(w...  16.1 us
    ppermute x9, starting transfers between devices, send(): lax.ppermute(value, 'wide', [(i, (i + k * CORES) % wide) for i in range(w...  15 us
    ppermute x3, waiting for transfers between devices, gather_by_halves(): tiles_by[m ^ bit] = lax.ppermute(tiles_by[m], 'wide', pairs)  8.95 us
    ppermute x1, waiting for transfers between devices, edge_rows(): lax.ppermute(first_row, 'narrow', [(j, i) for i, j in up])  4.72 us
    ppermute x1, starting transfers between devices, edge_rows(): lax.ppermute(last_row, 'narrow', up)  3.4 us
    ppermute x16, starting transfers between devices, swap(): return lax.ppermute(value, 'wide', [(i, i ^ 1) for i in range(wide)])  3.34 us
    ppermute x3, starting transfers between devices, gather_by_halves(): tiles_by[m ^ bit] = lax.ppermute(tiles_by[m], 'wide', pairs)  2.65 us
  transfers between devices with their start and end apart: 30, of which 11 were waited for; matrix products, arithmetic and copies ran while one was open for 0% of the time, Pallas kernels for 20%

profile of v4, /device:TPU:0, one launch (start us, length us, event | category | flops | bytes accessed | tf_op | source)
XLA Modules:
  0.0 84.9 jit_solution(10274720888636483716)
XLA Ops:
  1.4 6.3 %render.3 = (f32[2,4,40,256]{3,2,1,0:T(8,128)S(1)}, f32[2,4,40,256]{3,2,1,0:T(8,128)S(1)}) custom-call(s32[2]{0:T(128)S(1)} %pad_add_fusion.refs_0_, f32[2,3]{1,0:T(2,128)S(1)} %copy-done, f32[3]{0:T(128)S(1)} %copy-done.1, f32[16,64,2048]{2,1,0:T(8,128)} %refs_3_.5), custom_call_target="tpu_custom_call" | custom-call | bytes 22140000 | tf_op jit(solution)/shard_map/render/pallas_call | solution.py:25
  7.8 3.1 %collective-permute-start = (f32[2,4,40,256]{3,2,1,0:T(8,128)S(1)}, f32[2,4,40,256]{3,2,1,0:T(8,128)S(1)}, u32[]{:S(2)}, u32[]{:S(2)}) collective-permute-start(f32[2,4,40,256]{3,2,1,0:T(8,128)S(1)} %get-tuple-element.23), channel_id=1, source_target_pairs={{0,8},{4,12},{8,16},{12,20},{16,24},{20,28},{24,0},{28,4},{1,9},{5... | collective-permute-start | bytes 983048 | tf_op jit(solution)/shard_map/ppermute | solution.py:238
  10.8 2.6 %collective-permute-start.1 = (f32[2,4,40,256]{3,2,1,0:T(8,128)S(1)}, f32[2,4,40,256]{3,2,1,0:T(8,128)S(1)}, u32[]{:S(2)}, u32[]{:S(2)}) collective-permute-start(f32[2,4,40,256]{3,2,1,0:T(8,128)S(1)} %get-tuple-element.21.refs_4_), channel_id=1, source_target_pairs={{0,16},{4,20},{8,24},{12,28},{16,0},{20,4},{24,8},{28,12},{1,17},{... | collective-permute-start | bytes 983048 | tf_op jit(solution)/shard_map/ppermute | solution.py:238
  13.4 6.3 %render.4 = (f32[2,4,40,256]{3,2,1,0:T(8,128)S(1)}, f32[2,4,40,256]{3,2,1,0:T(8,128)S(1)}) custom-call(s32[2]{0:T(128)S(1)} %pad_add_fusion.refs_0_, f32[2,3]{1,0:T(2,128)S(1)} %copy-done, f32[3]{0:T(128)S(1)} %copy-done.1, f32[16,64,2048]{2,1,0:T(8,128)} %refs_3_.5, f32[2,4,40,256]{3,2,1,0:T(8,128)S(1)} %get-tuple-element.21.refs_4_), custom_call_target="tpu_custom_call" | custom-call | bytes 22140000 | tf_op jit(solution)/shard_map/render/pallas_call | solution.py:25
  19.8 1.4 %collective-permute-start.2 = (f32[2,4,40,256]{3,2,1,0:T(8,128)S(1)}, f32[2,4,40,256]{3,2,1,0:T(8,128)S(1)}, u32[]{:S(2)}, u32[]{:S(2)}) collective-permute-start(f32[2,4,40,256]{3,2,1,0:T(8,128)S(1)} %get-tuple-element.24.refs_1_.refs_6_), channel_id=1, source_target_pairs={{0,24},{4,28},{8,0},{12,4},{16,8},{20,12},{24,16},{28,20},{1,25},{... | collective-permute-start | bytes 983048 | tf_op jit(solution)/shard_map/ppermute | solution.py:238
  21.2 1.0 %edges.1 = (f32[16,1,2048]{2,1,0:T(1,128)S(1)}, f32[16,1,2048]{2,1,0:T(1,128)S(1)}) custom-call(f32[16,64,2048]{2,1,0:T(8,128)} %refs_3_.5, f32[2,4,40,256]{3,2,1,0:T(8,128)S(1)} %get-tuple-element.24.refs_1_.refs_6_), custom_call_target="tpu_custom_call" | custom-call | bytes 4428000 | tf_op jit(solution)/shard_map/edges/pallas_call | solution.py:25
  22.2 3.4 %collective-permute-start.4 = (f32[16,1,2048]{2,1,0:T(1,128)S(1)}, f32[16,1,2048]{2,1,0:T(1,128)S(1)}, u32[]{:S(2)}, u32[]{:S(2)}) collective-permute-start(f32[16,1,2048]{2,1,0:T(1,128)S(1)} %get-tuple-element.25), channel_id=1, source_target_pairs={{0,1},{1,2},{2,3},{4,5},{5,6},{6,7},{8,9},{9,10},{10,11},{12,13},{... | collective-permute-start | bytes 393224 | tf_op jit(solution)/shard_map/ppermute | solution.py:272
  25.6 1.3 %collective-permute-start.5 = (f32[16,1,2048]{2,1,0:T(1,128)S(1)}, f32[16,1,2048]{2,1,0:T(1,128)S(1)}, u32[]{:S(2)}, u32[]{:S(2)}) collective-permute-start(f32[16,1,2048]{2,1,0:T(1,128)S(1)} %get-tuple-element.26), channel_id=1, source_target_pairs={{1,0},{2,1},{3,2},{5,4},{6,5},{7,6},{9,8},{10,9},{11,10},{13,12},{... | collective-permute-start | bytes 393224 | tf_op jit(solution)/shard_map/ppermute | solution.py:272
  26.9 1.2 %collective-permute-done.4.refs_4_ = f32[16,1,2048]{2,1,0:T(1,128)S(1)} collective-permute-done((f32[16,1,2048]{2,1,0:T(1,128)S(1)}, f32[16,1,2048]{2,1,0:T(1,128)S(1)}, u32[]{:S(2)}, u32[]{:S(2)}) %collective-permute-start.4) | collective-permute-done | bytes 131104 | tf_op jit(solution)/shard_map/ppermute | solution.py:272
  28.1 4.7 %collective-permute-done.5.refs_5_ = f32[16,1,2048]{2,1,0:T(1,128)S(1)} collective-permute-done((f32[16,1,2048]{2,1,0:T(1,128)S(1)}, f32[16,1,2048]{2,1,0:T(1,128)S(1)}, u32[]{:S(2)}, u32[]{:S(2)}) %collective-permute-start.5) | collective-permute-done | bytes 131104 | tf_op jit(solution)/shard_map/ppermute | solution.py:272
  32.8 7.3 %render.5 = (f32[2,4,24,256]{3,2,1,0:T(8,128)S(1)}, f32[2,4,24,256]{3,2,1,0:T(8,128)S(1)}, f32[2,4,24,256]{3,2,1,0:T(8,128)S(1)}, f32[2,4,24,256]{3,2,1,0:T(8,128)S(1)}) custom-call(s32[2]{0:T(128)S(1)} %pad_add_fusion.refs_0_, f32[2,3]{1,0:T(2,128)S(1)} %copy-done, f32[3]{0:T(128)S(1)} %copy-done.1, f32[16,64,2048]{2,1,0:T(8,128)} %refs_3_.5, ...), custom_call_target="tpu_custom_call" | custom-call | bytes 26568000 | tf_op jit(solution)/shard_map/render/pallas_call | solution.py:25
  40.9 2.1 %collective-permute-start.16 = (f32[2,4,24,256]{3,2,1,0:T(8,128)S(1)}, f32[2,4,24,256]{3,2,1,0:T(8,128)S(1)}, u32[]{:S(2)}, u32[]{:S(2)}) collective-permute-start(f32[2,4,24,256]{3,2,1,0:T(8,128)S(1)} %get-tuple-element.31), channel_id=1, source_target_pairs={{0,8},{4,12},{8,16},{12,20},{16,24},{20,28},{24,0},{28,4},{1,9},{5... | collective-permute-start | bytes 589832 | tf_op jit(solution)/shard_map/ppermute | solution.py:238
  42.9 1.6 %collective-permute-start.17 = (f32[2,4,24,256]{3,2,1,0:T(8,128)S(1)}, f32[2,4,24,256]{3,2,1,0:T(8,128)S(1)}, u32[]{:S(2)}, u32[]{:S(2)}) collective-permute-start(f32[2,4,24,256]{3,2,1,0:T(8,128)S(1)} %get-tuple-element.32), channel_id=1, source_target_pairs={{0,16},{4,20},{8,24},{12,28},{16,0},{20,4},{24,8},{28,12},{1,17},{... | collective-permute-start | bytes 589832 | tf_op jit(solution)/shard_map/ppermute | solution.py:238
  45.3 1.3 %composite.2.refs_1_ = f32[3,40,256]{2,1,0:T(8,128)S(1)} custom-call(s32[2]{0:T(128)S(1)} %pad_add_fusion.refs_0_, s32[8]{0:T(128)S(1)} %copy-done.2, f32[2,4,40,256]{3,2,1,0:T(8,128)S(1)} %get-tuple-element.22.refs_0_.refs_2_, f32[2,4,40,256]{3,2,1,0:T(8,128)S(1)} %collective-permute-done.refs_0_.refs_3_, ...), custom_call_target="tpu_custom_call" | custom-call | bytes 3690000 | tf_op jit(solution)/shard_map/composite/pallas_call | solution.py:25
  46.6 1.5 %collective-permute-start.12 = (f32[3,40,256]{2,1,0:T(8,128)S(1)}, f32[3,40,256]{2,1,0:T(8,128)S(1)}, u32[]{:S(2)}, u32[]{:S(2)}) collective-permute-start(f32[3,40,256]{2,1,0:T(8,128)S(1)} %composite.2.refs_1_), channel_id=1, source_target_pairs={{0,16},{4,20},{8,24},{12,28},{16,0},{20,4},{24,8},{28,12},{1,17},{... | collective-permute-start | bytes 368648 | tf_op jit(solution)/shard_map/ppermute | solution.py:304
  48.1 1.2 %collective-permute-start.10 = (f32[3,40,256]{2,1,0:T(8,128)S(1)}, f32[3,40,256]{2,1,0:T(8,128)S(1)}, u32[]{:S(2)}, u32[]{:S(2)}) collective-permute-start(f32[3,40,256]{2,1,0:T(8,128)S(1)} %composite.2.refs_1_), channel_id=1, source_target_pairs={{0,8},{4,12},{8,0},{12,4},{16,24},{20,28},{24,16},{28,20},{1,9},{5... | collective-permute-start | bytes 368648 | tf_op jit(solution)/shard_map/ppermute | solution.py:304
  49.3 1.2 %collective-permute-done.16.refs_0_.refs_3_ = f32[2,4,24,256]{3,2,1,0:T(8,128)S(1)} collective-permute-done((f32[2,4,24,256]{3,2,1,0:T(8,128)S(1)}, f32[2,4,24,256]{3,2,1,0:T(8,128)S(1)}, u32[]{:S(2)}, u32[]{:S(2)}) %collective-permute-start.16) | collective-permute-done | bytes 196640 | tf_op jit(solution)/shard_map/ppermute | solution.py:238
  50.5 8.5 %collective-permute-done.17.refs_1_.refs_4_ = f32[2,4,24,256]{3,2,1,0:T(8,128)S(1)} collective-permute-done((f32[2,4,24,256]{3,2,1,0:T(8,128)S(1)}, f32[2,4,24,256]{3,2,1,0:T(8,128)S(1)}, u32[]{:S(2)}, u32[]{:S(2)}) %collective-permute-start.17) | collective-permute-done | bytes 196640 | tf_op jit(solution)/shard_map/ppermute | solution.py:238
  59.0 8.9 %collective-permute-done.12.refs_3_.refs_5_ = f32[3,40,256]{2,1,0:T(8,128)S(1)} collective-permute-done((f32[3,40,256]{2,1,0:T(8,128)S(1)}, f32[3,40,256]{2,1,0:T(8,128)S(1)}, u32[]{:S(2)}, u32[]{:S(2)}) %collective-permute-start.12) | collective-permute-done | bytes 122912 | tf_op jit(solution)/shard_map/ppermute | solution.py:304
  70.0 1.0 %composite.3.refs_9_ = f32[3,24,256]{2,1,0:T(8,128)S(1)} custom-call(s32[2]{0:T(128)S(1)} %pad_add_fusion.refs_0_, s32[8]{0:T(128)S(1)} %copy-done.2, f32[2,4,24,256]{3,2,1,0:T(8,128)S(1)} %get-tuple-element.27.refs_3_.refs_0_.refs_2_, f32[2,4,24,256]{3,2,1,0:T(8,128)S(1)} %collective-permute-done.16.refs_0_.refs_3_, ...), custom_call_target="tpu_custom_call" | custom-call | bytes 3690000 | tf_op jit(solution)/shard_map/composite/pallas_call | solution.py:25
  71.1 0.9 %collective-permute-start.28 = (f32[3,24,256]{2,1,0:T(8,128)S(1)}, f32[3,24,256]{2,1,0:T(8,128)S(1)}, u32[]{:S(2)}, u32[]{:S(2)}) collective-permute-start(f32[3,24,256]{2,1,0:T(8,128)S(1)} %composite.3.refs_9_), channel_id=1, source_target_pairs={{0,24},{4,28},{8,0},{12,4},{16,8},{20,12},{24,16},{28,20},{1,25},{... | collective-permute-start | bytes 221192 | tf_op jit(solution)/shard_map/ppermute | solution.py:238
  72.0 2.5 %collective-permute-start.26 = (f32[3,24,256]{2,1,0:T(8,128)S(1)}, f32[3,24,256]{2,1,0:T(8,128)S(1)}, u32[]{:S(2)}, u32[]{:S(2)}) collective-permute-start(f32[3,24,256]{2,1,0:T(8,128)S(1)} %composite.3.refs_9_), channel_id=1, source_target_pairs={{0,16},{4,20},{8,24},{12,28},{16,0},{20,4},{24,8},{28,12},{1,17},{... | collective-permute-start | bytes 221192 | tf_op jit(solution)/shard_map/ppermute | solution.py:238
  75.8 5.7 %collective-permute-done.26.refs_13_ = f32[3,24,256]{2,1,0:T(8,128)S(1)} collective-permute-done((f32[3,24,256]{2,1,0:T(8,128)S(1)}, f32[3,24,256]{2,1,0:T(8,128)S(1)}, u32[]{:S(2)}, u32[]{:S(2)}) %collective-permute-start.26) | collective-permute-done | bytes 73760 | tf_op jit(solution)/shard_map/ppermute | solution.py:238
  83.0 1.9 %place.1 = f32[3,64,2048]{2,1,0:T(8,128)} custom-call(s32[2]{0:T(128)S(1)} %pad_add_fusion.refs_0_, f32[3,40,256]{2,1,0:T(8,128)S(1)} %composite.2.refs_1_, f32[3,40,256]{2,1,0:T(8,128)S(1)} %collective-permute-done.9.refs_2_, f32[3,40,256]{2,1,0:T(8,128)S(1)} %collective-permute-done.10.refs_3_, f32[3,40,256]{2,1,0:T(8,128)S(1)} %collective-permute-done.11.refs_4_, ...), custom_call_target="tpu_custom_call" | custom-call | bytes 7380000 | tf_op jit(solution)/shard_map/place/pallas_call | solution.py:25
  (54 shorter events, 7.8 us)
Async XLA Ops:
  7.8 32.4 %collective-permute-start = (f32[2,4,40,256]{3,2,1,0:T(8,128)S(1)}, f32[2,4,40,256]{3,2,1,0:T(8,128)S(1)}, u32[]{:S(2)}, u32[]{:S(2)}) collective-permute-start(f32[2,4,40,256]{3,2,1,0:T(8,128)S(1)} %get-tuple-element.23), channel_id=1, source_target_pairs={{0,8},{4,12},{8,16},{12,20},{16,24},{20,28},{24,0},{28,4},{1,9},{5... | collective-permute-start | bytes 983048 | tf_op jit(solution)/shard_map/ppermute | solution.py:238
  10.8 29.3 %collective-permute-start.1 = (f32[2,4,40,256]{3,2,1,0:T(8,128)S(1)}, f32[2,4,40,256]{3,2,1,0:T(8,128)S(1)}, u32[]{:S(2)}, u32[]{:S(2)}) collective-permute-start(f32[2,4,40,256]{3,2,1,0:T(8,128)S(1)} %get-tuple-element.21.refs_4_), channel_id=1, source_target_pairs={{0,16},{4,20},{8,24},{12,28},{16,0},{20,4},{24,8},{28,12},{1,17},{... | collective-permute-start | bytes 983048 | tf_op jit(solution)/shard_map/ppermute | solution.py:238
  19.8 20.4 %collective-permute-start.2 = (f32[2,4,40,256]{3,2,1,0:T(8,128)S(1)}, f32[2,4,40,256]{3,2,1,0:T(8,128)S(1)}, u32[]{:S(2)}, u32[]{:S(2)}) collective-permute-start(f32[2,4,40,256]{3,2,1,0:T(8,128)S(1)} %get-tuple-element.24.refs_1_.refs_6_), channel_id=1, source_target_pairs={{0,24},{4,28},{8,0},{12,4},{16,8},{20,12},{24,16},{28,20},{1,25},{... | collective-permute-start | bytes 983048 | tf_op jit(solution)/shard_map/ppermute | solution.py:238
  22.2 5.9 %collective-permute-start.4 = (f32[16,1,2048]{2,1,0:T(1,128)S(1)}, f32[16,1,2048]{2,1,0:T(1,128)S(1)}, u32[]{:S(2)}, u32[]{:S(2)}) collective-permute-start(f32[16,1,2048]{2,1,0:T(1,128)S(1)} %get-tuple-element.25), channel_id=1, source_target_pairs={{0,1},{1,2},{2,3},{4,5},{5,6},{6,7},{8,9},{9,10},{10,11},{12,13},{... | collective-permute-start | bytes 393224 | tf_op jit(solution)/shard_map/ppermute | solution.py:272
  25.6 7.2 %collective-permute-start.5 = (f32[16,1,2048]{2,1,0:T(1,128)S(1)}, f32[16,1,2048]{2,1,0:T(1,128)S(1)}, u32[]{:S(2)}, u32[]{:S(2)}) collective-permute-start(f32[16,1,2048]{2,1,0:T(1,128)S(1)} %get-tuple-element.26), channel_id=1, source_target_pairs={{1,0},{2,1},{3,2},{5,4},{6,5},{7,6},{9,8},{10,9},{11,10},{13,12},{... | collective-permute-start | bytes 393224 | tf_op jit(solution)/shard_map/ppermute | solution.py:272
  28.1 14.9 %collective-permute-start.3 = (f32[1,4,40,256]{3,2,1,0:T(8,128)S(1)}, f32[1,4,40,256]{3,2,1,0:T(8,128)S(1)}, u32[]{:S(2)}, u32[]{:S(2)}) collective-permute-start(f32[1,4,40,256]{3,2,1,0:T(8,128)S(1)} %split.4), channel_id=1, source_target_pairs={{0,4},{4,0},{8,12},{12,8},{16,20},{20,16},{24,28},{28,24},{1,5},{5... | collective-permute-start | bytes 491528 | tf_op jit(solution)/shard_map/ppermute | solution.py:235
  40.2 4.3 %collective-permute-start.6 = (f32[1,4,40,256]{3,2,1,0:T(8,128)S(1)}, f32[1,4,40,256]{3,2,1,0:T(8,128)S(1)}, u32[]{:S(2)}, u32[]{:S(2)}) collective-permute-start(f32[1,4,40,256]{3,2,1,0:T(8,128)S(1)} %get-tuple-element.28), channel_id=1, source_target_pairs={{0,4},{4,0},{8,12},{12,8},{16,20},{20,16},{24,28},{28,24},{1,5},{5... | collective-permute-start | bytes 491528 | tf_op jit(solution)/shard_map/ppermute | solution.py:235
  40.3 5.0 %collective-permute-start.7 = (f32[1,4,40,256]{3,2,1,0:T(8,128)S(1)}, f32[1,4,40,256]{3,2,1,0:T(8,128)S(1)}, u32[]{:S(2)}, u32[]{:S(2)}) collective-permute-start(f32[1,4,40,256]{3,2,1,0:T(8,128)S(1)} %get-tuple-element.29), channel_id=1, source_target_pairs={{0,4},{4,0},{8,12},{12,8},{16,20},{20,16},{24,28},{28,24},{1,5},{5... | collective-permute-start | bytes 491528 | tf_op jit(solution)/shard_map/ppermute | solution.py:235
  40.8 4.5 %collective-permute-start.8 = (f32[1,4,40,256]{3,2,1,0:T(8,128)S(1)}, f32[1,4,40,256]{3,2,1,0:T(8,128)S(1)}, u32[]{:S(2)}, u32[]{:S(2)}) collective-permute-start(f32[1,4,40,256]{3,2,1,0:T(8,128)S(1)} %get-tuple-element.30), channel_id=1, source_target_pairs={{0,4},{4,0},{8,12},{12,8},{16,20},{20,16},{24,28},{28,24},{1,5},{5... | collective-permute-start | bytes 491528 | tf_op jit(solution)/shard_map/ppermute | solution.py:235
  40.9 9.6 %collective-permute-start.16 = (f32[2,4,24,256]{3,2,1,0:T(8,128)S(1)}, f32[2,4,24,256]{3,2,1,0:T(8,128)S(1)}, u32[]{:S(2)}, u32[]{:S(2)}) collective-permute-start(f32[2,4,24,256]{3,2,1,0:T(8,128)S(1)} %get-tuple-element.31), channel_id=1, source_target_pairs={{0,8},{4,12},{8,16},{12,20},{16,24},{20,28},{24,0},{28,4},{1,9},{5... | collective-permute-start | bytes 589832 | tf_op jit(solution)/shard_map/ppermute | solution.py:238
  42.9 16.0 %collective-permute-start.17 = (f32[2,4,24,256]{3,2,1,0:T(8,128)S(1)}, f32[2,4,24,256]{3,2,1,0:T(8,128)S(1)}, u32[]{:S(2)}, u32[]{:S(2)}) collective-permute-start(f32[2,4,24,256]{3,2,1,0:T(8,128)S(1)} %get-tuple-element.32), channel_id=1, source_target_pairs={{0,16},{4,20},{8,24},{12,28},{16,0},{20,4},{24,8},{28,12},{1,17},{... | collective-permute-start | bytes 589832 | tf_op jit(solution)/shard_map/ppermute | solution.py:238
  44.5 14.4 %collective-permute-start.18 = (f32[2,4,24,256]{3,2,1,0:T(8,128)S(1)}, f32[2,4,24,256]{3,2,1,0:T(8,128)S(1)}, u32[]{:S(2)}, u32[]{:S(2)}) collective-permute-start(f32[2,4,24,256]{3,2,1,0:T(8,128)S(1)} %get-tuple-element.33), channel_id=1, source_target_pairs={{0,24},{4,28},{8,0},{12,4},{16,8},{20,12},{24,16},{28,20},{1,25},{... | collective-permute-start | bytes 589832 | tf_op jit(solution)/shard_map/ppermute | solution.py:238
  46.6 21.3 %collective-permute-start.12 = (f32[3,40,256]{2,1,0:T(8,128)S(1)}, f32[3,40,256]{2,1,0:T(8,128)S(1)}, u32[]{:S(2)}, u32[]{:S(2)}) collective-permute-start(f32[3,40,256]{2,1,0:T(8,128)S(1)} %composite.2.refs_1_), channel_id=1, source_target_pairs={{0,16},{4,20},{8,24},{12,28},{16,0},{20,4},{24,8},{28,12},{1,17},{... | collective-permute-start | bytes 368648 | tf_op jit(solution)/shard_map/ppermute | solution.py:304
  48.1 20.5 %collective-permute-start.10 = (f32[3,40,256]{2,1,0:T(8,128)S(1)}, f32[3,40,256]{2,1,0:T(8,128)S(1)}, u32[]{:S(2)}, u32[]{:S(2)}) collective-permute-start(f32[3,40,256]{2,1,0:T(8,128)S(1)} %composite.2.refs_1_), channel_id=1, source_target_pairs={{0,8},{4,12},{8,0},{12,4},{16,24},{20,28},{24,16},{28,20},{1,9},{5... | collective-permute-start | bytes 368648 | tf_op jit(solution)/shard_map/ppermute | solution.py:304
  50.5 18.1 %collective-permute-start.19 = (f32[1,4,24,256]{3,2,1,0:T(8,128)S(1)}, f32[1,4,24,256]{3,2,1,0:T(8,128)S(1)}, u32[]{:S(2)}, u32[]{:S(2)}) collective-permute-start(f32[1,4,24,256]{3,2,1,0:T(8,128)S(1)} %split.6), channel_id=1, source_target_pairs={{0,4},{4,0},{8,12},{12,8},{16,20},{20,16},{24,28},{28,24},{1,5},{5... | collective-permute-start | bytes 294920 | tf_op jit(solution)/shard_map/ppermute | solution.py:235
  68.6 5.9 %collective-permute-start.14 = (f32[3,40,256]{2,1,0:T(8,128)S(1)}, f32[3,40,256]{2,1,0:T(8,128)S(1)}, u32[]{:S(2)}, u32[]{:S(2)}) collective-permute-start(f32[3,40,256]{2,1,0:T(8,128)S(1)} %collective-permute-done.12.refs_3_.refs_5_), channel_id=1, source_target_pairs={{0,8},{4,12},{8,0},{12,4},{16,24},{20,28},{24,16},{28,20},{1,9},{5... | collective-permute-start | bytes 368648 | tf_op jit(solution)/shard_map/ppermute | solution.py:304
  69.3 5.2 %collective-permute-start.13 = (f32[3,40,256]{2,1,0:T(8,128)S(1)}, f32[3,40,256]{2,1,0:T(8,128)S(1)}, u32[]{:S(2)}, u32[]{:S(2)}) collective-permute-start(f32[3,40,256]{2,1,0:T(8,128)S(1)} %collective-permute-done.12.refs_3_.refs_5_), channel_id=1, source_target_pairs={{0,4},{4,0},{8,12},{12,8},{16,20},{20,16},{24,28},{28,24},{1,5},{5... | collective-permute-start | bytes 368648 | tf_op jit(solution)/shard_map/ppermute | solution.py:235
  69.5 5.1 %collective-permute-start.11 = (f32[3,40,256]{2,1,0:T(8,128)S(1)}, f32[3,40,256]{2,1,0:T(8,128)S(1)}, u32[]{:S(2)}, u32[]{:S(2)}) collective-permute-start(f32[3,40,256]{2,1,0:T(8,128)S(1)} %collective-permute-done.10.refs_3_), channel_id=1, source_target_pairs={{0,4},{4,0},{8,12},{12,8},{16,20},{20,16},{24,28},{28,24},{1,5},{5... | collective-permute-start | bytes 368648 | tf_op jit(solution)/shard_map/ppermute | solution.py:235
  71.1 4.8 %collective-permute-start.28 = (f32[3,24,256]{2,1,0:T(8,128)S(1)}, f32[3,24,256]{2,1,0:T(8,128)S(1)}, u32[]{:S(2)}, u32[]{:S(2)}) collective-permute-start(f32[3,24,256]{2,1,0:T(8,128)S(1)} %composite.3.refs_9_), channel_id=1, source_target_pairs={{0,24},{4,28},{8,0},{12,4},{16,8},{20,12},{24,16},{28,20},{1,25},{... | collective-permute-start | bytes 221192 | tf_op jit(solution)/shard_map/ppermute | solution.py:238
  72.0 9.5 %collective-permute-start.26 = (f32[3,24,256]{2,1,0:T(8,128)S(1)}, f32[3,24,256]{2,1,0:T(8,128)S(1)}, u32[]{:S(2)}, u32[]{:S(2)}) collective-permute-start(f32[3,24,256]{2,1,0:T(8,128)S(1)} %composite.3.refs_9_), channel_id=1, source_target_pairs={{0,16},{4,20},{8,24},{12,28},{16,0},{20,4},{24,8},{28,12},{1,17},{... | collective-permute-start | bytes 221192 | tf_op jit(solution)/shard_map/ppermute | solution.py:238
  74.5 7.1 %collective-permute-start.24 = (f32[3,24,256]{2,1,0:T(8,128)S(1)}, f32[3,24,256]{2,1,0:T(8,128)S(1)}, u32[]{:S(2)}, u32[]{:S(2)}) collective-permute-start(f32[3,24,256]{2,1,0:T(8,128)S(1)} %composite.3.refs_9_), channel_id=1, source_target_pairs={{0,8},{4,12},{8,16},{12,20},{16,24},{20,28},{24,0},{28,4},{1,9},{5... | collective-permute-start | bytes 221192 | tf_op jit(solution)/shard_map/ppermute | solution.py:238
  74.5 8.4 %collective-permute-start.15 = (f32[3,40,256]{2,1,0:T(8,128)S(1)}, f32[3,40,256]{2,1,0:T(8,128)S(1)}, u32[]{:S(2)}, u32[]{:S(2)}) collective-permute-start(f32[3,40,256]{2,1,0:T(8,128)S(1)} %collective-permute-done.14.refs_7_), channel_id=1, source_target_pairs={{0,4},{4,0},{8,12},{12,8},{16,20},{20,16},{24,28},{28,24},{1,5},{5... | collective-permute-start | bytes 368648 | tf_op jit(solution)/shard_map/ppermute | solution.py:235
  74.6 7.5 %collective-permute-start.23 = (f32[3,24,256]{2,1,0:T(8,128)S(1)}, f32[3,24,256]{2,1,0:T(8,128)S(1)}, u32[]{:S(2)}, u32[]{:S(2)}) collective-permute-start(f32[3,24,256]{2,1,0:T(8,128)S(1)} %composite.3.refs_9_), channel_id=1, source_target_pairs={{0,4},{4,0},{8,12},{12,8},{16,20},{20,16},{24,28},{28,24},{1,5},{5... | collective-permute-start | bytes 221192 | tf_op jit(solution)/shard_map/ppermute | solution.py:235
  75.8 6.2 %collective-permute-start.29 = (f32[3,24,256]{2,1,0:T(8,128)S(1)}, f32[3,24,256]{2,1,0:T(8,128)S(1)}, u32[]{:S(2)}, u32[]{:S(2)}) collective-permute-start(f32[3,24,256]{2,1,0:T(8,128)S(1)} %collective-permute-done.28.refs_15_), channel_id=1, source_target_pairs={{0,4},{4,0},{8,12},{12,8},{16,20},{20,16},{24,28},{28,24},{1,5},{5... | collective-permute-start | bytes 221192 | tf_op jit(solution)/shard_map/ppermute | solution.py:235
  (9 other events, 37.3 us)

commit v5 on v4

--- a/solution.py
+++ b/solution.py
@@ -50,9 +50,12 @@
         copy.wait()
 
 
-def render_kernel(runs, tiles, chips, offsets, scale, where_ref, transfer_ref, light_ref, field_ref, *refs):
-    out_refs, (padded, sem) = refs[-2 - len(offsets) : -2], refs[-2:]
-    edges = list(refs[: -2 - len(offsets)])
+def render_kernel(runs, tiles, chips, offsets, scale, given, where_ref, transfer_ref, light_ref, field_ref, *refs):
+    if given:
+        edges, padded, out_refs, sem = [], refs[0], refs[1:-1], refs[-1]
+    else:
+        out_refs, (padded, sem) = refs[-2 - len(offsets) : -2], refs[-2:]
+        edges = list(refs[: -2 - len(offsets)])
     planes, _, columns = field_ref.shape
     part = out_refs[0].shape[3]
     my_chip, my_core = where_ref[0], where_ref[1]
@@ -70,12 +73,13 @@
         before = edges.pop(0) if first == 0 else None
         behind = edges.pop(0) if first + number == tiles else None
         layout.append((first, number, low, high, slot, written, before, behind))
-        for tile in range(low, high):
+        for tile in range(low, high) if not given else ():
             tile_copy(tile, slot + tile - low).start()
         slot, written = slot + high - low, written + number
-    rim = jnp.zeros((planes, padded.shape[1], LANE), jnp.float32)
-    padded[:, :, :LANE] = rim
-    padded[:, :, LANE + columns :] = rim
+    if not given:
+        rim = jnp.zeros((planes, padded.shape[1], LANE), jnp.float32)
+        padded[:, :, :LANE] = rim
+        padded[:, :, LANE + columns :] = rim
 
     light = [0.5 * light_ref[i] for i in range(3)]
     slope = [0.5 * transfer_ref[0, c] for c in range(3)]
@@ -135,7 +139,7 @@
     for step, (k, out_ref) in enumerate(zip(offsets, out_refs)):
         chip = lax.rem(my_chip + k, chips)
         for first, number, low, high, slot, written, before, behind in layout:
-            if step == 0:
+            if step == 0 and not given:
                 for tile in range(low, min(first + 1, high)):
                     tile_copy(tile, slot + tile - low).wait()
 
@@ -143,7 +147,7 @@
                 first, low, high, slot, written, before, behind = run
                 here = slot + first - low + index
 
-                if step == 0:
+                if step == 0 and not given:
 
                     @pl.when(first + index + 1 < high)
                     def _():
@@ -154,6 +158,10 @@
                 return carry
 
             lax.fori_loop(0, number, one_tile, 0)
+
+
+def relay_kernel(*refs):
+    del refs
 
 
 def split_kernel(*refs):
@@ -237,20 +245,18 @@
     def send(value, k):
         return lax.ppermute(value, "wide", [(i, (i + k * CORES) % wide) for i in range(wide)])
 
-    def render(runs, offsets, edges, events):
+    def render(runs, offsets, edges, events, keep=False, given=()):
         slots = sum(min(first + number + 1, tiles) - max(first - 1, 0) for first, number in runs)
         block = pltpu.VMEM((CORES, 4, tiles_of(runs) * SUB, part), jnp.float32)
+        buffer = pltpu.VMEM((planes, slots * SUB, columns + 2 * LANE), jnp.float32)
         return call(
-            functools.partial(render_kernel, runs, tiles, chips, offsets, scale),
-            [where, transfer, light_dir, field, *edges],
-            [smem] * 3 + [hbm] + [vmem] * len(edges),
+            functools.partial(render_kernel, runs, tiles, chips, offsets, scale, len(given)),
+            [where, transfer, light_dir, field, *edges, *given],
+            [smem] * 3 + [hbm] + [vmem] * (len(edges) + len(given)),
             events,
-            out_shape=[block] * len(offsets),
-            out_specs=[vmem] * len(offsets),
-            scratch_shapes=[
-                pltpu.VMEM((planes, slots * SUB, columns + 2 * LANE), jnp.float32),
-                pltpu.SemaphoreType.DMA((slots,)),
-            ],
+            out_shape=[block] * len(offsets) + [buffer] * keep,
+            out_specs=[vmem] * (len(offsets) + keep),
+            scratch_shapes=[buffer] * (not keep and not given) + [pltpu.SemaphoreType.DMA((slots,))],
             cost_estimate=lasting(0.6 * len(offsets) * tiles_of(runs)),
             name="render",
         )
@@ -271,8 +277,8 @@
         up = [(i, i + 1) for i in range(narrow - 1)]
         return lax.ppermute(last_row, "narrow", up), lax.ppermute(first_row, "narrow", [(j, i) for i, j in up])
 
-    def other_halves(arrays, events):
-        halves = call(
+    def split(arrays, events):
+        return call(
             split_kernel,
             arrays,
             [vmem] * len(arrays),
@@ -282,6 +288,11 @@
             cost_estimate=lasting(0.3),
             name="split",
         )
+
+    def other_halves(arrays, events, first):
+        halves = split(arrays[:first], events)
+        if arrays[first:]:
+            halves += split(arrays[first:], halves[:1])
         return [swap(value) for value in halves]
 
     def composite(own, other, runs):
@@ -295,14 +306,34 @@
             name="composite",
         )
 
+    def across(value, m):
+        return lax.ppermute(value, "wide", [(i, i ^ (m * CORES)) for i in range(wide)])
+
     def gather_by_halves(tile):
-        tiles_by = {0: tile}
-        bit = chips // 2
+        tiles_by, bit = {0: tile}, chips // 2
         while bit:
-            for m in list(tiles_by):
-                pairs = [(i, i ^ (bit * CORES)) for i in range(wide)]
-                tiles_by[m ^ bit] = lax.ppermute(tiles_by[m], "wide", pairs)
+            tiles_by[bit] = across(tile, bit)
             bit //= 2
+        return tiles_by
+
+    def gather_rest(tiles_by, events):
+        bits = sorted(tiles_by)[1:]
+        held = call(
+            relay_kernel,
+            [tiles_by[bit] for bit in bits],
+            [vmem] * len(bits),
+            events,
+            out_shape=[pltpu.VMEM(tiles_by[0].shape, jnp.float32)] * len(bits),
+            out_specs=[vmem] * len(bits),
+            input_output_aliases={i: i for i in range(len(bits))},
+            cost_estimate=lasting(0.1),
+            name="relay",
+        )
+        tiles_by = {0: tiles_by[0], **dict(zip(bits, held))}
+        for m in range(1, chips):
+            low = m & -m
+            if m not in tiles_by:
+                tiles_by[m] = across(tiles_by[m - low], low)
         order = sorted(tiles_by)
         return [tiles_by[m] for m in order], lambda chip: [jnp.bitwise_xor(chip, m) for m in order]
 
@@ -316,19 +347,25 @@
         if i == len(chunks) - 1:
             edges = edge_rows(last)
         blocks = {}
-        for offsets in early if i == 0 else [tuple(range(chips))]:
-            values = render(runs, offsets, edges, last)
+        given = ()
+        for step, offsets in enumerate(early if i == 0 else [tuple(range(chips))]):
+            keep = i == 0 and step == 0
+            values = render(runs, offsets, edges, last, keep, given)
+            given = values[len(offsets) :] if keep else given
             blocks.update(zip(offsets, values))
             last = list(values[:1])
-        near += other_halves([blocks[0]], [])
+        near += other_halves([blocks[0]], [], 1)
         sent.append([blocks[0]] + [send(blocks[k], k) for k in range(1, chips)])
 
+    def finish(i, events):
+        count = chips // 2 if i == 0 else chips - 1
+        other = [near[i]] + other_halves(sent[i][1:], events, count)
+        return composite(sent[i], other, chunks[i])
+
+    partial = gather_by_halves(finish(0, last))
+    tile = finish(1, [partial[1]])
     groups, finished = [], []
-    for runs, own, first, gather in zip(chunks, sent, near, (gather_by_halves, gather_directly)):
-        other = [first] + other_halves(own[1:], last)
-        tile = composite(own, other, runs)
-        values, chip_of = gather(tile)
-        last = values[2:3]
+    for runs, (values, chip_of) in zip(chunks, (gather_rest(partial, [tile]), gather_directly(tile))):
         groups.append((runs, chip_of))
         for value in values:
             finished += [value, swap(value)]

time: 85.1 us -> 82.4 us (0.968)
  waiting for transfers between devices: 32.3 us -> 29.5 us
  starting transfers between devices: 25.6 us -> 27.7 us
  Pallas kernels: 25.3 us -> 23.4 us
    ppermute x3, waiting for transfers between devices: 8.95 us -> 6.47 us  [across(): lax.ppermute(value, 'wide', [(i, i ^ m * CORES) for i in range(wide)])]
    pallas_call x11 -> x13, Pallas kernels: 25.3 us -> 23.4 us  [call(): pl.pallas_call(with_events, in_specs=list(specs) + [pl.BlockSpec(memory_s...]
    ppermute x9, starting transfers between devices: 15 us -> 16.7 us  [send(): lax.ppermute(value, 'wide', [(i, (i + k * CORES) % wide) for i in range(w...]
    ppermute x9, waiting for transfers between devices: 16.1 us -> 15.1 us  [send(): lax.ppermute(value, 'wide', [(i, (i + k * CORES) % wide) for i in range(w...]
  transfers between devices with their start and end apart: 30 -> 30, of which waited for: 11 -> 15; matrix products, arithmetic and copies ran while one was open for 0% -> 0% of each run, Pallas kernels for 20% -> 18%
where the time goes in v5:
time: 82.4 us; the launch traced here: 82.2 us
  waiting for transfers between devices  29.5 us (36%)
  starting transfers between devices  27.7 us (34%)
  Pallas kernels  23.4 us (28%)
  local copies, waits for them, and re-layouts  1.34 us (2%)
    pallas_call x13, Pallas kernels, call(): pl.pallas_call(with_events, in_specs=list(specs) + [pl.BlockSpec(memory_s...  23.4 us
    ppermute x9, starting transfers between devices, send(): lax.ppermute(value, 'wide', [(i, (i + k * CORES) % wide) for i in range(w...  16.7 us
    ppermute x9, waiting for transfers between devices, send(): lax.ppermute(value, 'wide', [(i, (i + k * CORES) % wide) for i in range(w...  15.1 us
    ppermute x3, waiting for transfers between devices, across(): lax.ppermute(value, 'wide', [(i, i ^ m * CORES) for i in range(wide)])  6.47 us
    ppermute x1, waiting for transfers between devices, edge_rows(): lax.ppermute(first_row, 'narrow', [(j, i) for i, j in up])  4.72 us
    ppermute x3, starting transfers between devices, across(): lax.ppermute(value, 'wide', [(i, i ^ m * CORES) for i in range(wide)])  3.46 us
    ppermute x1, starting transfers between devices, edge_rows(): lax.ppermute(last_row, 'narrow', up)  3.4 us
    ppermute x16, starting transfers between devices, swap(): return lax.ppermute(value, 'wide', [(i, i ^ 1) for i in range(wide)])  2.9 us
  transfers between devices with their start and end apart: 30, of which 15 were waited for; matrix products, arithmetic and copies ran while one was open for 0% of the time, Pallas kernels for 18%

profile of v5, /device:TPU:0, one launch (start us, length us, event | category | flops | bytes accessed | tf_op | source)
XLA Modules:
  0.0 82.2 jit_solution(12819067292179167544)
XLA Ops:
  1.4 6.3 %render.3 = (f32[2,4,40,256]{3,2,1,0:T(8,128)S(1)}, f32[2,4,40,256]{3,2,1,0:T(8,128)S(1)}, f32[16,56,2304]{2,1,0:T(8,128)S(1)}) custom-call(s32[2]{0:T(128)S(1)} %pad_add_fusion.refs_0_, f32[2,3]{1,0:T(2,128)S(1)} %copy-done, f32[3]{0:T(128)S(1)} %copy-done.1, f32[16,64,2048]{2,1,0:T(8,128)} %refs_3_.5), custom_call_target="tpu_custom_call" | custom-call | bytes 22140000 | tf_op jit(solution)/shard_map/render/pallas_call | solution.py:25
  7.7 3.1 %collective-permute-start = (f32[2,4,40,256]{3,2,1,0:T(8,128)S(1)}, f32[2,4,40,256]{3,2,1,0:T(8,128)S(1)}, u32[]{:S(2)}, u32[]{:S(2)}) collective-permute-start(f32[2,4,40,256]{3,2,1,0:T(8,128)S(1)} %get-tuple-element.26), channel_id=1, source_target_pairs={{0,8},{4,12},{8,16},{12,20},{16,24},{20,28},{24,0},{28,4},{1,9},{5... | collective-permute-start | bytes 983048 | tf_op jit(solution)/shard_map/ppermute | solution.py:246
  10.8 2.6 %collective-permute-start.1 = (f32[2,4,40,256]{3,2,1,0:T(8,128)S(1)}, f32[2,4,40,256]{3,2,1,0:T(8,128)S(1)}, u32[]{:S(2)}, u32[]{:S(2)}) collective-permute-start(f32[2,4,40,256]{3,2,1,0:T(8,128)S(1)} %get-tuple-element.24.refs_5_), channel_id=1, source_target_pairs={{0,16},{4,20},{8,24},{12,28},{16,0},{20,4},{24,8},{28,12},{1,17},{... | collective-permute-start | bytes 983048 | tf_op jit(solution)/shard_map/ppermute | solution.py:246
  13.4 4.5 %render.4 = (f32[2,4,40,256]{3,2,1,0:T(8,128)S(1)}, f32[2,4,40,256]{3,2,1,0:T(8,128)S(1)}) custom-call(s32[2]{0:T(128)S(1)} %pad_add_fusion.refs_0_, f32[2,3]{1,0:T(2,128)S(1)} %copy-done, f32[3]{0:T(128)S(1)} %copy-done.1, f32[16,64,2048]{2,1,0:T(8,128)} %refs_3_.5, f32[16,56,2304]{2,1,0:T(8,128)S(1)} %get-tuple-element.23.refs_4_, ...), custom_call_target="tpu_custom_call" | custom-call | bytes 22140000 | tf_op jit(solution)/shard_map/render/pallas_call | solution.py:25
  17.9 1.4 %collective-permute-start.2 = (f32[2,4,40,256]{3,2,1,0:T(8,128)S(1)}, f32[2,4,40,256]{3,2,1,0:T(8,128)S(1)}, u32[]{:S(2)}, u32[]{:S(2)}) collective-permute-start(f32[2,4,40,256]{3,2,1,0:T(8,128)S(1)} %get-tuple-element.27.refs_1_.refs_6_), channel_id=1, source_target_pairs={{0,24},{4,28},{8,0},{12,4},{16,8},{20,12},{24,16},{28,20},{1,25},{... | collective-permute-start | bytes 983048 | tf_op jit(solution)/shard_map/ppermute | solution.py:246
  20.3 3.4 %collective-permute-start.4 = (f32[16,1,2048]{2,1,0:T(1,128)S(1)}, f32[16,1,2048]{2,1,0:T(1,128)S(1)}, u32[]{:S(2)}, u32[]{:S(2)}) collective-permute-start(f32[16,1,2048]{2,1,0:T(1,128)S(1)} %get-tuple-element.28), channel_id=1, source_target_pairs={{0,1},{1,2},{2,3},{4,5},{5,6},{6,7},{8,9},{9,10},{10,11},{12,13},{... | collective-permute-start | bytes 393224 | tf_op jit(solution)/shard_map/ppermute | solution.py:278
  23.7 1.3 %collective-permute-start.5 = (f32[16,1,2048]{2,1,0:T(1,128)S(1)}, f32[16,1,2048]{2,1,0:T(1,128)S(1)}, u32[]{:S(2)}, u32[]{:S(2)}) collective-permute-start(f32[16,1,2048]{2,1,0:T(1,128)S(1)} %get-tuple-element.29), channel_id=1, source_target_pairs={{1,0},{2,1},{3,2},{5,4},{6,5},{7,6},{9,8},{10,9},{11,10},{13,12},{... | collective-permute-start | bytes 393224 | tf_op jit(solution)/shard_map/ppermute | solution.py:278
  25.0 1.2 %collective-permute-done.4.refs_4_ = f32[16,1,2048]{2,1,0:T(1,128)S(1)} collective-permute-done((f32[16,1,2048]{2,1,0:T(1,128)S(1)}, f32[16,1,2048]{2,1,0:T(1,128)S(1)}, u32[]{:S(2)}, u32[]{:S(2)}) %collective-permute-start.4) | collective-permute-done | bytes 131104 | tf_op jit(solution)/shard_map/ppermute | solution.py:278
  26.2 4.7 %collective-permute-done.5.refs_5_ = f32[16,1,2048]{2,1,0:T(1,128)S(1)} collective-permute-done((f32[16,1,2048]{2,1,0:T(1,128)S(1)}, f32[16,1,2048]{2,1,0:T(1,128)S(1)}, u32[]{:S(2)}, u32[]{:S(2)}) %collective-permute-start.5) | collective-permute-done | bytes 131104 | tf_op jit(solution)/shard_map/ppermute | solution.py:278
  30.9 7.3 %render.5 = (f32[2,4,24,256]{3,2,1,0:T(8,128)S(1)}, f32[2,4,24,256]{3,2,1,0:T(8,128)S(1)}, f32[2,4,24,256]{3,2,1,0:T(8,128)S(1)}, f32[2,4,24,256]{3,2,1,0:T(8,128)S(1)}) custom-call(s32[2]{0:T(128)S(1)} %pad_add_fusion.refs_0_, f32[2,3]{1,0:T(2,128)S(1)} %copy-done, f32[3]{0:T(128)S(1)} %copy-done.1, f32[16,64,2048]{2,1,0:T(8,128)} %refs_3_.5, ...), custom_call_target="tpu_custom_call" | custom-call | bytes 26568000 | tf_op jit(solution)/shard_map/render/pallas_call | solution.py:25
  39.0 3.9 %collective-permute-start.12 = (f32[2,4,24,256]{3,2,1,0:T(8,128)S(1)}, f32[2,4,24,256]{3,2,1,0:T(8,128)S(1)}, u32[]{:S(2)}, u32[]{:S(2)}) collective-permute-start(f32[2,4,24,256]{3,2,1,0:T(8,128)S(1)} %get-tuple-element.33), channel_id=1, source_target_pairs={{0,8},{4,12},{8,16},{12,20},{16,24},{20,28},{24,0},{28,4},{1,9},{5... | collective-permute-start | bytes 589832 | tf_op jit(solution)/shard_map/ppermute | solution.py:246
  42.9 1.7 %collective-permute-start.13 = (f32[2,4,24,256]{3,2,1,0:T(8,128)S(1)}, f32[2,4,24,256]{3,2,1,0:T(8,128)S(1)}, u32[]{:S(2)}, u32[]{:S(2)}) collective-permute-start(f32[2,4,24,256]{3,2,1,0:T(8,128)S(1)} %get-tuple-element.34), channel_id=1, source_target_pairs={{0,16},{4,20},{8,24},{12,28},{16,0},{20,4},{24,8},{28,12},{1,17},{... | collective-permute-start | bytes 589832 | tf_op jit(solution)/shard_map/ppermute | solution.py:246
  45.2 1.3 %composite.2.refs_1_ = f32[3,40,256]{2,1,0:T(8,128)S(1)} custom-call(s32[2]{0:T(128)S(1)} %pad_add_fusion.refs_0_, s32[8]{0:T(128)S(1)} %copy-done.2, f32[2,4,40,256]{3,2,1,0:T(8,128)S(1)} %get-tuple-element.25.refs_0_.refs_2_, f32[2,4,40,256]{3,2,1,0:T(8,128)S(1)} %collective-permute-done.refs_0_.refs_3_, ...), custom_call_target="tpu_custom_call" | custom-call | bytes 3690000 | tf_op jit(solution)/shard_map/composite/pallas_call | solution.py:25
  46.6 1.4 %collective-permute-start.10 = (f32[3,40,256]{2,1,0:T(8,128)S(1)}, f32[3,40,256]{2,1,0:T(8,128)S(1)}, u32[]{:S(2)}, u32[]{:S(2)}) collective-permute-start(f32[3,40,256]{2,1,0:T(8,128)S(1)} %composite.2.refs_1_), channel_id=1, source_target_pairs={{0,8},{4,12},{8,0},{12,4},{16,24},{20,28},{24,16},{28,20},{1,9},{5... | collective-permute-start | bytes 368648 | tf_op jit(solution)/shard_map/ppermute | solution.py:310
  48.0 1.8 %collective-permute-done.12.refs_0_.refs_3_ = f32[2,4,24,256]{3,2,1,0:T(8,128)S(1)} collective-permute-done((f32[2,4,24,256]{3,2,1,0:T(8,128)S(1)}, f32[2,4,24,256]{3,2,1,0:T(8,128)S(1)}, u32[]{:S(2)}, u32[]{:S(2)}) %collective-permute-start.12) | collective-permute-done | bytes 196640 | tf_op jit(solution)/shard_map/ppermute | solution.py:246
  49.8 1.0 %collective-permute-start.11 = (f32[3,40,256]{2,1,0:T(8,128)S(1)}, f32[3,40,256]{2,1,0:T(8,128)S(1)}, u32[]{:S(2)}, u32[]{:S(2)}) collective-permute-start(f32[3,40,256]{2,1,0:T(8,128)S(1)} %composite.2.refs_1_), channel_id=1, source_target_pairs={{0,16},{4,20},{8,24},{12,28},{16,0},{20,4},{24,8},{28,12},{1,17},{... | collective-permute-start | bytes 368648 | tf_op jit(solution)/shard_map/ppermute | solution.py:310
  50.9 7.1 %collective-permute-done.13.refs_1_.refs_4_ = f32[2,4,24,256]{3,2,1,0:T(8,128)S(1)} collective-permute-done((f32[2,4,24,256]{3,2,1,0:T(8,128)S(1)}, f32[2,4,24,256]{3,2,1,0:T(8,128)S(1)}, u32[]{:S(2)}, u32[]{:S(2)}) %collective-permute-start.13) | collective-permute-done | bytes 196640 | tf_op jit(solution)/shard_map/ppermute | solution.py:246
  58.0 2.5 %collective-permute-done.10.refs_3_.refs_0_ = f32[3,40,256]{2,1,0:T(8,128)S(1)} collective-permute-done((f32[3,40,256]{2,1,0:T(8,128)S(1)}, f32[3,40,256]{2,1,0:T(8,128)S(1)}, u32[]{:S(2)}, u32[]{:S(2)}) %collective-permute-start.10) | collective-permute-done | bytes 122912 | tf_op jit(solution)/shard_map/ppermute | solution.py:310
  62.4 1.0 %composite.3.refs_2_.refs_9_ = f32[3,24,256]{2,1,0:T(8,128)S(1)} custom-call(s32[2]{0:T(128)S(1)} %pad_add_fusion.refs_0_, s32[8]{0:T(128)S(1)} %copy-done.2, f32[2,4,24,256]{3,2,1,0:T(8,128)S(1)} %get-tuple-element.30.refs_2_.refs_0_, f32[2,4,24,256]{3,2,1,0:T(8,128)S(1)} %collective-permute-done.12.refs_0_.refs_3_, ...), custom_call_target="tpu_custom_call" | custom-call | bytes 3690000 | tf_op jit(solution)/shard_map/composite/pallas_call | solution.py:25
  63.4 4.0 %collective-permute-done.11.refs_1_ = f32[3,40,256]{2,1,0:T(8,128)S(1)} collective-permute-done((f32[3,40,256]{2,1,0:T(8,128)S(1)}, f32[3,40,256]{2,1,0:T(8,128)S(1)}, u32[]{:S(2)}, u32[]{:S(2)}) %collective-permute-start.11) | collective-permute-done | bytes 122912 | tf_op jit(solution)/shard_map/ppermute | solution.py:310
  69.3 1.6 %collective-permute-start.26 = (f32[3,24,256]{2,1,0:T(8,128)S(1)}, f32[3,24,256]{2,1,0:T(8,128)S(1)}, u32[]{:S(2)}, u32[]{:S(2)}) collective-permute-start(f32[3,24,256]{2,1,0:T(8,128)S(1)} %composite.3.refs_2_.refs_9_), channel_id=1, source_target_pairs={{0,16},{4,20},{8,24},{12,28},{16,0},{20,4},{24,8},{28,12},{1,17},{... | collective-permute-start | bytes 221192 | tf_op jit(solution)/shard_map/ppermute | solution.py:246
  71.9 3.8 %collective-permute-done.28.refs_15_ = f32[3,24,256]{2,1,0:T(8,128)S(1)} collective-permute-done((f32[3,24,256]{2,1,0:T(8,128)S(1)}, f32[3,24,256]{2,1,0:T(8,128)S(1)}, u32[]{:S(2)}, u32[]{:S(2)}) %collective-permute-start.28) | collective-permute-done | bytes 73760 | tf_op jit(solution)/shard_map/ppermute | solution.py:246
  75.6 2.4 %collective-permute-done.26.refs_13_ = f32[3,24,256]{2,1,0:T(8,128)S(1)} collective-permute-done((f32[3,24,256]{2,1,0:T(8,128)S(1)}, f32[3,24,256]{2,1,0:T(8,128)S(1)}, u32[]{:S(2)}, u32[]{:S(2)}) %collective-permute-start.26) | collective-permute-done | bytes 73760 | tf_op jit(solution)/shard_map/ppermute | solution.py:246
  80.3 1.9 %place.1 = f32[3,64,2048]{2,1,0:T(8,128)} custom-call(s32[2]{0:T(128)S(1)} %pad_add_fusion.refs_0_, f32[3,40,256]{2,1,0:T(8,128)S(1)} %composite.2.refs_1_, f32[3,40,256]{2,1,0:T(8,128)S(1)} %collective-permute-done.9.refs_2_, f32[3,40,256]{2,1,0:T(8,128)S(1)} %get-tuple-element.39.refs_3_, f32[3,40,256]{2,1,0:T(8,128)S(1)} %collective-permute-done.19.refs_4_, ...), custom_call_target="tpu_custom_call" | custom-call | bytes 7380000 | tf_op jit(solution)/shard_map/place/pallas_call | solution.py:25
  (56 shorter events, 10.9 us)
Async XLA Ops:
  7.7 30.5 %collective-permute-start = (f32[2,4,40,256]{3,2,1,0:T(8,128)S(1)}, f32[2,4,40,256]{3,2,1,0:T(8,128)S(1)}, u32[]{:S(2)}, u32[]{:S(2)}) collective-permute-start(f32[2,4,40,256]{3,2,1,0:T(8,128)S(1)} %get-tuple-element.26), channel_id=1, source_target_pairs={{0,8},{4,12},{8,16},{12,20},{16,24},{20,28},{24,0},{28,4},{1,9},{5... | collective-permute-start | bytes 983048 | tf_op jit(solution)/shard_map/ppermute | solution.py:246
  10.8 27.4 %collective-permute-start.1 = (f32[2,4,40,256]{3,2,1,0:T(8,128)S(1)}, f32[2,4,40,256]{3,2,1,0:T(8,128)S(1)}, u32[]{:S(2)}, u32[]{:S(2)}) collective-permute-start(f32[2,4,40,256]{3,2,1,0:T(8,128)S(1)} %get-tuple-element.24.refs_5_), channel_id=1, source_target_pairs={{0,16},{4,20},{8,24},{12,28},{16,0},{20,4},{24,8},{28,12},{1,17},{... | collective-permute-start | bytes 983048 | tf_op jit(solution)/shard_map/ppermute | solution.py:246
  17.9 20.4 %collective-permute-start.2 = (f32[2,4,40,256]{3,2,1,0:T(8,128)S(1)}, f32[2,4,40,256]{3,2,1,0:T(8,128)S(1)}, u32[]{:S(2)}, u32[]{:S(2)}) collective-permute-start(f32[2,4,40,256]{3,2,1,0:T(8,128)S(1)} %get-tuple-element.27.refs_1_.refs_6_), channel_id=1, source_target_pairs={{0,24},{4,28},{8,0},{12,4},{16,8},{20,12},{24,16},{28,20},{1,25},{... | collective-permute-start | bytes 983048 | tf_op jit(solution)/shard_map/ppermute | solution.py:246
  20.3 5.9 %collective-permute-start.4 = (f32[16,1,2048]{2,1,0:T(1,128)S(1)}, f32[16,1,2048]{2,1,0:T(1,128)S(1)}, u32[]{:S(2)}, u32[]{:S(2)}) collective-permute-start(f32[16,1,2048]{2,1,0:T(1,128)S(1)} %get-tuple-element.28), channel_id=1, source_target_pairs={{0,1},{1,2},{2,3},{4,5},{5,6},{6,7},{8,9},{9,10},{10,11},{12,13},{... | collective-permute-start | bytes 393224 | tf_op jit(solution)/shard_map/ppermute | solution.py:278
  23.7 7.2 %collective-permute-start.5 = (f32[16,1,2048]{2,1,0:T(1,128)S(1)}, f32[16,1,2048]{2,1,0:T(1,128)S(1)}, u32[]{:S(2)}, u32[]{:S(2)}) collective-permute-start(f32[16,1,2048]{2,1,0:T(1,128)S(1)} %get-tuple-element.29), channel_id=1, source_target_pairs={{1,0},{2,1},{3,2},{5,4},{6,5},{7,6},{9,8},{10,9},{11,10},{13,12},{... | collective-permute-start | bytes 393224 | tf_op jit(solution)/shard_map/ppermute | solution.py:278
  26.2 16.7 %collective-permute-start.3 = (f32[1,4,40,256]{3,2,1,0:T(8,128)S(1)}, f32[1,4,40,256]{3,2,1,0:T(8,128)S(1)}, u32[]{:S(2)}, u32[]{:S(2)}) collective-permute-start(f32[1,4,40,256]{3,2,1,0:T(8,128)S(1)} %split.5), channel_id=1, source_target_pairs={{0,4},{4,0},{8,12},{12,8},{16,20},{20,16},{24,28},{28,24},{1,5},{5... | collective-permute-start | bytes 491528 | tf_op jit(solution)/shard_map/ppermute | solution.py:243
  38.3 6.2 %collective-permute-start.8 = (f32[1,4,40,256]{3,2,1,0:T(8,128)S(1)}, f32[1,4,40,256]{3,2,1,0:T(8,128)S(1)}, u32[]{:S(2)}, u32[]{:S(2)}) collective-permute-start(f32[1,4,40,256]{3,2,1,0:T(8,128)S(1)} %split.7), channel_id=1, source_target_pairs={{0,4},{4,0},{8,12},{12,8},{16,20},{20,16},{24,28},{28,24},{1,5},{5... | collective-permute-start | bytes 491528 | tf_op jit(solution)/shard_map/ppermute | solution.py:243
  38.4 6.8 %collective-permute-start.7 = (f32[1,4,40,256]{3,2,1,0:T(8,128)S(1)}, f32[1,4,40,256]{3,2,1,0:T(8,128)S(1)}, u32[]{:S(2)}, u32[]{:S(2)}) collective-permute-start(f32[1,4,40,256]{3,2,1,0:T(8,128)S(1)} %get-tuple-element.32), channel_id=1, source_target_pairs={{0,4},{4,0},{8,12},{12,8},{16,20},{20,16},{24,28},{28,24},{1,5},{5... | collective-permute-start | bytes 491528 | tf_op jit(solution)/shard_map/ppermute | solution.py:243
  38.9 6.3 %collective-permute-start.6 = (f32[1,4,40,256]{3,2,1,0:T(8,128)S(1)}, f32[1,4,40,256]{3,2,1,0:T(8,128)S(1)}, u32[]{:S(2)}, u32[]{:S(2)}) collective-permute-start(f32[1,4,40,256]{3,2,1,0:T(8,128)S(1)} %get-tuple-element.31.refs_1_), channel_id=1, source_target_pairs={{0,4},{4,0},{8,12},{12,8},{16,20},{20,16},{24,28},{28,24},{1,5},{5... | collective-permute-start | bytes 491528 | tf_op jit(solution)/shard_map/ppermute | solution.py:243
  39.0 10.9 %collective-permute-start.12 = (f32[2,4,24,256]{3,2,1,0:T(8,128)S(1)}, f32[2,4,24,256]{3,2,1,0:T(8,128)S(1)}, u32[]{:S(2)}, u32[]{:S(2)}) collective-permute-start(f32[2,4,24,256]{3,2,1,0:T(8,128)S(1)} %get-tuple-element.33), channel_id=1, source_target_pairs={{0,8},{4,12},{8,16},{12,20},{16,24},{20,28},{24,0},{28,4},{1,9},{5... | collective-permute-start | bytes 589832 | tf_op jit(solution)/shard_map/ppermute | solution.py:246
  42.9 15.2 %collective-permute-start.13 = (f32[2,4,24,256]{3,2,1,0:T(8,128)S(1)}, f32[2,4,24,256]{3,2,1,0:T(8,128)S(1)}, u32[]{:S(2)}, u32[]{:S(2)}) collective-permute-start(f32[2,4,24,256]{3,2,1,0:T(8,128)S(1)} %get-tuple-element.34), channel_id=1, source_target_pairs={{0,16},{4,20},{8,24},{12,28},{16,0},{20,4},{24,8},{28,12},{1,17},{... | collective-permute-start | bytes 589832 | tf_op jit(solution)/shard_map/ppermute | solution.py:246
  44.5 13.5 %collective-permute-start.14 = (f32[2,4,24,256]{3,2,1,0:T(8,128)S(1)}, f32[2,4,24,256]{3,2,1,0:T(8,128)S(1)}, u32[]{:S(2)}, u32[]{:S(2)}) collective-permute-start(f32[2,4,24,256]{3,2,1,0:T(8,128)S(1)} %get-tuple-element.35), channel_id=1, source_target_pairs={{0,24},{4,28},{8,0},{12,4},{16,8},{20,12},{24,16},{28,20},{1,25},{... | collective-permute-start | bytes 589832 | tf_op jit(solution)/shard_map/ppermute | solution.py:246
  46.6 14.0 %collective-permute-start.10 = (f32[3,40,256]{2,1,0:T(8,128)S(1)}, f32[3,40,256]{2,1,0:T(8,128)S(1)}, u32[]{:S(2)}, u32[]{:S(2)}) collective-permute-start(f32[3,40,256]{2,1,0:T(8,128)S(1)} %composite.2.refs_1_), channel_id=1, source_target_pairs={{0,8},{4,12},{8,0},{12,4},{16,24},{20,28},{24,16},{28,20},{1,9},{5... | collective-permute-start | bytes 368648 | tf_op jit(solution)/shard_map/ppermute | solution.py:310
  48.0 13.2 %collective-permute-start.15 = (f32[1,4,24,256]{3,2,1,0:T(8,128)S(1)}, f32[1,4,24,256]{3,2,1,0:T(8,128)S(1)}, u32[]{:S(2)}, u32[]{:S(2)}) collective-permute-start(f32[1,4,24,256]{3,2,1,0:T(8,128)S(1)} %split.8), channel_id=1, source_target_pairs={{0,4},{4,0},{8,12},{12,8},{16,20},{20,16},{24,28},{28,24},{1,5},{5... | collective-permute-start | bytes 294920 | tf_op jit(solution)/shard_map/ppermute | solution.py:243
  49.8 17.6 %collective-permute-start.11 = (f32[3,40,256]{2,1,0:T(8,128)S(1)}, f32[3,40,256]{2,1,0:T(8,128)S(1)}, u32[]{:S(2)}, u32[]{:S(2)}) collective-permute-start(f32[3,40,256]{2,1,0:T(8,128)S(1)} %composite.2.refs_1_), channel_id=1, source_target_pairs={{0,16},{4,20},{8,24},{12,28},{16,0},{20,4},{24,8},{28,12},{1,17},{... | collective-permute-start | bytes 368648 | tf_op jit(solution)/shard_map/ppermute | solution.py:310
  60.6 1.4 %collective-permute-start.17 = (f32[1,4,24,256]{3,2,1,0:T(8,128)S(1)}, f32[1,4,24,256]{3,2,1,0:T(8,128)S(1)}, u32[]{:S(2)}, u32[]{:S(2)}) collective-permute-start(f32[1,4,24,256]{3,2,1,0:T(8,128)S(1)} %get-tuple-element.37), channel_id=1, source_target_pairs={{0,4},{4,0},{8,12},{12,8},{16,20},{20,16},{24,28},{28,24},{1,5},{5... | collective-permute-start | bytes 294920 | tf_op jit(solution)/shard_map/ppermute | solution.py:243
  61.2 9.7 %collective-permute-start.9 = (f32[3,40,256]{2,1,0:T(8,128)S(1)}, f32[3,40,256]{2,1,0:T(8,128)S(1)}, u32[]{:S(2)}, u32[]{:S(2)}) collective-permute-start(f32[3,40,256]{2,1,0:T(8,128)S(1)} %composite.2.refs_1_), channel_id=1, source_target_pairs={{0,4},{4,0},{8,12},{12,8},{16,20},{20,16},{24,28},{28,24},{1,5},{5... | collective-permute-start | bytes 368648 | tf_op jit(solution)/shard_map/ppermute | solution.py:243
  67.4 10.6 %collective-permute-start.21 = (f32[3,40,256]{2,1,0:T(8,128)S(1)}, f32[3,40,256]{2,1,0:T(8,128)S(1)}, u32[]{:S(2)}, u32[]{:S(2)}) collective-permute-start(f32[3,40,256]{2,1,0:T(8,128)S(1)} %get-tuple-element.40.refs_5_), channel_id=1, source_target_pairs={{0,8},{4,12},{8,0},{12,4},{16,24},{20,28},{24,16},{28,20},{1,9},{5... | collective-permute-start | bytes 368648 | tf_op jit(solution)/shard_map/ppermute | solution.py:310
  68.5 7.1 %collective-permute-start.28 = (f32[3,24,256]{2,1,0:T(8,128)S(1)}, f32[3,24,256]{2,1,0:T(8,128)S(1)}, u32[]{:S(2)}, u32[]{:S(2)}) collective-permute-start(f32[3,24,256]{2,1,0:T(8,128)S(1)} %composite.3.refs_2_.refs_9_), channel_id=1, source_target_pairs={{0,24},{4,28},{8,0},{12,4},{16,8},{20,12},{24,16},{28,20},{1,25},{... | collective-permute-start | bytes 221192 | tf_op jit(solution)/shard_map/ppermute | solution.py:246
  69.3 8.7 %collective-permute-start.26 = (f32[3,24,256]{2,1,0:T(8,128)S(1)}, f32[3,24,256]{2,1,0:T(8,128)S(1)}, u32[]{:S(2)}, u32[]{:S(2)}) collective-permute-start(f32[3,24,256]{2,1,0:T(8,128)S(1)} %composite.3.refs_2_.refs_9_), channel_id=1, source_target_pairs={{0,16},{4,20},{8,24},{12,28},{16,0},{20,4},{24,8},{28,12},{1,17},{... | collective-permute-start | bytes 221192 | tf_op jit(solution)/shard_map/ppermute | solution.py:246
  70.9 8.1 %collective-permute-start.19 = (f32[3,40,256]{2,1,0:T(8,128)S(1)}, f32[3,40,256]{2,1,0:T(8,128)S(1)}, u32[]{:S(2)}, u32[]{:S(2)}) collective-permute-start(f32[3,40,256]{2,1,0:T(8,128)S(1)} %get-tuple-element.39.refs_3_), channel_id=1, source_target_pairs={{0,4},{4,0},{8,12},{12,8},{16,20},{20,16},{24,28},{28,24},{1,5},{5... | collective-permute-start | bytes 368648 | tf_op jit(solution)/shard_map/ppermute | solution.py:243
  70.9 7.6 %collective-permute-start.24 = (f32[3,24,256]{2,1,0:T(8,128)S(1)}, f32[3,24,256]{2,1,0:T(8,128)S(1)}, u32[]{:S(2)}, u32[]{:S(2)}) collective-permute-start(f32[3,24,256]{2,1,0:T(8,128)S(1)} %composite.3.refs_2_.refs_9_), channel_id=1, source_target_pairs={{0,8},{4,12},{8,16},{12,20},{16,24},{20,28},{24,0},{28,4},{1,9},{5... | collective-permute-start | bytes 221192 | tf_op jit(solution)/shard_map/ppermute | solution.py:246
  75.6 3.0 %collective-permute-start.23 = (f32[3,24,256]{2,1,0:T(8,128)S(1)}, f32[3,24,256]{2,1,0:T(8,128)S(1)}, u32[]{:S(2)}, u32[]{:S(2)}) collective-permute-start(f32[3,24,256]{2,1,0:T(8,128)S(1)} %composite.3.refs_2_.refs_9_), channel_id=1, source_target_pairs={{0,4},{4,0},{8,12},{12,8},{16,20},{20,16},{24,28},{28,24},{1,5},{5... | collective-permute-start | bytes 221192 | tf_op jit(solution)/shard_map/ppermute | solution.py:243
  78.0 2.3 %collective-permute-start.22 = (f32[3,40,256]{2,1,0:T(8,128)S(1)}, f32[3,40,256]{2,1,0:T(8,128)S(1)}, u32[]{:S(2)}, u32[]{:S(2)}) collective-permute-start(f32[3,40,256]{2,1,0:T(8,128)S(1)} %collective-permute-done.21.refs_7_), channel_id=1, source_target_pairs={{0,4},{4,0},{8,12},{12,8},{16,20},{20,16},{24,28},{28,24},{1,5},{5... | collective-permute-start | bytes 368648 | tf_op jit(solution)/shard_map/ppermute | solution.py:243
  (9 other events, 36.6 us)

commit v6 on v5

--- a/solution.py
+++ b/solution.py
@@ -50,7 +50,14 @@
         copy.wait()
 
 
-def render_kernel(runs, tiles, chips, offsets, scale, given, where_ref, transfer_ref, light_ref, field_ref, *refs):
+def render_kernel(runs, tiles, chips, offsets, scale, given, where_ref, transfer_hbm_ref, light_hbm_ref, field_ref, *refs):
+    refs, (transfer_ref, light_ref, small_sem) = refs[:-3], refs[-3:]
+    small = [
+        pltpu.make_async_copy(source, target, small_sem.at[i])
+        for i, (source, target) in enumerate(((transfer_hbm_ref, transfer_ref), (light_hbm_ref, light_ref)))
+    ]
+    for copy in small:
+        copy.start()
     if given:
         edges, padded, out_refs, sem = [], refs[0], refs[1:-1], refs[-1]
     else:
@@ -81,6 +88,8 @@
         padded[:, :, :LANE] = rim
         padded[:, :, LANE + columns :] = rim
 
+    for copy in small:
+        copy.wait()
     light = [0.5 * light_ref[i] for i in range(3)]
     slope = [0.5 * transfer_ref[0, c] for c in range(3)]
     offset = [0.5 * transfer_ref[1, c] for c in range(3)]
@@ -237,7 +246,9 @@
     smem = pl.BlockSpec(memory_space=pltpu.SMEM)
     vmem = pl.BlockSpec(memory_space=pltpu.VMEM)
     hbm = pl.BlockSpec(memory_space=pltpu.HBM)
-    field = pltpu.with_memory_space_constraint(scalar_field, pltpu.HBM)
+    field, small_transfer, small_light = [
+        pltpu.with_memory_space_constraint(value, pltpu.HBM) for value in (scalar_field, transfer, light_dir)
+    ]
 
     def swap(value):
         return lax.ppermute(value, "wide", [(i, i ^ 1) for i in range(wide)])
@@ -251,12 +262,18 @@
         buffer = pltpu.VMEM((planes, slots * SUB, columns + 2 * LANE), jnp.float32)
         return call(
             functools.partial(render_kernel, runs, tiles, chips, offsets, scale, len(given)),
-            [where, transfer, light_dir, field, *edges, *given],
-            [smem] * 3 + [hbm] + [vmem] * (len(edges) + len(given)),
+            [where, small_transfer, small_light, field, *edges, *given],
+            [smem] + [hbm] * 3 + [vmem] * (len(edges) + len(given)),
             events,
             out_shape=[block] * len(offsets) + [buffer] * keep,
             out_specs=[vmem] * (len(offsets) + keep),
-            scratch_shapes=[buffer] * (not keep and not given) + [pltpu.SemaphoreType.DMA((slots,))],
+            scratch_shapes=[buffer] * (not keep and not given)
+            + [
+                pltpu.SemaphoreType.DMA((slots,)),
+                pltpu.SMEM(transfer.shape, jnp.float32),
+                pltpu.SMEM(light_dir.shape, jnp.float32),
+                pltpu.SemaphoreType.DMA((2,)),
+            ],
             cost_estimate=lasting(0.6 * len(offsets) * tiles_of(runs)),
             name="render",
         )

time: 82.4 us -> 81.1 us (0.984)
  local copies, waits for them, and re-layouts: 1.34 us -> 0.01 us
    unnamed x6 -> x2, local copies, waits for them, and re-layouts: 1.34 us -> 0.01 us
  transfers between devices with their start and end apart: 30 -> 30, of which waited for: 15 -> 15; matrix products, arithmetic and copies ran while one was open for 0% -> 0% of each run, Pallas kernels for 18% -> 20%
where the time goes in v6:
time: 81.1 us; the launch traced here: 80.9 us
  waiting for transfers between devices  29.4 us (36%)
  starting transfers between devices  27.1 us (33%)
  Pallas kernels  24.2 us (30%)
    pallas_call x13, Pallas kernels, call(): pl.pallas_call(with_events, in_specs=list(specs) + [pl.BlockSpec(memory_s...  24.2 us
    ppermute x9, starting transfers between devices, send(): lax.ppermute(value, 'wide', [(i, (i + k * CORES) % wide) for i in range(w...  16.1 us
    ppermute x9, waiting for transfers between devices, send(): lax.ppermute(value, 'wide', [(i, (i + k * CORES) % wide) for i in range(w...  15.1 us
    ppermute x3, waiting for transfers between devices, across(): lax.ppermute(value, 'wide', [(i, i ^ m * CORES) for i in range(wide)])  6.47 us
    ppermute x1, waiting for transfers between devices, edge_rows(): lax.ppermute(first_row, 'narrow', [(j, i) for i, j in up])  4.72 us
    ppermute x3, starting transfers between devices, across(): lax.ppermute(value, 'wide', [(i, i ^ m * CORES) for i in range(wide)])  3.41 us
    ppermute x1, starting transfers between devices, edge_rows(): lax.ppermute(last_row, 'narrow', up)  3.4 us
    ppermute x16, starting transfers between devices, swap(): return lax.ppermute(value, 'wide', [(i, i ^ 1) for i in range(wide)])  2.9 us
  transfers between devices with their start and end apart: 30, of which 15 were waited for; matrix products, arithmetic and copies ran while one was open for 0% of the time, Pallas kernels for 20%

profile of v6, /device:TPU:0, one launch (start us, length us, event | category | flops | bytes accessed | tf_op | source)
XLA Modules:
  0.0 80.9 jit_solution(3782070778664555946)
XLA Ops:
  0.1 6.3 %render.3 = (f32[2,4,40,256]{3,2,1,0:T(8,128)S(1)}, f32[2,4,40,256]{3,2,1,0:T(8,128)S(1)}, f32[16,56,2304]{2,1,0:T(8,128)S(1)}) custom-call(s32[2]{0:T(128)S(1)} %pad_add_fusion.refs_0_, f32[2,3]{1,0:T(2,128)} %refs_1_.7, f32[3]{0:T(128)} %refs_2_.5, f32[16,64,2048]{2,1,0:T(8,128)} %refs_3_.5), custom_call_target="tpu_custom_call" | custom-call | bytes 22140000 | tf_op jit(solution)/shard_map/render/pallas_call | solution.py:25
  6.4 3.1 %collective-permute-start = (f32[2,4,40,256]{3,2,1,0:T(8,128)S(1)}, f32[2,4,40,256]{3,2,1,0:T(8,128)S(1)}, u32[]{:S(2)}, u32[]{:S(2)}) collective-permute-start(f32[2,4,40,256]{3,2,1,0:T(8,128)S(1)} %get-tuple-element.26), channel_id=1, source_target_pairs={{0,8},{4,12},{8,16},{12,20},{16,24},{20,28},{24,0},{28,4},{1,9},{5... | collective-permute-start | bytes 983048 | tf_op jit(solution)/shard_map/ppermute | solution.py:257
  9.5 2.6 %collective-permute-start.1 = (f32[2,4,40,256]{3,2,1,0:T(8,128)S(1)}, f32[2,4,40,256]{3,2,1,0:T(8,128)S(1)}, u32[]{:S(2)}, u32[]{:S(2)}) collective-permute-start(f32[2,4,40,256]{3,2,1,0:T(8,128)S(1)} %get-tuple-element.24.refs_5_), channel_id=1, source_target_pairs={{0,16},{4,20},{8,24},{12,28},{16,0},{20,4},{24,8},{28,12},{1,17},{... | collective-permute-start | bytes 983048 | tf_op jit(solution)/shard_map/ppermute | solution.py:257
  12.1 5.2 %render.4 = (f32[2,4,40,256]{3,2,1,0:T(8,128)S(1)}, f32[2,4,40,256]{3,2,1,0:T(8,128)S(1)}) custom-call(s32[2]{0:T(128)S(1)} %pad_add_fusion.refs_0_, f32[2,3]{1,0:T(2,128)} %refs_1_.7, f32[3]{0:T(128)} %refs_2_.5, f32[16,64,2048]{2,1,0:T(8,128)} %refs_3_.5, f32[16,56,2304]{2,1,0:T(8,128)S(1)} %get-tuple-element.23.refs_4_, ...), custom_call_target="tpu_custom_call" | custom-call | bytes 22140000 | tf_op jit(solution)/shard_map/render/pallas_call | solution.py:25
  17.3 1.4 %collective-permute-start.2 = (f32[2,4,40,256]{3,2,1,0:T(8,128)S(1)}, f32[2,4,40,256]{3,2,1,0:T(8,128)S(1)}, u32[]{:S(2)}, u32[]{:S(2)}) collective-permute-start(f32[2,4,40,256]{3,2,1,0:T(8,128)S(1)} %get-tuple-element.27.refs_1_.refs_6_), channel_id=1, source_target_pairs={{0,24},{4,28},{8,0},{12,4},{16,8},{20,12},{24,16},{28,20},{1,25},{... | collective-permute-start | bytes 983048 | tf_op jit(solution)/shard_map/ppermute | solution.py:257
  19.6 3.4 %collective-permute-start.4 = (f32[16,1,2048]{2,1,0:T(1,128)S(1)}, f32[16,1,2048]{2,1,0:T(1,128)S(1)}, u32[]{:S(2)}, u32[]{:S(2)}) collective-permute-start(f32[16,1,2048]{2,1,0:T(1,128)S(1)} %get-tuple-element.28), channel_id=1, source_target_pairs={{0,1},{1,2},{2,3},{4,5},{5,6},{6,7},{8,9},{9,10},{10,11},{12,13},{... | collective-permute-start | bytes 393224 | tf_op jit(solution)/shard_map/ppermute | solution.py:295
  23.1 1.3 %collective-permute-start.5 = (f32[16,1,2048]{2,1,0:T(1,128)S(1)}, f32[16,1,2048]{2,1,0:T(1,128)S(1)}, u32[]{:S(2)}, u32[]{:S(2)}) collective-permute-start(f32[16,1,2048]{2,1,0:T(1,128)S(1)} %get-tuple-element.29), channel_id=1, source_target_pairs={{1,0},{2,1},{3,2},{5,4},{6,5},{7,6},{9,8},{10,9},{11,10},{13,12},{... | collective-permute-start | bytes 393224 | tf_op jit(solution)/shard_map/ppermute | solution.py:295
  24.4 1.2 %collective-permute-done.4.refs_4_ = f32[16,1,2048]{2,1,0:T(1,128)S(1)} collective-permute-done((f32[16,1,2048]{2,1,0:T(1,128)S(1)}, f32[16,1,2048]{2,1,0:T(1,128)S(1)}, u32[]{:S(2)}, u32[]{:S(2)}) %collective-permute-start.4) | collective-permute-done | bytes 131104 | tf_op jit(solution)/shard_map/ppermute | solution.py:295
  25.6 4.7 %collective-permute-done.5.refs_5_ = f32[16,1,2048]{2,1,0:T(1,128)S(1)} collective-permute-done((f32[16,1,2048]{2,1,0:T(1,128)S(1)}, f32[16,1,2048]{2,1,0:T(1,128)S(1)}, u32[]{:S(2)}, u32[]{:S(2)}) %collective-permute-start.5) | collective-permute-done | bytes 131104 | tf_op jit(solution)/shard_map/ppermute | solution.py:295
  30.3 7.3 %render.5 = (f32[2,4,24,256]{3,2,1,0:T(8,128)S(1)}, f32[2,4,24,256]{3,2,1,0:T(8,128)S(1)}, f32[2,4,24,256]{3,2,1,0:T(8,128)S(1)}, f32[2,4,24,256]{3,2,1,0:T(8,128)S(1)}) custom-call(s32[2]{0:T(128)S(1)} %pad_add_fusion.refs_0_, f32[2,3]{1,0:T(2,128)} %refs_1_.7, f32[3]{0:T(128)} %refs_2_.5, f32[16,64,2048]{2,1,0:T(8,128)} %refs_3_.5, ...), custom_call_target="tpu_custom_call" | custom-call | bytes 26568000 | tf_op jit(solution)/shard_map/render/pallas_call | solution.py:25
  38.4 3.2 %collective-permute-start.12 = (f32[2,4,24,256]{3,2,1,0:T(8,128)S(1)}, f32[2,4,24,256]{3,2,1,0:T(8,128)S(1)}, u32[]{:S(2)}, u32[]{:S(2)}) collective-permute-start(f32[2,4,24,256]{3,2,1,0:T(8,128)S(1)} %get-tuple-element.33), channel_id=1, source_target_pairs={{0,8},{4,12},{8,16},{12,20},{16,24},{20,28},{24,0},{28,4},{1,9},{5... | collective-permute-start | bytes 589832 | tf_op jit(solution)/shard_map/ppermute | solution.py:257
  41.6 1.6 %collective-permute-start.13 = (f32[2,4,24,256]{3,2,1,0:T(8,128)S(1)}, f32[2,4,24,256]{3,2,1,0:T(8,128)S(1)}, u32[]{:S(2)}, u32[]{:S(2)}) collective-permute-start(f32[2,4,24,256]{3,2,1,0:T(8,128)S(1)} %get-tuple-element.34), channel_id=1, source_target_pairs={{0,16},{4,20},{8,24},{12,28},{16,0},{20,4},{24,8},{28,12},{1,17},{... | collective-permute-start | bytes 589832 | tf_op jit(solution)/shard_map/ppermute | solution.py:257
  43.9 1.3 %composite.2.refs_1_ = f32[3,40,256]{2,1,0:T(8,128)S(1)} custom-call(s32[2]{0:T(128)S(1)} %pad_add_fusion.refs_0_, s32[8]{0:T(128)S(1)} %copy-done, f32[2,4,40,256]{3,2,1,0:T(8,128)S(1)} %get-tuple-element.25.refs_0_.refs_2_, f32[2,4,40,256]{3,2,1,0:T(8,128)S(1)} %collective-permute-done.refs_0_.refs_3_, ...), custom_call_target="tpu_custom_call" | custom-call | bytes 3690000 | tf_op jit(solution)/shard_map/composite/pallas_call | solution.py:25
  45.3 1.3 %collective-permute-start.10 = (f32[3,40,256]{2,1,0:T(8,128)S(1)}, f32[3,40,256]{2,1,0:T(8,128)S(1)}, u32[]{:S(2)}, u32[]{:S(2)}) collective-permute-start(f32[3,40,256]{2,1,0:T(8,128)S(1)} %composite.2.refs_1_), channel_id=1, source_target_pairs={{0,8},{4,12},{8,0},{12,4},{16,24},{20,28},{24,16},{28,20},{1,9},{5... | collective-permute-start | bytes 368648 | tf_op jit(solution)/shard_map/ppermute | solution.py:327
  46.7 1.8 %collective-permute-done.12.refs_0_.refs_3_ = f32[2,4,24,256]{3,2,1,0:T(8,128)S(1)} collective-permute-done((f32[2,4,24,256]{3,2,1,0:T(8,128)S(1)}, f32[2,4,24,256]{3,2,1,0:T(8,128)S(1)}, u32[]{:S(2)}, u32[]{:S(2)}) %collective-permute-start.12) | collective-permute-done | bytes 196640 | tf_op jit(solution)/shard_map/ppermute | solution.py:257
  48.5 1.0 %collective-permute-start.11 = (f32[3,40,256]{2,1,0:T(8,128)S(1)}, f32[3,40,256]{2,1,0:T(8,128)S(1)}, u32[]{:S(2)}, u32[]{:S(2)}) collective-permute-start(f32[3,40,256]{2,1,0:T(8,128)S(1)} %composite.2.refs_1_), channel_id=1, source_target_pairs={{0,16},{4,20},{8,24},{12,28},{16,0},{20,4},{24,8},{28,12},{1,17},{... | collective-permute-start | bytes 368648 | tf_op jit(solution)/shard_map/ppermute | solution.py:327
  49.6 7.1 %collective-permute-done.13.refs_1_.refs_4_ = f32[2,4,24,256]{3,2,1,0:T(8,128)S(1)} collective-permute-done((f32[2,4,24,256]{3,2,1,0:T(8,128)S(1)}, f32[2,4,24,256]{3,2,1,0:T(8,128)S(1)}, u32[]{:S(2)}, u32[]{:S(2)}) %collective-permute-start.13) | collective-permute-done | bytes 196640 | tf_op jit(solution)/shard_map/ppermute | solution.py:257
  56.7 2.5 %collective-permute-done.10.refs_3_.refs_0_ = f32[3,40,256]{2,1,0:T(8,128)S(1)} collective-permute-done((f32[3,40,256]{2,1,0:T(8,128)S(1)}, f32[3,40,256]{2,1,0:T(8,128)S(1)}, u32[]{:S(2)}, u32[]{:S(2)}) %collective-permute-start.10) | collective-permute-done | bytes 122912 | tf_op jit(solution)/shard_map/ppermute | solution.py:327
  61.1 1.0 %composite.3.refs_2_.refs_9_ = f32[3,24,256]{2,1,0:T(8,128)S(1)} custom-call(s32[2]{0:T(128)S(1)} %pad_add_fusion.refs_0_, s32[8]{0:T(128)S(1)} %copy-done, f32[2,4,24,256]{3,2,1,0:T(8,128)S(1)} %get-tuple-element.30.refs_2_.refs_0_, f32[2,4,24,256]{3,2,1,0:T(8,128)S(1)} %collective-permute-done.12.refs_0_.refs_3_, ...), custom_call_target="tpu_custom_call" | custom-call | bytes 3690000 | tf_op jit(solution)/shard_map/composite/pallas_call | solution.py:25
  62.1 4.0 %collective-permute-done.11.refs_1_ = f32[3,40,256]{2,1,0:T(8,128)S(1)} collective-permute-done((f32[3,40,256]{2,1,0:T(8,128)S(1)}, f32[3,40,256]{2,1,0:T(8,128)S(1)}, u32[]{:S(2)}, u32[]{:S(2)}) %collective-permute-start.11) | collective-permute-done | bytes 122912 | tf_op jit(solution)/shard_map/ppermute | solution.py:327
  68.0 1.6 %collective-permute-start.26 = (f32[3,24,256]{2,1,0:T(8,128)S(1)}, f32[3,24,256]{2,1,0:T(8,128)S(1)}, u32[]{:S(2)}, u32[]{:S(2)}) collective-permute-start(f32[3,24,256]{2,1,0:T(8,128)S(1)} %composite.3.refs_2_.refs_9_), channel_id=1, source_target_pairs={{0,16},{4,20},{8,24},{12,28},{16,0},{20,4},{24,8},{28,12},{1,17},{... | collective-permute-start | bytes 221192 | tf_op jit(solution)/shard_map/ppermute | solution.py:257
  70.6 3.7 %collective-permute-done.28.refs_15_ = f32[3,24,256]{2,1,0:T(8,128)S(1)} collective-permute-done((f32[3,24,256]{2,1,0:T(8,128)S(1)}, f32[3,24,256]{2,1,0:T(8,128)S(1)}, u32[]{:S(2)}, u32[]{:S(2)}) %collective-permute-start.28) | collective-permute-done | bytes 73760 | tf_op jit(solution)/shard_map/ppermute | solution.py:257
  74.3 2.3 %collective-permute-done.26.refs_13_ = f32[3,24,256]{2,1,0:T(8,128)S(1)} collective-permute-done((f32[3,24,256]{2,1,0:T(8,128)S(1)}, f32[3,24,256]{2,1,0:T(8,128)S(1)}, u32[]{:S(2)}, u32[]{:S(2)}) %collective-permute-start.26) | collective-permute-done | bytes 73760 | tf_op jit(solution)/shard_map/ppermute | solution.py:257
  79.0 1.9 %place.1 = f32[3,64,2048]{2,1,0:T(8,128)} custom-call(s32[2]{0:T(128)S(1)} %pad_add_fusion.refs_0_, f32[3,40,256]{2,1,0:T(8,128)S(1)} %composite.2.refs_1_, f32[3,40,256]{2,1,0:T(8,128)S(1)} %collective-permute-done.9.refs_2_, f32[3,40,256]{2,1,0:T(8,128)S(1)} %get-tuple-element.39.refs_3_, f32[3,40,256]{2,1,0:T(8,128)S(1)} %collective-permute-done.19.refs_4_, ...), custom_call_target="tpu_custom_call" | custom-call | bytes 7380000 | tf_op jit(solution)/shard_map/place/pallas_call | solution.py:25
  (52 shorter events, 9.7 us)
Async XLA Ops:
  6.4 31.2 %collective-permute-start = (f32[2,4,40,256]{3,2,1,0:T(8,128)S(1)}, f32[2,4,40,256]{3,2,1,0:T(8,128)S(1)}, u32[]{:S(2)}, u32[]{:S(2)}) collective-permute-start(f32[2,4,40,256]{3,2,1,0:T(8,128)S(1)} %get-tuple-element.26), channel_id=1, source_target_pairs={{0,8},{4,12},{8,16},{12,20},{16,24},{20,28},{24,0},{28,4},{1,9},{5... | collective-permute-start | bytes 983048 | tf_op jit(solution)/shard_map/ppermute | solution.py:257
  9.5 28.2 %collective-permute-start.1 = (f32[2,4,40,256]{3,2,1,0:T(8,128)S(1)}, f32[2,4,40,256]{3,2,1,0:T(8,128)S(1)}, u32[]{:S(2)}, u32[]{:S(2)}) collective-permute-start(f32[2,4,40,256]{3,2,1,0:T(8,128)S(1)} %get-tuple-element.24.refs_5_), channel_id=1, source_target_pairs={{0,16},{4,20},{8,24},{12,28},{16,0},{20,4},{24,8},{28,12},{1,17},{... | collective-permute-start | bytes 983048 | tf_op jit(solution)/shard_map/ppermute | solution.py:257
  17.3 20.4 %collective-permute-start.2 = (f32[2,4,40,256]{3,2,1,0:T(8,128)S(1)}, f32[2,4,40,256]{3,2,1,0:T(8,128)S(1)}, u32[]{:S(2)}, u32[]{:S(2)}) collective-permute-start(f32[2,4,40,256]{3,2,1,0:T(8,128)S(1)} %get-tuple-element.27.refs_1_.refs_6_), channel_id=1, source_target_pairs={{0,24},{4,28},{8,0},{12,4},{16,8},{20,12},{24,16},{28,20},{1,25},{... | collective-permute-start | bytes 983048 | tf_op jit(solution)/shard_map/ppermute | solution.py:257
  19.6 5.9 %collective-permute-start.4 = (f32[16,1,2048]{2,1,0:T(1,128)S(1)}, f32[16,1,2048]{2,1,0:T(1,128)S(1)}, u32[]{:S(2)}, u32[]{:S(2)}) collective-permute-start(f32[16,1,2048]{2,1,0:T(1,128)S(1)} %get-tuple-element.28), channel_id=1, source_target_pairs={{0,1},{1,2},{2,3},{4,5},{5,6},{6,7},{8,9},{9,10},{10,11},{12,13},{... | collective-permute-start | bytes 393224 | tf_op jit(solution)/shard_map/ppermute | solution.py:295
  23.1 7.2 %collective-permute-start.5 = (f32[16,1,2048]{2,1,0:T(1,128)S(1)}, f32[16,1,2048]{2,1,0:T(1,128)S(1)}, u32[]{:S(2)}, u32[]{:S(2)}) collective-permute-start(f32[16,1,2048]{2,1,0:T(1,128)S(1)} %get-tuple-element.29), channel_id=1, source_target_pairs={{1,0},{2,1},{3,2},{5,4},{6,5},{7,6},{9,8},{10,9},{11,10},{13,12},{... | collective-permute-start | bytes 393224 | tf_op jit(solution)/shard_map/ppermute | solution.py:295
  25.6 16.0 %collective-permute-start.3 = (f32[1,4,40,256]{3,2,1,0:T(8,128)S(1)}, f32[1,4,40,256]{3,2,1,0:T(8,128)S(1)}, u32[]{:S(2)}, u32[]{:S(2)}) collective-permute-start(f32[1,4,40,256]{3,2,1,0:T(8,128)S(1)} %split.5), channel_id=1, source_target_pairs={{0,4},{4,0},{8,12},{12,8},{16,20},{20,16},{24,28},{28,24},{1,5},{5... | collective-permute-start | bytes 491528 | tf_op jit(solution)/shard_map/ppermute | solution.py:254
  37.7 5.5 %collective-permute-start.8 = (f32[1,4,40,256]{3,2,1,0:T(8,128)S(1)}, f32[1,4,40,256]{3,2,1,0:T(8,128)S(1)}, u32[]{:S(2)}, u32[]{:S(2)}) collective-permute-start(f32[1,4,40,256]{3,2,1,0:T(8,128)S(1)} %split.7), channel_id=1, source_target_pairs={{0,4},{4,0},{8,12},{12,8},{16,20},{20,16},{24,28},{28,24},{1,5},{5... | collective-permute-start | bytes 491528 | tf_op jit(solution)/shard_map/ppermute | solution.py:254
  37.8 6.2 %collective-permute-start.7 = (f32[1,4,40,256]{3,2,1,0:T(8,128)S(1)}, f32[1,4,40,256]{3,2,1,0:T(8,128)S(1)}, u32[]{:S(2)}, u32[]{:S(2)}) collective-permute-start(f32[1,4,40,256]{3,2,1,0:T(8,128)S(1)} %get-tuple-element.32), channel_id=1, source_target_pairs={{0,4},{4,0},{8,12},{12,8},{16,20},{20,16},{24,28},{28,24},{1,5},{5... | collective-permute-start | bytes 491528 | tf_op jit(solution)/shard_map/ppermute | solution.py:254
  38.3 5.7 %collective-permute-start.6 = (f32[1,4,40,256]{3,2,1,0:T(8,128)S(1)}, f32[1,4,40,256]{3,2,1,0:T(8,128)S(1)}, u32[]{:S(2)}, u32[]{:S(2)}) collective-permute-start(f32[1,4,40,256]{3,2,1,0:T(8,128)S(1)} %get-tuple-element.31.refs_1_), channel_id=1, source_target_pairs={{0,4},{4,0},{8,12},{12,8},{16,20},{20,16},{24,28},{28,24},{1,5},{5... | collective-permute-start | bytes 491528 | tf_op jit(solution)/shard_map/ppermute | solution.py:254
  38.4 10.2 %collective-permute-start.12 = (f32[2,4,24,256]{3,2,1,0:T(8,128)S(1)}, f32[2,4,24,256]{3,2,1,0:T(8,128)S(1)}, u32[]{:S(2)}, u32[]{:S(2)}) collective-permute-start(f32[2,4,24,256]{3,2,1,0:T(8,128)S(1)} %get-tuple-element.33), channel_id=1, source_target_pairs={{0,8},{4,12},{8,16},{12,20},{16,24},{20,28},{24,0},{28,4},{1,9},{5... | collective-permute-start | bytes 589832 | tf_op jit(solution)/shard_map/ppermute | solution.py:257
  41.6 15.1 %collective-permute-start.13 = (f32[2,4,24,256]{3,2,1,0:T(8,128)S(1)}, f32[2,4,24,256]{3,2,1,0:T(8,128)S(1)}, u32[]{:S(2)}, u32[]{:S(2)}) collective-permute-start(f32[2,4,24,256]{3,2,1,0:T(8,128)S(1)} %get-tuple-element.34), channel_id=1, source_target_pairs={{0,16},{4,20},{8,24},{12,28},{16,0},{20,4},{24,8},{28,12},{1,17},{... | collective-permute-start | bytes 589832 | tf_op jit(solution)/shard_map/ppermute | solution.py:257
  43.2 13.5 %collective-permute-start.14 = (f32[2,4,24,256]{3,2,1,0:T(8,128)S(1)}, f32[2,4,24,256]{3,2,1,0:T(8,128)S(1)}, u32[]{:S(2)}, u32[]{:S(2)}) collective-permute-start(f32[2,4,24,256]{3,2,1,0:T(8,128)S(1)} %get-tuple-element.35), channel_id=1, source_target_pairs={{0,24},{4,28},{8,0},{12,4},{16,8},{20,12},{24,16},{28,20},{1,25},{... | collective-permute-start | bytes 589832 | tf_op jit(solution)/shard_map/ppermute | solution.py:257
  45.3 13.9 %collective-permute-start.10 = (f32[3,40,256]{2,1,0:T(8,128)S(1)}, f32[3,40,256]{2,1,0:T(8,128)S(1)}, u32[]{:S(2)}, u32[]{:S(2)}) collective-permute-start(f32[3,40,256]{2,1,0:T(8,128)S(1)} %composite.2.refs_1_), channel_id=1, source_target_pairs={{0,8},{4,12},{8,0},{12,4},{16,24},{20,28},{24,16},{28,20},{1,9},{5... | collective-permute-start | bytes 368648 | tf_op jit(solution)/shard_map/ppermute | solution.py:327
  46.6 13.2 %collective-permute-start.15 = (f32[1,4,24,256]{3,2,1,0:T(8,128)S(1)}, f32[1,4,24,256]{3,2,1,0:T(8,128)S(1)}, u32[]{:S(2)}, u32[]{:S(2)}) collective-permute-start(f32[1,4,24,256]{3,2,1,0:T(8,128)S(1)} %split.8), channel_id=1, source_target_pairs={{0,4},{4,0},{8,12},{12,8},{16,20},{20,16},{24,28},{28,24},{1,5},{5... | collective-permute-start | bytes 294920 | tf_op jit(solution)/shard_map/ppermute | solution.py:254
  48.5 17.6 %collective-permute-start.11 = (f32[3,40,256]{2,1,0:T(8,128)S(1)}, f32[3,40,256]{2,1,0:T(8,128)S(1)}, u32[]{:S(2)}, u32[]{:S(2)}) collective-permute-start(f32[3,40,256]{2,1,0:T(8,128)S(1)} %composite.2.refs_1_), channel_id=1, source_target_pairs={{0,16},{4,20},{8,24},{12,28},{16,0},{20,4},{24,8},{28,12},{1,17},{... | collective-permute-start | bytes 368648 | tf_op jit(solution)/shard_map/ppermute | solution.py:327
  59.3 1.4 %collective-permute-start.17 = (f32[1,4,24,256]{3,2,1,0:T(8,128)S(1)}, f32[1,4,24,256]{3,2,1,0:T(8,128)S(1)}, u32[]{:S(2)}, u32[]{:S(2)}) collective-permute-start(f32[1,4,24,256]{3,2,1,0:T(8,128)S(1)} %get-tuple-element.37), channel_id=1, source_target_pairs={{0,4},{4,0},{8,12},{12,8},{16,20},{20,16},{24,28},{28,24},{1,5},{5... | collective-permute-start | bytes 294920 | tf_op jit(solution)/shard_map/ppermute | solution.py:254
  59.9 9.7 %collective-permute-start.9 = (f32[3,40,256]{2,1,0:T(8,128)S(1)}, f32[3,40,256]{2,1,0:T(8,128)S(1)}, u32[]{:S(2)}, u32[]{:S(2)}) collective-permute-start(f32[3,40,256]{2,1,0:T(8,128)S(1)} %composite.2.refs_1_), channel_id=1, source_target_pairs={{0,4},{4,0},{8,12},{12,8},{16,20},{20,16},{24,28},{28,24},{1,5},{5... | collective-permute-start | bytes 368648 | tf_op jit(solution)/shard_map/ppermute | solution.py:254
  66.1 10.6 %collective-permute-start.21 = (f32[3,40,256]{2,1,0:T(8,128)S(1)}, f32[3,40,256]{2,1,0:T(8,128)S(1)}, u32[]{:S(2)}, u32[]{:S(2)}) collective-permute-start(f32[3,40,256]{2,1,0:T(8,128)S(1)} %get-tuple-element.40.refs_5_), channel_id=1, source_target_pairs={{0,8},{4,12},{8,0},{12,4},{16,24},{20,28},{24,16},{28,20},{1,9},{5... | collective-permute-start | bytes 368648 | tf_op jit(solution)/shard_map/ppermute | solution.py:327
  67.1 7.2 %collective-permute-start.28 = (f32[3,24,256]{2,1,0:T(8,128)S(1)}, f32[3,24,256]{2,1,0:T(8,128)S(1)}, u32[]{:S(2)}, u32[]{:S(2)}) collective-permute-start(f32[3,24,256]{2,1,0:T(8,128)S(1)} %composite.3.refs_2_.refs_9_), channel_id=1, source_target_pairs={{0,24},{4,28},{8,0},{12,4},{16,8},{20,12},{24,16},{28,20},{1,25},{... | collective-permute-start | bytes 221192 | tf_op jit(solution)/shard_map/ppermute | solution.py:257
  68.0 8.6 %collective-permute-start.26 = (f32[3,24,256]{2,1,0:T(8,128)S(1)}, f32[3,24,256]{2,1,0:T(8,128)S(1)}, u32[]{:S(2)}, u32[]{:S(2)}) collective-permute-start(f32[3,24,256]{2,1,0:T(8,128)S(1)} %composite.3.refs_2_.refs_9_), channel_id=1, source_target_pairs={{0,16},{4,20},{8,24},{12,28},{16,0},{20,4},{24,8},{28,12},{1,17},{... | collective-permute-start | bytes 221192 | tf_op jit(solution)/shard_map/ppermute | solution.py:257
  69.6 8.1 %collective-permute-start.19 = (f32[3,40,256]{2,1,0:T(8,128)S(1)}, f32[3,40,256]{2,1,0:T(8,128)S(1)}, u32[]{:S(2)}, u32[]{:S(2)}) collective-permute-start(f32[3,40,256]{2,1,0:T(8,128)S(1)} %get-tuple-element.39.refs_3_), channel_id=1, source_target_pairs={{0,4},{4,0},{8,12},{12,8},{16,20},{20,16},{24,28},{28,24},{1,5},{5... | collective-permute-start | bytes 368648 | tf_op jit(solution)/shard_map/ppermute | solution.py:254
  69.6 7.6 %collective-permute-start.24 = (f32[3,24,256]{2,1,0:T(8,128)S(1)}, f32[3,24,256]{2,1,0:T(8,128)S(1)}, u32[]{:S(2)}, u32[]{:S(2)}) collective-permute-start(f32[3,24,256]{2,1,0:T(8,128)S(1)} %composite.3.refs_2_.refs_9_), channel_id=1, source_target_pairs={{0,8},{4,12},{8,16},{12,20},{16,24},{20,28},{24,0},{28,4},{1,9},{5... | collective-permute-start | bytes 221192 | tf_op jit(solution)/shard_map/ppermute | solution.py:257
  74.3 2.9 %collective-permute-start.23 = (f32[3,24,256]{2,1,0:T(8,128)S(1)}, f32[3,24,256]{2,1,0:T(8,128)S(1)}, u32[]{:S(2)}, u32[]{:S(2)}) collective-permute-start(f32[3,24,256]{2,1,0:T(8,128)S(1)} %composite.3.refs_2_.refs_9_), channel_id=1, source_target_pairs={{0,4},{4,0},{8,12},{12,8},{16,20},{20,16},{24,28},{28,24},{1,5},{5... | collective-permute-start | bytes 221192 | tf_op jit(solution)/shard_map/ppermute | solution.py:254
  76.7 2.3 %collective-permute-start.22 = (f32[3,40,256]{2,1,0:T(8,128)S(1)}, f32[3,40,256]{2,1,0:T(8,128)S(1)}, u32[]{:S(2)}, u32[]{:S(2)}) collective-permute-start(f32[3,40,256]{2,1,0:T(8,128)S(1)} %collective-permute-done.21.refs_7_), channel_id=1, source_target_pairs={{0,4},{4,0},{8,12},{12,8},{16,20},{20,16},{24,28},{28,24},{1,5},{5... | collective-permute-start | bytes 368648 | tf_op jit(solution)/shard_map/ppermute | solution.py:254
  (7 other events, 34.6 us)
